TPU v7x, 32 devices: a whole 2x2x4 slice. The times are simulated.
32 devices in a mesh: fsdp: 8 (over z, x), dp: 4 (over y, core).
Axes of the slice: x: 2, y: 2, z: 4, core: 2. Of those that a mesh axis runs over, the one named last changes fastest.
Arguments:
- patches: bfloat16 [128, 256, 588], P(('fsdp', 'dp')), may hold values from -6 to 6
- patch_mask: int32 [128, 256], P(('fsdp', 'dp')), may hold values 0 or 1
- image_valid: int32 [128], replicated, may hold values from 0 to 1, as said below
- centre: float32 [65536], replicated, may hold values from -0.6 to 0.6
- w_patch: float32 [384, 588], P('fsdp'), may hold values from -0.25 to 0.25
- first_patch: float32 [384, 588], P('fsdp'), may hold values from -1.1920929e-06 to 1.1920929e-06
- second_patch: float32 [384, 588], P('fsdp'), may hold values from 9.598043e-16 to 3.839217e-15
- teacher_patch: float32 [384, 588], P('fsdp'), may hold values from -0.25 to 0.25
- w_layer: float32 [2, 384, 4608], P(None, 'fsdp'), may hold values from -0.3125 to 0.3125
- first_layer: float32 [2, 384, 4608], P(None, 'fsdp'), may hold values from -1.1920929e-06 to 1.1920929e-06
- second_layer: float32 [2, 384, 4608], P(None, 'fsdp'), may hold values from 3.839217e-15 to 1.5356868e-14
- teacher_layer: float32 [2, 384, 4608], P(None, 'fsdp'), may hold values from -0.3125 to 0.3125
- w_head: float32 [2688, 2048], P('fsdp'), may hold values from -0.125 to 0.125
- first_head: float32 [2688, 2048], P('fsdp'), may hold values from -1.1920929e-06 to 1.1920929e-06
- second_head: float32 [2688, 2048], P('fsdp'), may hold values from 3.839217e-15 to 1.5356868e-14
- teacher_head: float32 [2688, 2048], P('fsdp'), may hold values from -0.125 to 0.125
- w_proto: float32 [65536, 256], P('fsdp'), may hold values from -1.25 to 1.25
- first_proto: float32 [65536, 256], P('fsdp'), may hold values from -1.1920929e-06 to 1.1920929e-06
- second_proto: float32 [65536, 256], P('fsdp'), may hold values from 3.839217e-15 to 1.5356868e-14
- teacher_proto: float32 [65536, 256], P('fsdp'), may hold values from -1.25 to 1.25
- vectors: float32 [274, 384], replicated, as said below
- first_vectors: float32 [274, 384], replicated, may hold values from -1.1920929e-06 to 1.1920929e-06
- second_vectors: float32 [274, 384], replicated, may hold values from 1.1517652e-14 to 4.6070607e-14
- teacher_vectors: float32 [274, 384], replicated, as said below
Outputs:
- loss_sum: float32 [], replicated
- valid_count: float32 [], replicated
- grad_norm: float32 [], replicated
- new_centre: float32 [65536], replicated
- new_patch: float32 [384, 588], P('fsdp')
- new_first_patch: float32 [384, 588], P('fsdp')
- new_second_patch: float32 [384, 588], P('fsdp')
- new_teacher_patch: float32 [384, 588], P('fsdp')
- new_layer: float32 [2, 384, 4608], P(None, 'fsdp')
- new_first_layer: float32 [2, 384, 4608], P(None, 'fsdp')
- new_second_layer: float32 [2, 384, 4608], P(None, 'fsdp')
- new_teacher_layer: float32 [2, 384, 4608], P(None, 'fsdp')
- new_head: float32 [2688, 2048], P('fsdp')
- new_first_head: float32 [2688, 2048], P('fsdp')
- new_second_head: float32 [2688, 2048], P('fsdp')
- new_teacher_head: float32 [2688, 2048], P('fsdp')
- new_proto: float32 [65536, 256], P('fsdp')
- new_first_proto: float32 [65536, 256], P('fsdp')
- new_second_proto: float32 [65536, 256], P('fsdp')
- new_teacher_proto: float32 [65536, 256], P('fsdp')
- new_vectors: float32 [274, 384], replicated
- new_first_vectors: float32 [274, 384], replicated
- new_second_vectors: float32 [274, 384], replicated
- new_teacher_vectors: float32 [274, 384], replicated
Inputs may be any that keep to these rules, and one draw needn't show every extreme that they name: `image_valid`: the last image always counts. `vectors`: rows follow the layout of the vector table; gains are positive. `teacher_vectors`: same layout as vectors.
All inputs are finite; a program needn't handle non-finite values. No bound on the sum of `patch_mask` on one device may be relied on, other than what follows from the above.
Results may differ from a plain program's by a relative error of at most 0.02.
Values may be sent and summed in bfloat16 or wider, within the bound.
A program may use at most 448 MiB of HBM per device.

v0:
```python
from functools import partial

import jax
import jax.numpy as jnp
from jax import lax
from jax.sharding import PartitionSpec as P

HEADS = 6
STEP = 10
IMG_MB = 2


PRECISION_MODE = lax.Precision.DEFAULT
STUDENT_TEMP = 0.1
TEACHER_TEMP = 0.07
CENTRE_KEEP = 0.9
TEACHER_KEEP = 0.8
BETA_ONE = 0.9
BETA_TWO = 0.999
CLIP_NORM = 0.01
RATES = (0.1, 0.15, 0.07, 0.5, 0.5)
DECAYS = (0.04, 0.04, 0.04, 0.04, 0.0)


def round_value(value):
    return lax.optimization_barrier(value.astype(jnp.bfloat16)).astype(jnp.float32)


def lowered(value):

    def rounded_keep(inner):
        return (round_value(inner), None)

    def rounded_pass(kept, grad):
        return (grad,)

    rounding = jax.custom_vjp(round_value)
    rounding.defvjp(rounded_keep, rounded_pass)
    return rounding(value)


def lowered_back(value):

    def same_value(inner):
        return inner

    def passed_keep(inner):
        return (inner, None)

    def passed_round(kept, grad):
        return (round_value(grad),)

    passing = jax.custom_vjp(same_value)
    passing.defvjp(passed_keep, passed_round)
    return passing(value)


def matmul(left, right):
    return lowered_back(jnp.dot(lowered(left), lowered(right), precision=PRECISION_MODE))


def layer_norm(x, gain, shift):
    centred = x - jnp.mean(x, -1, keepdims=True)
    spread = jnp.mean(centred * centred, -1, keepdims=True)
    return centred * lax.rsqrt(spread + 1e-06) * gain + shift


def embed(pixels, covered, patch_weight, vecs):
    length = pixels.shape[1] + 1
    tokens = matmul(pixels, patch_weight.T) + vecs[length + 2]
    covered_col = covered[..., None]
    tokens = tokens * (1.0 - covered_col) + vecs[length + 1] * covered_col
    leading = jnp.broadcast_to(vecs[length], (pixels.shape[0], 1, vecs.shape[1]))
    return jnp.concatenate([leading, tokens], 1) + vecs[:length]


def block(x, layer_weight, vecs, depth_index):
    images, length, model_width = x.shape
    layer_rows = vecs[length + 3 + 6 * depth_index : length + 9 + 6 * depth_index]
    head_width = model_width // HEADS
    normed = layer_norm(x, layer_rows[0], layer_rows[1])
    triple = matmul(normed, layer_weight[:, : 3 * model_width]).reshape(
        images, length, 3, HEADS, head_width
    )
    queries = lowered(triple[:, :, 0])
    key_rows = lowered(triple[:, :, 1])
    value_rows = lowered(triple[:, :, 2])
    scores = lowered_back(
        jnp.einsum("nqhe,nkhe->nhqk", queries, key_rows, precision=PRECISION_MODE)
    ) * head_width ** (-0.5)
    scores = scores - jnp.max(scores, -1, keepdims=True)
    attention = jnp.exp(scores)
    attention = attention / jnp.sum(attention, -1, keepdims=True)
    mixture = lowered_back(
        jnp.einsum("nhqk,nkhe->nqhe", lowered(attention), value_rows, precision=PRECISION_MODE)
    )
    mixture = mixture.reshape(images, length, model_width)
    x = x + layer_rows[2] * matmul(mixture, layer_weight[:, 3 * model_width : 4 * model_width])
    normed = layer_norm(x, layer_rows[3], layer_rows[4])
    hidden = (layer_weight.shape[1] - 4 * model_width) // 2
    activated = jax.nn.gelu(
        matmul(normed, layer_weight[:, 4 * model_width : 4 * model_width + hidden])
    )
    return x + layer_rows[5] * matmul(activated, layer_weight[:, 4 * model_width + hidden :].T)


def head(cls_rows, head_weight, vecs):
    model_width = cls_rows.shape[-1]
    hidden = head_weight.shape[1]
    normed = layer_norm(cls_rows, vecs[-2], vecs[-1])
    leading = jax.nn.gelu(matmul(normed, head_weight[:model_width]))
    second = jax.nn.gelu(matmul(leading, head_weight[model_width : model_width + hidden]))
    bottleneck = matmul(second, head_weight[model_width + hidden :].T)
    return bottleneck * lax.rsqrt(jnp.sum(bottleneck * bottleneck, -1, keepdims=True) + 1e-06)


def teacher_probs(logits, centre):
    scaled = (logits - centre) / TEACHER_TEMP
    expo = jnp.exp(scaled - jnp.max(scaled, -1, keepdims=True))
    return expo / jnp.sum(expo, -1, keepdims=True)


def adamw(weight, moment, second, gradient, factor, step_rate, weight_decay):
    clipped = gradient * factor
    moment = BETA_ONE * moment + (1.0 - BETA_ONE) * clipped
    second = BETA_TWO * second + (1.0 - BETA_TWO) * clipped * clipped
    direction = (
        moment / (1.0 - BETA_ONE**STEP) / (jnp.sqrt(second / (1.0 - BETA_TWO**STEP)) + 1e-08)
    )
    return (weight - step_rate * (direction + weight_decay * weight), moment, second)


def layer_full(owned):
    return lax.all_gather(owned.astype(jnp.bfloat16), "fsdp", axis=0, tiled=True).astype(
        jnp.float32
    )


def end_weights(patch_owned, head_owned):
    patch_full, head_full = (
        lax.all_gather(patch_owned.astype(jnp.bfloat16), "fsdp", axis=0, tiled=True),
        lax.all_gather(head_owned.astype(jnp.bfloat16), "fsdp", axis=0, tiled=True),
    )
    return (patch_full.astype(jnp.float32), head_full.astype(jnp.float32))


def backbone(pixels, covered, layers_owned, patch_full, vecs):
    x = embed(pixels, covered, patch_full, vecs)
    seen, gathered = ([], [])
    for depth_index in range(layers_owned.shape[0]):
        layer_weight = layer_full(layers_owned[depth_index])
        seen.append(x)
        gathered.append(layer_weight)
        x = block(x, layer_weight, vecs, depth_index)
    return (x, seen, gathered)


def proto_logits(bottleneck, owned):
    low_rows = bottleneck.astype(jnp.bfloat16)
    return jnp.dot(
        low_rows,
        lax.all_gather(owned.astype(jnp.bfloat16), "fsdp", axis=0, tiled=True).T,
        preferred_element_type=jnp.float32,
    )


def proto_back(grad_logits, owned):
    start_value = jnp.zeros((grad_logits.shape[0], owned.shape[1]), jnp.float32)
    segment = lax.all_gather(owned.astype(jnp.bfloat16), "fsdp", axis=0, tiled=True)
    columns = lax.slice_in_dim(grad_logits, 0, segment.shape[0], axis=1)
    return start_value + jnp.dot(columns, segment, preferred_element_type=jnp.float32)


def per_device(
    patches,
    patch_mask,
    image_valid,
    centre,
    w_patch,
    first_patch,
    second_patch,
    teacher_patch,
    w_layer,
    first_layer,
    second_layer,
    teacher_layer,
    w_head,
    first_head,
    second_head,
    teacher_head,
    w_proto,
    first_proto,
    second_proto,
    teacher_proto,
    vectors,
    first_vectors,
    second_vectors,
    teacher_vectors,
):
    local_images = patches.shape[0]
    batches = local_images // IMG_MB
    layer_count = w_layer.shape[0]
    counted_all = image_valid.astype(jnp.float32)
    counted_total = jnp.maximum(jnp.sum(counted_all), 1.0)
    counted = lax.dynamic_slice_in_dim(
        counted_all, lax.axis_index(("fsdp", "dp")) * local_images, local_images
    )
    pixels_all = patches.astype(jnp.float32)
    covered_all = patch_mask.astype(jnp.float32)
    student_ends = end_weights(w_patch, w_head)
    teacher_ends = end_weights(teacher_patch, teacher_head)
    student_cls, teacher_cls, inputs, kept_weights = ([], [], [], [])
    for batch_index in range(batches):
        pixels = pixels_all[batch_index * IMG_MB : (batch_index + 1) * IMG_MB]
        covered = covered_all[batch_index * IMG_MB : (batch_index + 1) * IMG_MB]
        highest, _, _ = backbone(
            pixels, jnp.zeros_like(covered), teacher_layer, teacher_ends[0], teacher_vectors
        )
        teacher_cls.append(highest[:, 0])
        highest, seen, gathered = backbone(pixels, covered, w_layer, student_ends[0], vectors)
        student_cls.append(highest[:, 0])
        inputs.append(seen)
        kept_weights.append(None)
    cls_student = jnp.concatenate(student_cls, 0)
    cls_teacher = jnp.concatenate(teacher_cls, 0)
    teacher_logits = proto_logits(
        head(cls_teacher, teacher_ends[1], teacher_vectors), teacher_proto
    )
    bottleneck = head(cls_student, student_ends[1], vectors)
    logits = proto_logits(bottleneck, w_proto)
    target = teacher_probs(teacher_logits, centre)
    scaled = logits / STUDENT_TEMP
    shifted = scaled - jnp.max(scaled, -1, keepdims=True)
    log_total = jnp.log(jnp.sum(jnp.exp(shifted), -1, keepdims=True))
    loss_local = jnp.sum(counted * -jnp.sum(target * (shifted - log_total), -1))
    teacher_sum = jnp.sum(counted[:, None] * teacher_logits, 0)
    weighting = (counted / counted_total)[:, None]
    grad_logits = (
        weighting
        * (jnp.exp(shifted - log_total) * jnp.sum(target, -1, keepdims=True) - target)
        / STUDENT_TEMP
    ).astype(jnp.bfloat16)
    grad_bottleneck = proto_back(grad_logits, w_proto)
    back_ends = end_weights(w_patch, w_head)
    _, pullback = jax.vjp(head, cls_student, back_ends[1], vectors)
    grad_cls, grad_head, grad_vectors = pullback(grad_bottleneck)
    grad_patch = jnp.zeros_like(back_ends[0])
    grad_layer = jnp.zeros((layer_count, vectors.shape[1], w_layer.shape[2]), jnp.float32)
    for batch_index in range(batches):
        pixels = pixels_all[batch_index * IMG_MB : (batch_index + 1) * IMG_MB]
        covered = covered_all[batch_index * IMG_MB : (batch_index + 1) * IMG_MB]
        grad_stream = jnp.zeros(inputs[batch_index][0].shape, jnp.float32)
        grad_stream = grad_stream.at[:, 0].set(
            grad_cls[batch_index * IMG_MB : (batch_index + 1) * IMG_MB]
        )
        for depth_index in reversed(range(layer_count)):
            layer_weight = layer_full(w_layer[depth_index])
            _, pullback = jax.vjp(
                partial(block, depth_index=depth_index),
                inputs[batch_index][depth_index],
                layer_weight,
                vectors,
            )
            grad_stream, grad_weight, grad_piece = pullback(grad_stream)
            grad_layer = grad_layer.at[depth_index].add(grad_weight)
            grad_vectors = grad_vectors + grad_piece
        _, pullback = jax.vjp(partial(embed, pixels, covered), back_ends[0], vectors)
        grad_weight, grad_piece = pullback(grad_stream)
        grad_patch = grad_patch + grad_weight
        grad_vectors = grad_vectors + grad_piece
    grad_proto = jnp.dot(
        grad_logits.T, bottleneck.astype(jnp.bfloat16), preferred_element_type=jnp.float32
    )
    owned_parts = (
        lax.psum_scatter(grad_patch, "fsdp", scatter_dimension=0, tiled=True),
        lax.psum_scatter(grad_layer, "fsdp", scatter_dimension=1, tiled=True),
        lax.psum_scatter(grad_head, "fsdp", scatter_dimension=0, tiled=True),
        lax.psum_scatter(grad_proto, "fsdp", scatter_dimension=0, tiled=True),
    )
    owned_grads = (
        lax.psum(owned_parts[0].astype(jnp.bfloat16), "dp").astype(jnp.float32),
        lax.psum(owned_parts[1].astype(jnp.bfloat16), "dp").astype(jnp.float32),
        lax.psum(owned_parts[2].astype(jnp.bfloat16), "dp").astype(jnp.float32),
        lax.psum(owned_parts[3].astype(jnp.bfloat16), "dp").astype(jnp.float32),
    )
    owned_squares = sum((jnp.sum(gradient * gradient) for gradient in owned_grads))
    vector_grad, loss_total, teacher_total = lax.psum(
        (grad_vectors, loss_local, teacher_sum), ("fsdp", "dp")
    )
    squares = lax.psum(owned_squares, "fsdp") + jnp.sum(vector_grad * vector_grad)
    norm_value = jnp.sqrt(squares)
    factor = CLIP_NORM / jnp.maximum(norm_value, CLIP_NORM)
    updated_centre = CENTRE_KEEP * centre + (1.0 - CENTRE_KEEP) * teacher_total / counted_total
    weights_owned = (w_patch, w_layer, w_head, w_proto, vectors)
    moments = (first_patch, first_layer, first_head, first_proto, first_vectors)
    seconds = (second_patch, second_layer, second_head, second_proto, second_vectors)
    teachers = (teacher_patch, teacher_layer, teacher_head, teacher_proto, teacher_vectors)
    gradients = tuple(owned_grads) + (vector_grad,)
    results = [loss_total, counted_total, norm_value, updated_centre]
    for group in range(5):
        updated, moment, second = adamw(
            weights_owned[group],
            moments[group],
            seconds[group],
            gradients[group],
            factor,
            RATES[group],
            DECAYS[group],
        )
        results.extend(
            [
                updated,
                moment,
                second,
                TEACHER_KEEP * teachers[group] + (1.0 - TEACHER_KEEP) * updated,
            ]
        )
    return tuple(results)


def solution(mesh):
    in_specs = (
        P(("fsdp", "dp"), None, None),
        P(("fsdp", "dp"), None),
        P(),
        P(),
        P("fsdp", None),
        P("fsdp", None),
        P("fsdp", None),
        P("fsdp", None),
        P(None, "fsdp", None),
        P(None, "fsdp", None),
        P(None, "fsdp", None),
        P(None, "fsdp", None),
        P("fsdp", None),
        P("fsdp", None),
        P("fsdp", None),
        P("fsdp", None),
        P("fsdp", None),
        P("fsdp", None),
        P("fsdp", None),
        P("fsdp", None),
        P(),
        P(),
        P(),
        P(),
    )
    out_specs = (
        P(),
        P(),
        P(),
        P(),
        P("fsdp", None),
        P("fsdp", None),
        P("fsdp", None),
        P("fsdp", None),
        P(None, "fsdp", None),
        P(None, "fsdp", None),
        P(None, "fsdp", None),
        P(None, "fsdp", None),
        P("fsdp", None),
        P("fsdp", None),
        P("fsdp", None),
        P("fsdp", None),
        P("fsdp", None),
        P("fsdp", None),
        P("fsdp", None),
        P("fsdp", None),
        P(),
        P(),
        P(),
        P(),
    )
    return jax.shard_map(
        per_device, mesh=mesh, in_specs=in_specs, out_specs=out_specs, check_vma=False
    )
```

profile of v0, /device:TPU:0, one launch (start us, length us, event | category | flops | bytes accessed | tf_op | source)
XLA Modules:
  0.0 4227.5 jit_solution(4947273629233612165)
XLA Ops:
  18.3 6.0 convert_element_type.941
  24.3 5.8 convert_element_type.429
  33.7 35.0 all_gather.40
  68.7 31.9 all_gather.45
  109.4 3.6 add_convert_fusion.19
  123.6 3.1 add_convert_fusion.11
  132.5 23.2 all-gather.25.cloned.1.call-done
  158.6 63.5 %all-gather.23.cloned.1.call-done = bf16[1,384,4608]{2,1,0:T(8,128)(2,1)} async-done(((bf16[1,48,4608]{2,1,0:T(8,128)(2,1)}), bf16[1,384,4608]{2,1,0:T(8,128)(2,1)}) %all-gather.23.cloned.1.call-update) | async-done | bytes 3538960 | tf_op jit(solution)/shard_map/all_gather | solution.py:134
  226.0 62.5 %all-gather.21.cloned.1.call-done = bf16[1,384,4608]{2,1,0:T(8,128)(2,1)} async-done(((bf16[1,48,4608]{2,1,0:T(8,128)(2,1)}), bf16[1,384,4608]{2,1,0:T(8,128)(2,1)}) %all-gather.21.cloned.1.call-update) | async-done | bytes 3538960 | tf_op jit(solution)/shard_map/all_gather | solution.py:134
  291.6 3.5 slice_bitcast_fusion
  331.3 5.0 fusion.380
  340.7 5.2 fusion.379
  367.5 3.1 add_convert_fusion.17
  385.5 5.3 fusion.382
  395.1 5.2 fusion.381
  439.0 4.7 multiply_convert_fusion.5
  443.8 3.1 multiply_convert_fusion.7
  455.7 3.9 add_convert_fusion.9
  492.6 3.4 add_convert_fusion.8
  496.1 4.6 multiply_convert_fusion.4
  502.9 3.1 multiply_convert_fusion.6
  512.6 92.3 %all-gather.13.cloned.1.call-done = bf16[2688,2048]{1,0:T(8,128)(2,1)} async-done(((bf16[336,2048]{1,0:T(8,128)(2,1)}), bf16[2688,2048]{1,0:T(8,128)(2,1)}) %all-gather.13.cloned.1.call-update) | async-done | bytes 11010064 | tf_op jit(solution)/shard_map/all_gather | solution.py:142
  606.2 8.7 slice.738
  615.0 8.6 slice.769
  625.5 5.4 fusion.302
  633.9 608.4 %all-gather.19.cloned.1.call-done = bf16[65536,256]{1,0:T(8,128)(2,1)} async-done(((bf16[8192,256]{1,0:T(8,128)(2,1)}), bf16[65536,256]{1,0:T(8,128)(2,1)}) %all-gather.19.cloned.1.call-update) | async-done | bytes 33554448 | tf_op jit(solution)/shard_map/all_gather | solution.py:162
  1242.4 15.6 fusion.378
  1258.8 622.8 %all-gather.15.cloned.1.call-done = bf16[65536,256]{1,0:T(8,128)(2,1)} async-done(((bf16[8192,256]{1,0:T(8,128)(2,1)}), bf16[65536,256]{1,0:T(8,128)(2,1)}) %all-gather.15.cloned.1.call-update) | async-done | bytes 33554448 | tf_op jit(solution)/shard_map/all_gather | solution.py:162
  1881.7 14.7 fusion.158
  1901.1 15.6 multiply_reduce_fusion.59
  1945.6 9.7 multiply_reduce_fusion.27
  1958.1 9.3 fusion.349
  1980.0 4.1 multiply_reduce_fusion.1
  1999.8 4.1 multiply_reduce_fusion.3
  2015.5 9.7 multiply_reduce_fusion.25
  2027.1 9.0 fusion.348
  2062.6 9.1 multiply_reduce_fusion.23
  2075.4 9.8 fusion.347
  2094.4 3.7 convolution_bitcast_fusion.14
  2101.5 4.2 multiply_reduce_fusion.2
  2108.1 6.3 convert_reduce_fusion
  2128.8 3.9 add_bitcast_fusion
  2134.3 3.3 fusion.13
  2137.6 11.1 pad_maximum_fusion
  2148.6 6.8 bitcast_dynamic-update-slice_fusion
  2157.4 5.4 fusion.8
  2167.0 13.2 pad_add_fusion
  2181.8 24.6 fusion.328
  2214.9 8.8 multiply_reduce_fusion.21
  2225.6 8.9 fusion.346
  2242.0 150.1 %reduce-scatter.7.cloned.1.call-done = f32[2,48,4608]{2,1,0:T(8,128)} async-done(((f32[2,384,4608]{2,1,0:T(8,128)}), f32[2,48,4608]{2,1,0:T(8,128)}) %reduce-scatter.7.cloned.1.call-update) | async-done | bytes 1769488 | tf_op jit(solution)/shard_map/reduce_scatter | solution.py:276
  2394.6 358.9 %reduce-scatter.9.cloned.1.call-done = f32[336,2048]{1,0:T(8,128)} async-done(((f32[2688,2048]{1,0:T(8,128)}), f32[336,2048]{1,0:T(8,128)}) %reduce-scatter.9.cloned.1.call-update) | async-done | bytes 2752528 | tf_op jit(solution)/shard_map/reduce_scatter | solution.py:277
  2756.5 1055.6 %reduce-scatter.11.cloned.1.call-done = f32[8192,256]{1,0:T(8,128)} async-done(((f32[65536,256]{1,0:T(8,128)}), f32[8192,256]{1,0:T(8,128)}) %reduce-scatter.11.cloned.1.call-update) | async-done | bytes 8388624 | tf_op jit(solution)/shard_map/reduce_scatter | solution.py:278
  3812.1 5.8 convert_element_type.990
  3819.2 39.7 psum.56
  3859.0 87.6 %all-reduce.76.cloned.1.call-done = (f32[274,384]{1,0:T(8,128)}, f32[65536]{0:T(1024)}) async-done(((f32[274,384]{1,0:T(8,128)}, f32[65536]{0:T(1024)}), (f32[274,384]{1,0:T(8,128)}, f32[65536]{0:T(1024)})) %all-reduce.76.cloned.1.call-update) | async-done | bytes 683024 | tf_op jit(solution)/shard_map/psum | solution.py:287
  3948.3 66.0 %reduce-scatter.5.cloned.1.call-done = f32[48,588]{1,0:T(8,128)} async-done(((f32[384,588]{1,0:T(8,128)}), f32[48,588]{1,0:T(8,128)}) %reduce-scatter.5.cloned.1.call-update) | async-done | bytes 112912 | tf_op jit(solution)/shard_map/reduce_scatter | solution.py:275
  4015.2 11.4 psum.57
  4027.3 112.6 %all-reduce.78.cloned.1.call-done = (bf16[2,48,4608]{2,1,0:T(8,128)(2,1)}, bf16[336,2048]{1,0:T(8,128)(2,1)}, bf16[8192,256]{1,0:T(8,128)(2,1)}) async-done(((bf16[2,48,4608]{2,1,0:T(8,128)(2,1)}, bf16[336,2048]{1,0:T(8,128)(2,1)}, bf16[8192,256]{1,0:T(8,128)(2,1)}), (bf16[2,48,4608]{2,1,0:T(8,128)(2,1)}, bf16[336,2048]{1,0:T(8,128)(2,1)}, bf16[8192,256]{1,0:T(8,128)(2,1)})) %all-reduce.78.cloned.1.call-update) | async-done | bytes 6455312 | tf_op jit(solution)/shard_map/psum | solution.py:282
  4139.8 5.1 fusion.6
  4151.7 22.0 psum.61
  4180.2 6.0 multiply_add_fusion.2
  4187.8 5.0 multiply_add_fusion.1
  4192.9 25.7 multiply_add_fusion
  (1198 shorter events, 407.7 us)
Async XLA Ops:
  7.2 121.4 %all-gather.27.cloned.1.call-start = ((), (), s32[]{:S(2)}) async-start(), calls=%async_computation.15 | async-start | bytes 3981312 | tf_op jit(solution)/shard_map/all_gather | solution.py:134
  9.8 145.9 %all-gather.25.cloned.1.call-start = ((), (), s32[]{:S(2)}) async-start(), calls=%async_computation.14 | async-start | bytes 3981312 | tf_op jit(solution)/shard_map/all_gather | solution.py:134
  10.6 211.6 %all-gather.23.cloned.1.call-start = ((), (), s32[]{:S(2)}) async-start(), calls=%async_computation.13 | async-start | bytes 3981312 | tf_op jit(solution)/shard_map/all_gather | solution.py:134
  13.2 275.3 %all-gather.21.cloned.1.call-start = ((), (), s32[]{:S(2)}) async-start(), calls=%async_computation.12 | async-start | bytes 3981312 | tf_op jit(solution)/shard_map/all_gather | solution.py:134
  13.7 497.4 %all-gather.17.cloned.1.call-start = ((), (), s32[]{:S(2)}) async-start(), calls=%async_computation.6 | async-start | bytes 12386304 | tf_op jit(solution)/shard_map/all_gather | solution.py:142
  15.1 589.8 %all-gather.13.cloned.1.call-start = ((), (), s32[]{:S(2)}) async-start(), calls=%async_computation.4 | async-start | bytes 12386304 | tf_op jit(solution)/shard_map/all_gather | solution.py:142
  18.2 1224.1 %all-gather.19.cloned.1.call-start = ((), (), s32[]{:S(2)}) async-start(), calls=%async_computation.7 | async-start | bytes 37748736 | tf_op jit(solution)/shard_map/all_gather | solution.py:162
  24.3 1857.4 %all-gather.15.cloned.1.call-start = ((), (), s32[]{:S(2)}) async-start(), calls=%async_computation.5 | async-start | bytes 37748736 | tf_op jit(solution)/shard_map/all_gather | solution.py:162
  30.2 2361.9 %reduce-scatter.7.cloned.1.call-start = ((), (), s32[]{:S(2)}) async-start(), calls=%async_computation.9 | async-start | bytes 15925248 | tf_op jit(solution)/shard_map/reduce_scatter | solution.py:276
  31.1 88.0 %copy-start.312 = (f32[2,256]{1,0:T(2,128)}, f32[2,256]{1,0:T(2,128)S(1)}, u32[]{:S(2)}) copy-start(f32[2,256]{1,0:T(2,128)S(1)} %get-tuple-element.322) | copy-start | bytes 6148
  32.1 83.3 %copy-start.227 = (f32[2,256]{0,1:T(8,128)}, f32[2,256]{0,1:T(8,128)S(1)}, u32[]{:S(2)}) copy-start(f32[2,256]{0,1:T(8,128)S(1)} %copy.1079) | copy-start | bytes 6148
  68.7 35.8 copy-start.194
  100.6 14.1 copy-start.123
  103.5 11.2 copy-start.45
  103.5 15.7 copy-start.83
  114.7 317.5 %copy-start.308 = (f32[384]{0:T(512)}, f32[384]{0:T(512)S(1)}, u32[]{:S(2)}) copy-start(f32[384]{0:T(512)S(1)} %get-tuple-element.132) | copy-start | bytes 4612
  114.7 321.9 %copy-start.280 = (f32[384]{0:T(512)}, f32[384]{0:T(512)S(1)}, u32[]{:S(2)}) copy-start(f32[384]{0:T(512)S(1)} %get-tuple-element.128) | copy-start | bytes 4612
  118.0 314.2 %copy-start.12 = (f32[2,257,384]{2,0,1:T(2,128)}, f32[2,257,384]{2,0,1:T(2,128)S(1)}, u32[]{:S(2)}) copy-start(f32[2,257,384]{2,0,1:T(2,128)S(1)} %get-tuple-element.230) | copy-start | bytes 2368516
  122.3 312.7 %copy-start.6 = (f32[2,257,384]{2,1,0:T(8,128)}, f32[2,257,384]{2,1,0:T(8,128)S(1)}, u32[]{:S(2)}) copy-start(f32[2,257,384]{2,1,0:T(8,128)S(1)} %get-tuple-element.238) | copy-start | bytes 2368516
  123.4 32.3 copy-start.286
  123.6 32.1 copy-start.180
  158.6 165.4 %copy-start.18 = (bf16[384,1152]{1,0:T(8,128)(2,1)}, bf16[384,1152]{1,0:T(8,128)(2,1)S(1)}, u32[]{:S(2)}) copy-start(bf16[384,1152]{1,0:T(8,128)(2,1)S(1)} %slice.742) | copy-start | bytes 2654212
  433.3 15.7 copy-start.14
  435.2 17.4 copy-start.8
  451.5 34.0 copy-start.16
  454.4 35.4 copy-start.10
  467.6 15.4 copy-start.91
  488.1 19.4 copy-start.30
  491.2 11.6 copy-start.28
  508.5 106.4 %copy-start.341 = (f32[4]{0:T(128)}, f32[4]{0:T(128)S(1)}, u32[]{:S(2)}) copy-start(f32[4]{0:T(128)S(1)} %multiply_reduce_fusion.57) | copy-start | bytes 52
  508.7 122.2 %copy-start.300 = (bf16[4,384]{1,0:T(4,128)(2,1)}, bf16[4,384]{1,0:T(4,128)(2,1)S(1)}, u32[]{:S(2)}) copy-start(bf16[4,384]{1,0:T(4,128)(2,1)S(1)} %add_convert_fusion.20) | copy-start | bytes 9220
  512.6 120.8 %copy-start.49 = (bf16[2048,256]{0,1:T(8,128)(2,1)}, bf16[2048,256]{0,1:T(8,128)(2,1)S(1)}, u32[]{:S(2)}) copy-start(bf16[2048,256]{0,1:T(8,128)(2,1)S(1)} %slice_bitcast_fusion.4) | copy-start | bytes 3145732
  633.9 624.1 %copy-start.339 = (f32[4]{0:T(128)}, f32[4]{0:T(128)S(1)}, u32[]{:S(2)}) copy-start(f32[4]{0:T(128)S(1)} %get-tuple-element.379) | copy-start | bytes 52
  633.9 1282.9 %copy-start.270 = (f32[4,256]{1,0:T(4,128)}, f32[4,256]{1,0:T(4,128)S(1)}, u32[]{:S(2)}) copy-start(f32[4,256]{1,0:T(4,128)S(1)} %get-tuple-element.380) | copy-start | bytes 12292
  633.9 1282.9 %copy-start.330 = (f32[4]{0:T(128)}, f32[4]{0:T(128)S(1)}, u32[]{:S(2)}) copy-start(f32[4]{0:T(128)S(1)} %add_rsqrt_fusion.10) | copy-start | bytes 52
  1242.4 639.3 %copy-start.125 = (f32[65536]{0:T(1024)S(1)}, f32[65536]{0:T(1024)}, u32[]{:S(2)}) copy-start(f32[65536]{0:T(1024)} %param.39) | copy-start | bytes 786436
  1258.0 643.0 %copy-start.4 = (f32[4,65536]{1,0:T(4,128)}, f32[4,65536]{1,0:T(4,128)S(1)}, u32[]{:S(2)}) copy-start(f32[4,65536]{1,0:T(4,128)S(1)} %get-tuple-element.382) | copy-start | bytes 3145732
  1258.0 643.0 %copy-start.276 = (f32[4]{0:T(128)}, f32[4]{0:T(128)S(1)}, u32[]{:S(2)}) copy-start(f32[4]{0:T(128)S(1)} %get-tuple-element.381) | copy-start | bytes 52
  1258.8 642.3 %copy-start.304 = (f32[4]{0:T(128)}, f32[4]{0:T(128)S(1)}, u32[]{:S(2)}) copy-start(f32[4]{0:T(128)S(1)} %log.8) | copy-start | bytes 52
  1881.6 14.7 copy-start.333
  1898.4 20.0 slice-start.10
  1901.1 15.7 copy-start.306
  1901.1 15.7 copy-start.340
  1901.1 17.3 slice-start.11
  1931.6 13.9 copy-start.157
  1945.5 10.9 copy-start.299
  1958.1 12.5 copy-start.116
  2013.2 12.0 copy-start.66
  2013.3 12.0 copy-start.293
  2013.3 12.2 copy-start.295
  2050.5 12.0 copy-start.158
  2062.5 11.2 copy-start.291
  2137.6 11.1 copy-start.176
  2162.8 590.7 %reduce-scatter.9.cloned.1.call-start = ((), (), s32[]{:S(2)}) async-start(), calls=%async_computation.10 | async-start | bytes 24772608 | tf_op jit(solution)/shard_map/reduce_scatter | solution.py:277
  2180.3 1631.8 %reduce-scatter.11.cloned.1.call-start = ((), (), s32[]{:S(2)}) async-start(), calls=%async_computation.11 | async-start | bytes 75497472 | tf_op jit(solution)/shard_map/reduce_scatter | solution.py:278
  2206.6 1740.0 %all-reduce.76.cloned.1.call-start = ((), (), s32[]{:S(2)}) async-start(), calls=%async_computation.16 | async-start | bytes 1384448 | tf_op jit(solution)/shard_map/psum | solution.py:287
  2211.2 12.7 copy-start.287
  2211.2 13.5 copy-start.285
  2239.9 1774.4 %reduce-scatter.5.cloned.1.call-start = ((), (), s32[]{:S(2)}) async-start(), calls=%async_computation.8 | async-start | bytes 1105920 | tf_op jit(solution)/shard_map/reduce_scatter | solution.py:275
  2242.0 1897.9 %all-reduce.78.cloned.1.call-start = ((), (), s32[]{:S(2)}) async-start(), calls=%async_computation.17 | async-start | bytes 12910592 | tf_op jit(solution)/shard_map/psum | solution.py:282
  3818.0 128.6 %copy-start.126 = (f32[65536]{0:T(1024)S(1)}, f32[65536]{0:T(1024)}, u32[]{:S(2)}) copy-start(f32[65536]{0:T(1024)} %param.39) | copy-start | bytes 786436
  4026.6 118.3 %copy-start.250 = (bf16[48,588]{1,0:T(8,128)(2,1)}, bf16[48,588]{1,0:T(8,128)(2,1)S(1)}, u32[]{:S(2)}) copy-start(bf16[48,588]{1,0:T(8,128)(2,1)S(1)} %psum.57) | copy-start | bytes 169348
  4146.2 33.9 copy-start.79
  4146.2 33.9 copy-start.80
  (320 other events, 1185.3 us)
Sparse Core Ops, SparseCore 0:
  10.8 78.2 all-gather.26
  91.8 63.8 all-gather.24
  158.4 63.6 all-gather.22
  224.7 63.6 all-gather.20
  291.0 155.7 all-gather.16
  449.4 155.4 all-gather.12
  606.4 635.9 all-gather.18
  1243.9 637.6 all-gather.14
  2162.9 229.1 reduce-scatter.6
  2395.9 357.5 reduce-scatter.8
  2757.7 1054.3 reduce-scatter.10
  3819.3 127.2 all-reduce.75
  3950.5 63.7 reduce-scatter.4
  4018.0 121.8 all-reduce.77
where the time goes:
time: 4240 us; the launch traced here: 4230 us
  waiting for transfers between devices  3300 us (78%)
  other arithmetic  339 us (8%)
  matrix products  271 us (6%)
  local copies, waits for them, and re-layouts  146 us (3%)
  blocking collectives  140 us (3%)
    all_gather x2, waiting for transfers between devices, proto_logits(): lax.all_gather(owned.astype(jnp.bfloat16), 'fsdp', axis=0, tiled=True)  1230 us
    reduce_scatter x1, waiting for transfers between devices, per_device(): lax.psum_scatter(grad_proto, 'fsdp', scatter_dimension=0, tiled=True)  1060 us
    reduce_scatter x1, waiting for transfers between devices, per_device(): lax.psum_scatter(grad_head, 'fsdp', scatter_dimension=0, tiled=True)  359 us
    reduce_scatter x1, waiting for transfers between devices, per_device(): lax.psum_scatter(grad_layer, 'fsdp', scatter_dimension=1, tiled=True)  150 us
    all_gather x4, waiting for transfers between devices, layer_full(): lax.all_gather(owned.astype(jnp.bfloat16), 'fsdp', axis=0, tiled=True)  149 us
    dot_general x82, matrix products, matmul(): jnp.dot(lowered(left), lowered(right), precision=PRECISION_MODE)  136 us
    psum x1, waiting for transfers between devices, per_device(): lax.psum(owned_parts[1].astype(jnp.bfloat16), 'dp').astype(jnp.float32)  113 us
    all_gather x2, waiting for transfers between devices, end_weights(): lax.all_gather(head_owned.astype(jnp.bfloat16), 'fsdp', axis=0, tiled=True)  92.3 us
  transfers between devices with their start and end apart: 14, of which 12 were waited for; matrix products, arithmetic and copies ran while one was open for 10% of the time, Pallas kernels for 0%

commit v1 on v0

v1 whole, which is shorter than its diff:
```python
from functools import partial

import jax
import jax.numpy as jnp
from jax import lax
from jax.sharding import PartitionSpec as P

HEADS = 6
STEP = 10
STUDENT_TEMP = 0.1
TEACHER_TEMP = 0.07
CENTRE_KEEP = 0.9
TEACHER_KEEP = 0.8
BETA_ONE = 0.9
BETA_TWO = 0.999
CLIP_NORM = 0.01
RATES = (0.1, 0.15, 0.07, 0.5, 0.5)
DECAYS = (0.04, 0.04, 0.04, 0.04, 0.0)
F32 = jnp.float32
BF16 = jnp.bfloat16


def dot(left, right, dims):
    return lax.dot_general(left, right, (dims, ((), ())), preferred_element_type=F32)


@jax.custom_vjp
def matmul(left, right):
    return jnp.dot(left.astype(BF16), right.astype(BF16), preferred_element_type=F32)


def matmul_keep(left, right):
    left, right = left.astype(BF16), right.astype(BF16)
    return jnp.dot(left, right, preferred_element_type=F32), (left, right)


def matmul_pull(kept, grad):
    left, right = kept
    grad = grad.astype(BF16)
    width = left.ndim - 1
    lead = tuple(range(width))
    return dot(grad, right, ((width,), (1,))), dot(left, grad, (lead, lead))


matmul.defvjp(matmul_keep, matmul_pull)


@partial(jax.custom_vjp, nondiff_argnums=(2,))
def contract(left, right, spec):
    return jnp.einsum(spec, left.astype(BF16), right.astype(BF16), preferred_element_type=F32)


def contract_keep(left, right, spec):
    left, right = left.astype(BF16), right.astype(BF16)
    return jnp.einsum(spec, left, right, preferred_element_type=F32), (left, right)


def contract_pull(spec, kept, grad):
    left, right = kept
    grad = grad.astype(BF16)
    operands, result = spec.split("->")
    first, second = operands.split(",")
    return (
        jnp.einsum(result + "," + second + "->" + first, grad, right, preferred_element_type=F32),
        jnp.einsum(result + "," + first + "->" + second, grad, left, preferred_element_type=F32),
    )


contract.defvjp(contract_keep, contract_pull)


def layer_norm(x, gain, shift):
    centred = x - jnp.mean(x, -1, keepdims=True)
    spread = jnp.mean(centred * centred, -1, keepdims=True)
    return centred * lax.rsqrt(spread + 1e-06) * gain + shift


def embed(pixels, covered, patch_weight, vecs):
    length = pixels.shape[1] + 1
    tokens = matmul(pixels, patch_weight.T) + vecs[length + 2]
    covered_col = covered[..., None]
    tokens = tokens * (1.0 - covered_col) + vecs[length + 1] * covered_col
    leading = jnp.broadcast_to(vecs[length], (pixels.shape[0], 1, vecs.shape[1]))
    return jnp.concatenate([leading, tokens], 1) + vecs[:length]


def mlp(x, layer_weight, rows):
    model_width = x.shape[-1]
    normed = layer_norm(x, rows[3], rows[4])
    hidden = (layer_weight.shape[1] - 4 * model_width) // 2
    up = layer_weight[:, 4 * model_width : 4 * model_width + hidden]
    down = layer_weight[:, 4 * model_width + hidden :]
    activated = jax.nn.gelu(matmul(normed, up))
    return x + rows[5] * matmul(activated, down.T)


def block(x, layer_weight, vecs, depth_index, last):
    images, length, model_width = x.shape
    rows = vecs[length + 3 + 6 * depth_index : length + 9 + 6 * depth_index]
    head_width = model_width // HEADS
    normed = layer_norm(x, rows[0], rows[1])
    asking = normed[:, :1] if last else normed
    queries = matmul(asking, layer_weight[:, :model_width])
    pair = matmul(normed, layer_weight[:, model_width : 3 * model_width])
    queries = queries.reshape(images, -1, HEADS, head_width)
    pair = pair.reshape(images, length, 2, HEADS, head_width)
    scores = contract(queries, pair[:, :, 0], "nqhe,nkhe->nhqk") * head_width ** (-0.5)
    attention = jax.nn.softmax(scores, -1)
    mixture = contract(attention, pair[:, :, 1], "nhqk,nkhe->nqhe")
    mixture = mixture.reshape(images, -1, model_width)
    kept = x[:, :1] if last else x
    x = kept + rows[2] * matmul(mixture, layer_weight[:, 3 * model_width : 4 * model_width])
    return mlp(x, layer_weight, rows)


def backbone(patch_weight, layers, vecs, pixels, covered):
    x = embed(pixels, covered, patch_weight, vecs)
    count = len(layers)
    for depth_index in range(count):
        x = block(x, layers[depth_index], vecs, depth_index, depth_index == count - 1)
    return x[:, 0]


def gathered(owned, axis):
    return lax.all_gather(owned.astype(BF16), "fsdp", axis=axis, tiled=True)


def gathered_layers(owned):
    return [gathered(owned[index], 0) for index in range(owned.shape[0])]


def gelu_slope(x):
    _, pull = jax.vjp(jax.nn.gelu, x)
    return pull(jnp.ones_like(x))[0]


def head_forward(cls, weight, vecs):
    width, hidden = cls.shape[1], weight.shape[1]
    low_n = layer_norm(cls, vecs[-2], vecs[-1]).astype(BF16)
    pre_a = jnp.dot(low_n, weight[:width], preferred_element_type=F32)
    low_a = jax.nn.gelu(pre_a).astype(BF16)
    pre_b = jnp.dot(low_a, weight[width : width + hidden], preferred_element_type=F32)
    low_b = jax.nn.gelu(pre_b).astype(BF16)
    raw = dot(low_b, weight[width + hidden :], ((1,), (1,)))
    return low_n, pre_a, low_a, pre_b, low_b, raw


def unit(raw):
    return raw * lax.rsqrt(jnp.sum(raw * raw, -1, keepdims=True) + 1e-06)


def adamw(weight, moment, second, gradient, factor, step_rate, weight_decay):
    clipped = gradient * factor
    moment = BETA_ONE * moment + (1.0 - BETA_ONE) * clipped
    second = BETA_TWO * second + (1.0 - BETA_TWO) * clipped * clipped
    direction = (
        moment / (1.0 - BETA_ONE**STEP) / (jnp.sqrt(second / (1.0 - BETA_TWO**STEP)) + 1e-08)
    )
    return (weight - step_rate * (direction + weight_decay * weight), moment, second)


def per_device(
    patches,
    patch_mask,
    image_valid,
    centre,
    w_patch,
    first_patch,
    second_patch,
    teacher_patch,
    w_layer,
    first_layer,
    second_layer,
    teacher_layer,
    w_head,
    first_head,
    second_head,
    teacher_head,
    w_proto,
    first_proto,
    second_proto,
    teacher_proto,
    vectors,
    first_vectors,
    second_vectors,
    teacher_vectors,
):
    everyone = ("fsdp", "dp")
    local = patches.shape[0]
    place = lax.axis_index(everyone) * local
    fsdp_index = lax.axis_index("fsdp")
    counted = image_valid.astype(F32)
    counted_total = jnp.maximum(jnp.sum(counted), 1.0)
    covered = patch_mask.astype(F32)

    teacher_patch_full = gathered(teacher_patch, 0)
    teacher_layers_full = gathered_layers(teacher_layer)
    patch_full = gathered(w_patch, 0)
    layers_full = gathered_layers(w_layer)
    teacher_head_full = gathered(teacher_head, 0)
    head_full = gathered(w_head, 0)

    teacher_cls = backbone(
        teacher_patch_full, teacher_layers_full, teacher_vectors, patches, jnp.zeros_like(covered)
    )
    cls, pull_backbone = jax.vjp(
        lambda pw, lw, vv: backbone(pw, lw, vv, patches, covered),
        patch_full.astype(F32),
        [weight.astype(F32) for weight in layers_full],
        vectors,
    )

    teacher_unit = unit(head_forward(teacher_cls, teacher_head_full, teacher_vectors)[-1])
    low_n, pre_a, low_a, pre_b, low_b, raw = head_forward(cls, head_full, vectors)
    bottleneck, pull_unit = jax.vjp(unit, raw)
    both = jnp.concatenate([teacher_unit.astype(BF16), bottleneck.astype(BF16)], -1)
    both = lax.all_gather(both, everyone, axis=0, tiled=True)
    width = raw.shape[1]
    teacher_rows, student_rows = both[:, :width], both[:, width:]

    owned_k = w_proto.shape[0]
    low_proto = w_proto.astype(BF16)
    teacher_logits = dot(teacher_rows, teacher_proto.astype(BF16), ((1,), (1,)))
    logits = dot(student_rows, low_proto, ((1,), (1,)))
    own_centre = lax.dynamic_slice_in_dim(centre, fsdp_index * owned_k, owned_k)
    scaled_t = (teacher_logits - own_centre) / TEACHER_TEMP
    scaled_s = logits / STUDENT_TEMP
    max_t = jnp.max(scaled_t, -1)
    max_s = jnp.max(scaled_s, -1)
    expo_t = jnp.exp(scaled_t - max_t[:, None])
    expo_s = jnp.exp(scaled_s - max_s[:, None])
    parts = jnp.stack(
        [
            max_t,
            jnp.sum(expo_t, -1),
            max_s,
            jnp.sum(expo_s, -1),
            jnp.sum(expo_t * (scaled_s - max_s[:, None]), -1),
        ]
    )
    parts = lax.all_gather(parts, "fsdp", axis=0)
    top_t = jnp.max(parts[:, 0], 0)
    lift_t = jnp.exp(parts[:, 0] - top_t)
    total_t = jnp.sum(parts[:, 1] * lift_t, 0)
    top_s = jnp.max(parts[:, 2], 0)
    total_s = jnp.sum(parts[:, 3] * jnp.exp(parts[:, 2] - top_s), 0)
    crossed = jnp.sum(lift_t * (parts[:, 4] + (parts[:, 2] - top_s) * parts[:, 1]), 0) / total_t
    losses = jnp.log(total_s) - crossed
    loss_total = jnp.sum(counted * losses)
    weighting = counted / counted_total / STUDENT_TEMP
    share_s = weighting * jnp.exp(max_s - top_s) / total_s
    share_t = weighting * jnp.exp(max_t - top_t) / total_t
    grad_logits = (expo_s * share_s[:, None] - expo_t * share_t[:, None]).astype(BF16)
    teacher_sum = jnp.sum(counted[:, None] * teacher_logits, 0)
    teacher_total = lax.all_gather(teacher_sum, "fsdp", axis=0, tiled=True)
    grad_proto = dot(grad_logits, student_rows, ((0,), (0,)))
    grad_rows = jnp.dot(grad_logits, low_proto, preferred_element_type=F32)
    dp_count = lax.axis_size("dp")
    grad_rows = grad_rows.reshape(-1, dp_count, local, width)
    grad_rows = lax.dynamic_index_in_dim(grad_rows, lax.axis_index("dp"), 1, keepdims=False)
    grad_bottleneck = lax.psum_scatter(grad_rows, "fsdp", scatter_dimension=0, tiled=False)

    model_width, hidden = cls.shape[1], head_full.shape[1]
    low_dz = pull_unit(grad_bottleneck)[0].astype(BF16)
    grad_b = jnp.dot(low_dz, head_full[model_width + hidden :], preferred_element_type=F32)
    low_db = (grad_b * gelu_slope(pre_b)).astype(BF16)
    grad_a = dot(low_db, head_full[model_width : model_width + hidden], ((1,), (1,)))
    low_da = (grad_a * gelu_slope(pre_a)).astype(BF16)
    grad_n = dot(low_da, head_full[:model_width], ((1,), (1,)))
    _, pull_norm = jax.vjp(layer_norm, cls, vectors[-2], vectors[-1])
    grad_cls, grad_gain, grad_shift = pull_norm(grad_n)

    packed = jnp.concatenate([low_n, low_a, low_dz, low_da, low_db, low_b], -1)
    packed = lax.all_gather(packed, everyone, axis=0, tiled=True)
    total_rows = model_width + hidden + width
    lefts, rights = packed[:, :total_rows], packed[:, total_rows:]
    own_rows = w_head.shape[0]
    start = fsdp_index * own_rows
    left = lax.dynamic_slice_in_dim(lefts, start, own_rows, 1)
    row = start + lax.broadcasted_iota(jnp.int32, (1, own_rows), 1)
    kind = jnp.where(row < model_width, 0, jnp.where(row < model_width + hidden, 1, 2))
    left = jnp.concatenate([jnp.where(kind == index, left, 0) for index in range(3)], 0)
    right = jnp.concatenate(
        [rights[:, index * hidden : (index + 1) * hidden] for index in range(3)], 0
    )
    grad_head = dot(left, right, ((0,), (0,)))

    grad_patch, grad_layers, grad_vectors = pull_backbone(grad_cls)
    grad_vectors = grad_vectors.at[-2].add(grad_gain).at[-1].add(grad_shift)
    own_patch = lax.psum_scatter(
        grad_patch.astype(BF16), "fsdp", scatter_dimension=0, tiled=True
    )
    own_layers = [
        lax.psum_scatter(piece.astype(BF16), "fsdp", scatter_dimension=0, tiled=True)
        for piece in grad_layers
    ]
    own_patch, own_layers = lax.psum((own_patch, jnp.stack(own_layers)), "dp")
    own_patch, own_layers = own_patch.astype(F32), own_layers.astype(F32)
    vector_grad = lax.psum(grad_vectors, everyone)
    owned_grads = (own_patch, own_layers, grad_head, grad_proto)
    owned_squares = sum((jnp.sum(gradient * gradient) for gradient in owned_grads))
    squares = lax.psum(owned_squares, "fsdp") + jnp.sum(vector_grad * vector_grad)
    norm_value = jnp.sqrt(squares)
    factor = CLIP_NORM / jnp.maximum(norm_value, CLIP_NORM)
    updated_centre = CENTRE_KEEP * centre + (1.0 - CENTRE_KEEP) * teacher_total / counted_total
    weights_owned = (w_patch, w_layer, w_head, w_proto, vectors)
    moments = (first_patch, first_layer, first_head, first_proto, first_vectors)
    seconds = (second_patch, second_layer, second_head, second_proto, second_vectors)
    teachers = (teacher_patch, teacher_layer, teacher_head, teacher_proto, teacher_vectors)
    gradients = owned_grads + (vector_grad,)
    results = [loss_total, counted_total, norm_value, updated_centre]
    for group in range(5):
        updated, moment, second = adamw(
            weights_owned[group],
            moments[group],
            seconds[group],
            gradients[group],
            factor,
            RATES[group],
            DECAYS[group],
        )
        results.extend(
            [
                updated,
                moment,
                second,
                TEACHER_KEEP * teachers[group] + (1.0 - TEACHER_KEEP) * updated,
            ]
        )
    return tuple(results)


def solution(mesh):
    whole, rows, middle = P(), P("fsdp", None), P(None, "fsdp", None)
    in_specs = (
        (P(("fsdp", "dp"), None, None), P(("fsdp", "dp"), None), whole, whole)
        + (rows,) * 4
        + (middle,) * 4
        + (rows,) * 8
        + (whole,) * 4
    )
    out_specs = (whole,) * 4 + (rows,) * 4 + (middle,) * 4 + (rows,) * 8 + (whole,) * 4
    return jax.shard_map(
        per_device, mesh=mesh, in_specs=in_specs, out_specs=out_specs, check_vma=False
    )
```

time: 4240 us -> 1430 us (0.34)
  waiting for transfers between devices: 3300 us -> 699 us
  other arithmetic: 339 us -> 187 us
  blocking collectives: 140 us -> 238 us
  matrix products: 271 us -> 189 us
  local copies, waits for them, and re-layouts: 146 us -> 80 us
    reduce_scatter x4 -> x3, waiting for transfers between devices: 1630 us -> 147 us  [the longest x2 94.4 us: per_device(): lax.psum_scatter(piece.astype(BF16), 'fsdp', scatter_dimension=0, tiled=T...]
    all_gather x8 -> x7, waiting for transfers between devices: 1470 us -> 396 us  [the longest x6 348 us: gathered(): return lax.all_gather(owned.astype(BF16), 'fsdp', axis=axis, tiled=True)]
    all_gather x2 -> x5, blocking collectives: 66.9 us -> 170 us  [the longest x2 66.5 us: gathered(): return lax.all_gather(owned.astype(BF16), 'fsdp', axis=axis, tiled=True)]
    dot_general x114 -> x68, matrix products: 250 us -> 189 us  [the longest x8 34.8 us: dot(): lax.dot_general(left, right, (dims, ((), ())), preferred_element_type=F32)]
    convert_element_type x42 -> x21, other arithmetic: 83.5 us -> 37.4 us  [the longest x1 10.6 us: block(): contract(queries, pair[:, :, 0], 'nqhe,nkhe->nhqk') * head_width ** (-0.5)]
    reduce_sum x23 -> x9, other arithmetic: 54.8 us -> 9.78 us  [layer_norm(): centred = x - jnp.mean(x, -1, keepdims=True)]
    psum x2, waiting for transfers between devices: 200 us -> 155 us  [the longest x1 127 us: per_device(): vector_grad = lax.psum(grad_vectors, everyone)]
  transfers between devices with their start and end apart: 14 -> 12, of which waited for: 12 -> 11; matrix products, arithmetic and copies ran while one was open for 10% -> 16% of each run, Pallas kernels for 0% -> 0%
where the time goes in v1:
time: 1430 us; the launch traced here: 1420 us
  waiting for transfers between devices  699 us (49%)
  blocking collectives  238 us (17%)
  matrix products  189 us (13%)
  other arithmetic  187 us (13%)
  local copies, waits for them, and re-layouts  80 us (6%)
  between operations  24.5 us (2%)
    all_gather x6, waiting for transfers between devices, gathered(): return lax.all_gather(owned.astype(BF16), 'fsdp', axis=axis, tiled=True)  348 us
    psum x1, waiting for transfers between devices, per_device(): vector_grad = lax.psum(grad_vectors, everyone)  127 us
    reduce_scatter x2, waiting for transfers between devices, per_device(): lax.psum_scatter(piece.astype(BF16), 'fsdp', scatter_dimension=0, tiled=T...  94.4 us
    all_gather x2, blocking collectives, gathered(): return lax.all_gather(owned.astype(BF16), 'fsdp', axis=axis, tiled=True)  66.5 us
    reduce_scatter x1, waiting for transfers between devices, per_device(): lax.psum_scatter(grad_patch.astype(BF16), 'fsdp', scatter_dimension=0, ti...  52.8 us
    all_gather x1, waiting for transfers between devices, per_device(): packed = lax.all_gather(packed, everyone, axis=0, tiled=True)  47.6 us
    add x5, other arithmetic, per_device(): TEACHER_KEEP * teachers[group] + (1.0 - TEACHER_KEEP) * updated  43 us
    all_gather x1, blocking collectives, per_device(): both = lax.all_gather(both, everyone, axis=0, tiled=True)  41.6 us
  transfers between devices with their start and end apart: 12, of which 11 were waited for; matrix products, arithmetic and copies ran while one was open for 16% of the time, Pallas kernels for 0%

profile of v1, /device:TPU:0, one launch (start us, length us, event | category | flops | bytes accessed | tf_op | source)
XLA Modules:
  0.0 1419.2 jit_solution(9288674974436962950)
XLA Ops:
  12.3 3.1 convert_element_type.355
  15.5 3.1 convert_element_type.384
  20.4 34.0 %all_gather.39 = bf16[384,588]{1,0:T(8,128)(2,1)S(1)} all-gather(bf16[48,588]{1,0:T(8,128)(2,1)S(1)} %convert_element_type.331), channel_id=1, replica_groups=mesh['fsdp'=8,'dp'=4] {'fsdp'}, dimensions={0}, use_global_device_ids=true | all-gather | bytes 508032 | tf_op jit(solution)/shard_map/all_gather | solution.py:125
  59.9 32.6 %all_gather.43 = bf16[384,588]{1,0:T(8,128)(2,1)S(1)} all-gather(bf16[48,588]{1,0:T(8,128)(2,1)S(1)} %convert_element_type.359), channel_id=1, replica_groups=mesh['fsdp'=8,'dp'=4] {'fsdp'}, dimensions={0}, use_global_device_ids=true | all-gather | bytes 508032 | tf_op jit(solution)/shard_map/all_gather | solution.py:125
  97.4 4.3 multiply_reduce_fusion.20
  110.0 3.0 add_convert_fusion.9
  113.1 3.7 convolution_convert_fusion.3
  119.6 4.0 copy.259
  125.3 3.2 fusion.80
  128.4 5.3 fusion.347
  133.8 5.2 fusion.66
  142.2 7.1 fusion.349
  151.4 4.0 all-gather.22.cloned.1.call-done
  165.4 56.5 %all-gather.24.cloned.1.call-done = bf16[1,384,4608]{2,1,0:T(8,128)(2,1)} async-done(((bf16[1,48,4608]{2,1,0:T(8,128)(2,1)}), bf16[1,384,4608]{2,1,0:T(8,128)(2,1)}) %all-gather.24.cloned.1.call-update) | async-done | bytes 3538960 | tf_op jit(solution)/shard_map/all_gather | solution.py:125
  231.6 7.3 fusion.95
  238.9 9.3 fusion.345
  252.0 3.4 convolution_convert_fusion.5
  261.9 3.1 fusion.116
  265.0 4.4 fusion.117
  275.1 3.1 add_convert_fusion.7
  278.2 10.0 all-gather.26.cloned.1.call-done
  288.2 3.5 convolution_convert_fusion
  291.7 3.9 copy.295
  319.7 126.9 %all-gather.16.cloned.1.call-done = bf16[2688,2048]{1,0:T(8,128)(2,1)} async-done(((bf16[336,2048]{1,0:T(8,128)(2,1)}), bf16[2688,2048]{1,0:T(8,128)(2,1)}) %all-gather.16.cloned.1.call-update) | async-done | bytes 11010064 | tf_op jit(solution)/shard_map/all_gather | solution.py:125
  446.6 5.4 fusion.209
  454.3 150.4 %all-gather.18.cloned.1.call-done = bf16[2688,2048]{1,0:T(8,128)(2,1)} async-done(((bf16[336,2048]{1,0:T(8,128)(2,1)}), bf16[2688,2048]{1,0:T(8,128)(2,1)}) %all-gather.18.cloned.1.call-update) | async-done | bytes 11010064 | tf_op jit(solution)/shard_map/all_gather | solution.py:125
  607.1 4.6 fusion.12
  614.0 41.6 %all-gather.5 = bf16[32,4,512]{2,1,0:T(4,128)(2,1)} all-gather(bf16[1,4,512]{2,1,0:T(4,128)(2,1)S(1)} %maximum_bitcast_fusion), channel_id=1, replica_groups=mesh['fsdp'=8,'dp'=4] {'fsdp','dp'}, dimensions={0}, use_global_device_ids=true | all-gather | bytes 135168 | tf_op jit(solution)/shard_map/all_gather | solution.py:217
  656.6 5.0 fusion.350
  661.6 6.5 fusion.38
  668.1 3.2 multiply_reduce_fusion.5
  672.6 30.5 %all-gather.6 = f32[8,5,128]{2,1,0:T(8,128)S(1)} all-gather(f32[1,5,128]{2,1,0:T(8,128)} %bitcast.416), channel_id=6, replica_groups=mesh['fsdp'=8,'dp'=4] {'fsdp'}, dimensions={0}, use_global_device_ids=true | all-gather | bytes 23040 | tf_op jit(solution)/shard_map/all_gather | solution.py:241
  710.9 5.5 subtract_convert_fusion
  717.7 4.8 fusion.49
  725.6 34.6 %all-reduce.34 = f32[8,4,256]{2,1,0:T(4,128)} all-reduce(f32[8,4,256]{2,1,0:T(4,128)} %dynamic-slice_bitcast_fusion), channel_id=7, replica_groups=mesh['fsdp'=8,'dp'=4] {'fsdp'}, use_global_device_ids=true, to_apply=%region_42.0.clone | all-reduce | flops 8192 | bytes 65536
  766.3 6.4 constant_dynamic-update-slice_fusion.2
  786.2 6.5 multiply_reduce_fusion.14
  797.1 5.9 fusion.329
  805.6 7.4 fusion.20
  822.9 6.3 multiply_reduce_fusion.12
  829.2 5.2 multiply_reduce_fusion.11
  841.2 5.8 convolution_bitcast_fusion.3
  847.0 9.4 multiply_reduce_fusion
  856.5 10.6 multiply_convert_fusion
  867.1 4.5 convolution_bitcast_fusion.2
  873.0 5.4 convolution_bitcast_fusion.1
  900.1 4.8 fusion.318
  905.2 5.6 multiply_reduce_fusion.10
  910.8 4.4 fusion.327
  921.9 31.0 %all_gather.51 = f32[65536]{0:T(1024)S(1)} all-gather(f32[8192]{0:T(1024)S(1)} %copy-done.105), channel_id=1, replica_groups=mesh['fsdp'=8,'dp'=4] {'fsdp'}, dimensions={0}, use_global_device_ids=true | all-gather | bytes 294912 | tf_op jit(solution)/shard_map/all_gather | solution.py:255
  953.6 11.6 reduce-scatter.6.cloned.1.call-done
  965.2 82.8 %reduce-scatter.8.cloned.1.call-done = bf16[48,4608]{1,0:T(8,128)(2,1)} async-done(((bf16[384,4608]{1,0:T(8,128)(2,1)}), bf16[48,4608]{1,0:T(8,128)(2,1)}) %reduce-scatter.8.cloned.1.call-update) | async-done | bytes 442384 | tf_op jit(solution)/shard_map/reduce_scatter | solution.py:294
  1050.3 7.9 multiply_reduce_fusion.3
  1058.2 52.8 %reduce-scatter.4.cloned.1.call-done = bf16[48,588]{1,0:T(8,128)(2,1)} async-done(((bf16[384,588]{1,0:T(8,128)(2,1)}), bf16[48,588]{1,0:T(8,128)(2,1)}) %reduce-scatter.4.cloned.1.call-update) | async-done | bytes 56464 | tf_op jit(solution)/shard_map/reduce_scatter | solution.py:290
  1111.0 11.2 psum.28
  1122.8 47.6 %all-gather.28.cloned.1.call-done = bf16[32,4,8832]{2,1,0:T(4,128)(2,1)} async-done(((bf16[1,4,8832]{2,1,0:T(4,128)(2,1)}), bf16[32,4,8832]{2,1,0:T(4,128)(2,1)}) %all-gather.28.cloned.1.call-update) | async-done | bytes 2261008 | tf_op jit(solution)/shard_map/all_gather | solution.py:274
  1170.4 4.0 reshape.780
  1176.2 3.0 multiply_reduce_fusion.6
  1179.2 28.2 %all-reduce.38.cloned.1.call-done = bf16[2,48,4608]{2,1,0:T(8,128)(2,1)} async-done(((bf16[2,48,4608]{2,1,0:T(8,128)(2,1)}), bf16[2,48,4608]{2,1,0:T(8,128)(2,1)}) %all-reduce.38.cloned.1.call-update) | async-done | bytes 884752 | tf_op jit(solution)/shard_map/psum | solution.py:297
  1212.3 127.0 %all-reduce.40.cloned.1.call-done = f32[274,384]{1,0:T(8,128)} async-done(((f32[274,384]{1,0:T(8,128)}), f32[274,384]{1,0:T(8,128)}) %all-reduce.40.cloned.1.call-update) | async-done | bytes 420880 | tf_op jit(solution)/shard_map/psum | solution.py:299
  1341.0 23.0 %psum.30 = f32[]{:T(128)} all-reduce(f32[]{:T(128)S(6)} %add.655), channel_id=1, replica_groups=mesh['fsdp'=8,'dp'=4] {'fsdp'}, use_global_device_ids=true, to_apply=%region_65.66 | all-reduce | flops 1 | bytes 8 | tf_op jit(solution)/shard_map/psum | solution.py:302
  1366.3 27.8 %multiply_add_fusion = (f32[8192,256]{1,0:T(8,128)}, f32[8192,256]{1,0:T(8,128)}, f32[8192,256]{1,0:T(8,128)}, f32[8192,256]{1,0:T(8,128)}) fusion(f32[8192,256]{1,0:T(8,128)} %param.47, f32[8192,256]{1,0:T(8,128)} %param.44, f32[8192,256]{1,0:T(8,128)} %get-tuple-element.210, f32[]{:T(128)S(6)} %div.370, f32[8192,256]{1,0:T(8,128)} %param.45, ...), kind=kLoop, calls=%fused_computation.23 | loop fusion | flops 39845888 | bytes 75497472 | tf_op jit(solution)/shard_map/add | solution.py:327
  1394.2 8.9 multiply_add_fusion.2
  1405.9 4.1 multiply_add_fusion.4
  (704 shorter events, 199.4 us)
Async XLA Ops:
  7.2 105.9 %all-gather.20.cloned.1.call-start = ((), (), s32[]{:S(2)}) async-start(), calls=%async_computation.10 | async-start | bytes 3981312 | tf_op jit(solution)/shard_map/all_gather | solution.py:125
  9.8 145.6 %all-gather.22.cloned.1.call-start = ((), (), s32[]{:S(2)}) async-start(), calls=%async_computation.11 | async-start | bytes 3981312 | tf_op jit(solution)/shard_map/all_gather | solution.py:125
  10.6 211.3 %all-gather.24.cloned.1.call-start = ((), (), s32[]{:S(2)}) async-start(), calls=%async_computation.12 | async-start | bytes 3981312 | tf_op jit(solution)/shard_map/all_gather | solution.py:125
  11.7 276.5 %all-gather.26.cloned.1.call-start = ((), (), s32[]{:S(2)}) async-start(), calls=%async_computation.13 | async-start | bytes 3981312 | tf_op jit(solution)/shard_map/all_gather | solution.py:125
  12.3 434.3 %all-gather.16.cloned.1.call-start = ((), (), s32[]{:S(2)}) async-start(), calls=%async_computation.3 | async-start | bytes 12386304 | tf_op jit(solution)/shard_map/all_gather | solution.py:125
  15.4 589.2 %all-gather.18.cloned.1.call-start = ((), (), s32[]{:S(2)}) async-start(), calls=%async_computation.4 | async-start | bytes 12386304 | tf_op jit(solution)/shard_map/all_gather | solution.py:125
  18.6 946.6 %reduce-scatter.6.cloned.1.call-start = ((), (), s32[]{:S(2)}) async-start(), calls=%async_computation.6 | async-start | bytes 3981312 | tf_op jit(solution)/shard_map/reduce_scatter | solution.py:294
  19.4 37.7 %copy-start.46 = (f32[257,384]{1,0:T(8,128)}, f32[257,384]{1,0:T(8,128)S(1)}, u32[]{:S(2)}) copy-start(f32[257,384]{1,0:T(8,128)S(1)} %slice.368) | copy-start | bytes 1184260
  20.3 89.7 %copy-start.126 = (f32[384]{0:T(512)}, f32[384]{0:T(512)S(1)}, u32[]{:S(2)}) copy-start(f32[384]{0:T(512)S(1)} %get-tuple-element.91) | copy-start | bytes 4612
  20.3 89.7 %copy-start.6 = (f32[257,384]{1,0:T(8,128)}, f32[257,384]{1,0:T(8,128)S(1)}, u32[]{:S(2)}) copy-start(f32[257,384]{1,0:T(8,128)S(1)} %slice.407) | copy-start | bytes 1184260
  56.6 60.2 %copy-start.40 = (f32[4,256,384]{2,1,0:T(8,128)}, f32[4,256,384]{2,1,0:T(8,128)S(1)}, u32[]{:S(2)}) copy-start(f32[4,256,384]{2,1,0:T(8,128)S(1)} %add_add_fusion.6) | copy-start | bytes 4718596
  142.2 7.7 copy-start.181
  142.2 7.7 copy-start.182
  231.6 7.4 copy-start.17
  248.3 70.8 %copy-start.84 = (f32[4,6,257]{2,1,0:T(8,128)}, f32[4,6,257]{2,1,0:T(8,128)S(1)}, u32[]{:S(2)}) copy-start(f32[4,6,257]{2,1,0:T(8,128)S(1)} %get-tuple-element.179) | copy-start | bytes 74020
  274.3 17.4 %copy-start.121 = (f32[4,257]{1,0:T(4,128)}, f32[4,257]{1,0:T(4,128)S(1)}, u32[]{:S(2)}) copy-start(f32[4,257]{1,0:T(4,128)S(1)} %copy.292) | copy-start | bytes 12340
  299.5 7.0 copy-start.178
  301.4 7.3 copy-start.186
  301.4 7.3 copy-start.187
  301.4 7.4 copy-start.211
  303.9 14.5 %copy-start.140 = (f32[4,6]{1,0:T(4,128)}, f32[4,6]{1,0:T(4,128)S(1)}, u32[]{:S(2)}) copy-start(f32[4,6]{1,0:T(4,128)S(1)} %get-tuple-element.181) | copy-start | bytes 292
  306.4 7.2 copy-start.137
  306.4 7.2 copy-start.156
  306.5 8.6 copy-start.145
  311.1 7.8 copy-start.142
  311.1 7.8 copy-start.184
  317.6 287.0 %copy-start.113 = (f32[4,1,384]{2,0,1:T(4,128)}, f32[4,1,384]{2,0,1:T(4,128)S(1)}, u32[]{:S(2)}) copy-start(f32[4,1,384]{2,0,1:T(4,128)S(1)} %get-tuple-element.151) | copy-start | bytes 18436
  446.6 158.1 %copy-start.143 = (f32[384]{0:T(512)S(1)}, f32[384]{0:T(512)}, u32[]{:S(2)}) copy-start(f32[384]{0:T(512)} %get-tuple-element.80) | copy-start | bytes 4612
  446.6 158.1 %copy-start.175 = (f32[4]{0:T(128)S(1)}, f32[4]{0:T(128)}, u32[]{:S(2)}) copy-start(f32[4]{0:T(128)} %copy-done.174) | copy-start | bytes 52
  446.6 158.1 %copy-start.185 = (f32[384]{0:T(512)S(1)}, f32[384]{0:T(512)}, u32[]{:S(2)}) copy-start(f32[384]{0:T(512)} %get-tuple-element.96) | copy-start | bytes 4612
  606.5 7.1 copy-start.117
  661.6 6.5 copy-start.4
  661.6 6.5 copy-start.163
  661.6 6.5 copy-start.218
  766.3 6.5 copy-start.144
  766.3 6.5 copy-start.176
  766.3 6.5 copy-start.203
  766.3 9.1 copy-start.222
  766.3 9.4 copy-start.52
  766.3 9.4 copy-start.111
  766.3 9.4 copy-start.192
  805.4 7.7 copy-start.77
  847.0 9.5 copy-start.85
  856.5 10.6 copy-start.18
  887.6 160.4 %reduce-scatter.8.cloned.1.call-start = ((), (), s32[]{:S(2)}) async-start(), calls=%async_computation.7 | async-start | bytes 3981312 | tf_op jit(solution)/shard_map/reduce_scatter | solution.py:294
  895.3 215.6 %reduce-scatter.4.cloned.1.call-start = ((), (), s32[]{:S(2)}) async-start(), calls=%async_computation.5 | async-start | bytes 552960 | tf_op jit(solution)/shard_map/reduce_scatter | solution.py:290
  919.1 33.8 %copy-start.96 = (f32[65536]{0:T(1024)S(1)}, f32[65536]{0:T(1024)}, u32[]{:S(2)}) copy-start(f32[65536]{0:T(1024)} %param.31) | copy-start | bytes 786436
  919.1 251.3 %all-gather.28.cloned.1.call-start = ((), (), s32[]{:S(2)}) async-start(), calls=%async_computation.14 | async-start | bytes 2331648 | tf_op jit(solution)/shard_map/all_gather | solution.py:274
  920.4 287.0 %all-reduce.38.cloned.1.call-start = ((), (), s32[]{:S(2)}) async-start(), calls=%async_computation.8 | async-start | bytes 1769472 | tf_op jit(solution)/shard_map/psum | solution.py:297
  921.9 128.4 %copy-start.58 = (f32[274,384]{1,0:T(8,128)}, f32[274,384]{1,0:T(8,128)S(1)}, u32[]{:S(2)}) copy-start(f32[274,384]{1,0:T(8,128)S(1)} %scatter-add.9) | copy-start | bytes 1262596
  1050.2 289.1 %all-reduce.40.cloned.1.call-start = ((), (), s32[]{:S(2)}) async-start(), calls=%async_computation.9 | async-start | bytes 860160 | tf_op jit(solution)/shard_map/psum | solution.py:299
  1176.2 189.2 %copy-start.88 = (f32[48,588]{1,0:T(8,128)S(1)}, f32[48,588]{1,0:T(8,128)}, u32[]{:S(2)}) copy-start(f32[48,588]{1,0:T(8,128)} %param.32) | copy-start | bytes 338692
  1176.2 189.2 %copy-start.90 = (f32[48,588]{1,0:T(8,128)S(1)}, f32[48,588]{1,0:T(8,128)}, u32[]{:S(2)}) copy-start(f32[48,588]{1,0:T(8,128)} %param.35) | copy-start | bytes 338692
  1176.2 189.2 %copy-start.108 = (f32[48,588]{1,0:T(8,128)S(1)}, f32[48,588]{1,0:T(8,128)}, u32[]{:S(2)}) copy-start(f32[48,588]{1,0:T(8,128)} %param.33) | copy-start | bytes 338692
  1176.2 189.2 %copy-start.109 = (f32[48,588]{1,0:T(8,128)S(1)}, f32[48,588]{1,0:T(8,128)}, u32[]{:S(2)}) copy-start(f32[48,588]{1,0:T(8,128)} %param.34) | copy-start | bytes 338692
  1366.3 27.8 %copy-start.23 = (f32[336,2048]{1,0:T(8,128)S(1)}, f32[336,2048]{1,0:T(8,128)}, u32[]{:S(2)}) copy-start(f32[336,2048]{1,0:T(8,128)} %param.43) | copy-start | bytes 8257540
  1394.1 9.0 copy-start.60
  1394.1 9.0 copy-start.62
  1394.1 9.0 copy-start.63
  1394.1 9.0 copy-start.91
  1394.1 9.0 copy-start.92
  1394.1 10.4 copy-start.49
  1394.1 10.4 copy-start.56
  1394.2 10.4 copy-start.57
  (175 other events, 532.5 us)
Sparse Core Ops, SparseCore 0:
  10.8 77.3 all-gather.19
  90.9 64.5 all-gather.21
  158.2 63.6 all-gather.23
  224.5 63.6 all-gather.25
  290.8 155.7 all-gather.15
  449.2 155.4 all-gather.17
  887.7 77.4 reduce-scatter.5
  969.4 78.5 reduce-scatter.7
  1051.9 58.9 reduce-scatter.3
  1114.3 56.0 all-gather.27
  1173.4 34.0 all-reduce.37
  1213.2 126.0 all-reduce.39

commit v2 on v1

--- a/solution.py
+++ b/solution.py
@@ -1,8 +1,10 @@
-from functools import partial
+import functools
 
 import jax
 import jax.numpy as jnp
 from jax import lax
+from jax.experimental import pallas as pl
+from jax.experimental.pallas import tpu as pltpu
 from jax.sharding import PartitionSpec as P
 
 HEADS = 6
@@ -18,115 +20,907 @@
 DECAYS = (0.04, 0.04, 0.04, 0.04, 0.0)
 F32 = jnp.float32
 BF16 = jnp.bfloat16
+MESH = pl.DeviceIdType.MESH
+
+
+def third_ranges(width, start):
+    tiles = width // 128
+    sizes = [(tiles + 2 - part) // 3 * 128 for part in range(3)]
+    spans, at = [], start
+    for size in sizes:
+        spans.append((at, size))
+        at += size
+    return spans
+
+
+def gather_kernel(items, lines, sources, targets, send, recv, copied):
+    fsdp, dp = lax.axis_index("fsdp"), lax.axis_index("dp")
+    z, x = fsdp // 2, fsdp % 2
+    y, core = dp // 2, dp % 2
+    across = z * 2 + 1 - x
+    mate = y * 2 + 1 - core
+    opposite = (1 - y) * 2 + core
+
+    barrier = pltpu.get_barrier_semaphore()
+
+    def greet(f, d):
+        pl.semaphore_signal(barrier, 1, device_id=(f, d), device_id_type=pl.DeviceIdType.MESH)
+
+    def when(condition, body):
+        pl.when(condition)(body)
+
+    greet(across, dp)
+    greet(fsdp, mate)
+    when(z + 1 < lines, lambda: greet(fsdp + 2, dp))
+    when(z > 0, lambda: greet(fsdp - 2, dp))
+    when(core == 0, lambda: greet(fsdp, opposite))
+    ends = (z + 1 < lines).astype(jnp.int32) + (z > 0).astype(jnp.int32)
+    pl.semaphore_wait(barrier, 3 - core + ends)
+
+    hops = lines - 1
+    UP, DOWN, ACROSS, OPPOSITE, MATE = 0, hops, 2 * hops, 4 * hops + 1, 4 * hops + 2
+
+    def roles(body):
+        when((core == 0) & (y == 0), lambda: body(0))
+        when(core == 1, lambda: body(1))
+        when((core == 0) & (y == 1), lambda: body(2))
+
+    def region(index, part, f):
+        number, rows, spans = items[index]
+        at, size = spans[part]
+        return targets[number].at[pl.ds(pl.multiple_of(f * rows, rows), rows), pl.ds(at, size)]
+
+    def whole(index, part):
+        number, rows, spans = items[index]
+        at, size = spans[part]
+        return targets[number].at[:, pl.ds(at, size)]
+
+    def own(index, part):
+        number, rows, spans = items[index]
+        at, size = spans[part]
+        return sources[number].at[:, pl.ds(at, size)]
+
+    def move(index, slot, source, target, f, d):
+        return pltpu.make_async_remote_copy(
+            src_ref=source,
+            dst_ref=target,
+            send_sem=send.at[index, slot],
+            recv_sem=recv.at[index, slot],
+            device_id=(f, d),
+            device_id_type=pl.DeviceIdType.MESH,
+        )
+
+    def piece(index, part, slot, f_source, f_target, mine=False):
+        target = region(index, part, f_source)
+        return move(index, slot, own(index, part) if mine else target, target, f_target, dp)
+
+    def keep(index, part):
+        return pltpu.make_async_copy(own(index, part), region(index, part, fsdp), copied.at[index])
+
+    def z_steps(index, part, hop, act):
+        mine = hop == 0
+        if hop < hops:
+            when(
+                (z - hop >= 0) & (z + 1 < lines),
+                lambda: act(piece(index, part, UP + hop, fsdp - 2 * hop, fsdp + 2, mine)),
+            )
+            when(
+                (z + hop < lines) & (z > 0),
+                lambda: act(piece(index, part, DOWN + hop, fsdp + 2 * hop, fsdp - 2, mine)),
+            )
+
+    def x_steps(index, part, hop, act):
+        if hop == 0:
+            act(piece(index, part, ACROSS, fsdp, across, True))
+        else:
+            when(
+                z - hop >= 0,
+                lambda: act(piece(index, part, ACROSS + hop, fsdp - 2 * hop, across)),
+            )
+            when(
+                z + hop < lines,
+                lambda: act(piece(index, part, ACROSS + hops + hop, fsdp + 2 * hop, across)),
+            )
+
+    def z_arrive(index, part, hop):
+        when(
+            z - hop >= 0,
+            lambda: piece(index, part, UP + hop - 1, fsdp - 2 * hop, fsdp).wait_recv(),
+        )
+        when(
+            z + hop < lines,
+            lambda: piece(index, part, DOWN + hop - 1, fsdp + 2 * hop, fsdp).wait_recv(),
+        )
+
+    def x_arrive(index, part):
+        piece(index, part, ACROSS, across, across).wait_recv()
+        for hop in range(1, lines):
+            when(
+                z - hop >= 0,
+                lambda hop=hop: piece(
+                    index, part, ACROSS + hop, across - 2 * hop, across
+                ).wait_recv(),
+            )
+            when(
+                z + hop < lines,
+                lambda hop=hop: piece(
+                    index, part, ACROSS + hops + hop, across + 2 * hop, across
+                ).wait_recv(),
+            )
+
+    def to_opposite(index, part):
+        return move(index, OPPOSITE, whole(index, part), whole(index, part), fsdp, opposite)
+
+    def to_mate(index, part, second=0):
+        return move(index, MATE + second, whole(index, part), whole(index, part), fsdp, mate)
+
+    def stage(index, part, step):
+        if step == 0:
+            keep(index, part).start()
+            z_steps(index, part, 0, lambda copy: copy.start())
+            x_steps(index, part, 0, lambda copy: copy.start())
+        elif step < lines:
+            z_arrive(index, part, step)
+            z_steps(index, part, step, lambda copy: copy.start())
+            x_steps(index, part, step, lambda copy: copy.start())
+        elif step == lines:
+            keep(index, part).wait()
+            x_arrive(index, part)
+            if part != 1:
+                to_opposite(index, part).start()
+            to_mate(index, part).start()
+        elif step == lines + 1:
+            if part != 1:
+                to_opposite(index, 2 - part).wait_recv()
+                to_mate(index, 2 - part, 1).start()
+        else:
+            if part != 1:
+                to_mate(index, 1).wait_recv()
+            else:
+                when(y == 0, lambda: to_mate(index, 0).wait_recv())
+                when(y == 0, lambda: to_mate(index, 2, 1).wait_recv())
+                when(y == 1, lambda: to_mate(index, 2).wait_recv())
+                when(y == 1, lambda: to_mate(index, 0, 1).wait_recv())
+
+    def run(part):
+        steps = lines + 3
+        for tick in range(len(items) + steps - 1):
+            for step in range(steps):
+                if 0 <= tick - step < len(items):
+                    stage(tick - step, part, step)
+        for index in range(len(items)):
+            for hop in range(lines):
+                z_steps(index, part, hop, lambda copy: copy.wait_send())
+                x_steps(index, part, hop, lambda copy: copy.wait_send())
+            if part != 1:
+                to_opposite(index, part).wait_send()
+                to_mate(index, 2 - part, 1).wait_send()
+            to_mate(index, part).wait_send()
+
+    roles(run)
+
+
+def gather_rows(arrays, fsdp_count, cuts, collective_id):
+    lines = fsdp_count // 2
+    items = []
+    for number, array in enumerate(arrays):
+        rows, width = array.shape
+        step = width // cuts[number]
+        for cut in range(cuts[number]):
+            items.append((number, rows, third_ranges(step, cut * step)))
+    count = len(arrays)
+    slots = 4 * (lines - 1) + 4
+
+    def kernel(*refs):
+        gather_kernel(items, lines, refs[:count], refs[count : 2 * count], *refs[2 * count :])
+
+    return pl.pallas_call(
+        kernel,
+        out_shape=[
+            jax.ShapeDtypeStruct((fsdp_count * a.shape[0], a.shape[1]), a.dtype) for a in arrays
+        ],
+        in_specs=[pl.BlockSpec(memory_space=pl.ANY)] * count,
+        out_specs=[pl.BlockSpec(memory_space=pl.ANY)] * count,
+        scratch_shapes=[
+            pltpu.SemaphoreType.DMA((len(items), slots)),
+            pltpu.SemaphoreType.DMA((len(items), slots)),
+            pltpu.SemaphoreType.DMA((len(items),)),
+        ],
+        compiler_params=pltpu.CompilerParams(collective_id=collective_id, has_side_effects=True),
+        name="gather_rows",
+    )(*arrays)
+
+
+def reduce_kernel(
+    cuts, lines, grads, out, mate_a, mate_b, facing, side, sums, up_out, up_in, down_out, down_in,
+    ending, ended, result, send, recv
+):
+    fsdp, dp = lax.axis_index("fsdp"), lax.axis_index("dp")
+    z, x = fsdp // 2, fsdp % 2
+    y, core = dp // 2, dp % 2
+    across = z * 2 + 1 - x
+    mate = y * 2 + 1 - core
+    opposite = (1 - y) * 2 + core
+    size = mate_a.shape[-1]
+    lone = core == 1
+    part = jnp.where(lone, 1, 2 * y)
+    mate_part = jnp.where(lone, 2 * y, 1)
+
+    barrier = pltpu.get_barrier_semaphore()
+
+    def greet(f, d):
+        pl.semaphore_signal(barrier, 1, device_id=(f, d), device_id_type=MESH)
+
+    greet(across, dp)
+    greet(fsdp, mate)
+    greet(fsdp, opposite)
+    pl.when(z + 1 < lines)(lambda: greet(fsdp + 2, dp))
+    pl.when(z > 0)(lambda: greet(fsdp - 2, dp))
+    ends = (z + 1 < lines).astype(jnp.int32) + (z > 0).astype(jnp.int32)
+    pl.semaphore_wait(barrier, 3 + ends)
+
+    MATE_A, MATE_B, FACING, ACROSS, UP, DOWN, ENDING, LAST_MATE, LAST_SECOND, LAST_FACING = range(10)
+
+    def move(cut, slot, source, target, f, d):
+        return pltpu.make_async_remote_copy(
+            src_ref=source,
+            dst_ref=target,
+            send_sem=send.at[cut, slot],
+            recv_sem=recv.at[cut, slot],
+            device_id=(f, d),
+            device_id_type=MESH,
+        )
+
+    def columns(cut, which):
+        return pl.ds(pl.multiple_of((3 * cut + which) * size, 128), size)
+
+    def mine(cut, which):
+        return grads[:, :, :, columns(cut, which)].astype(F32)
+
+    def to_mate_a(cut):
+        return move(cut, MATE_A, grads.at[:, :, :, columns(cut, mate_part)], mate_a.at[cut], fsdp, mate)
+
+    def to_mate_b(cut):
+        return move(
+            cut, MATE_B, grads.at[:, :, :, columns(cut, 2 - mate_part)], mate_b.at[cut], fsdp, mate
+        )
+
+    def to_facing(cut):
+        return move(cut, FACING, mate_b.at[cut], facing.at[cut], fsdp, opposite)
+
+    def to_across(cut):
+        return move(cut, ACROSS, mate_a.at[cut, :, 1 - x], side.at[cut], across, dp)
+
+    def going_up(cut, count):
+        blocks = pl.ds(0, count)
+        return move(cut, UP, up_out.at[cut, blocks], up_in.at[cut, blocks], fsdp + 2, dp)
+
+    def going_down(cut, count):
+        blocks = pl.ds(0, count)
+        return move(cut, DOWN, down_out.at[cut, blocks], down_in.at[cut, blocks], fsdp - 2, dp)
+
+    def to_ending(cut):
+        return move(cut, ENDING, ending.at[cut], ended.at[cut], fsdp, opposite)
+
+    def last(cut, slot, which, d):
+        place = result.at[:, columns(cut, which)]
+        return move(cut, slot, place, place, fsdp, d)
+
+    def step_0(cut):
+        to_mate_a(cut).start()
+        pl.when(lone)(lambda: to_mate_b(cut).start())
+
+    def step_1(cut):
+        @pl.when(jnp.logical_not(lone))
+        def _():
+            to_mate_b(cut).wait_recv()
+            mate_b[cut] = (mine(cut, 2 - part) + mate_b[cut].astype(F32)).astype(BF16)
+            to_facing(cut).start()
+
+    def step_2(cut):
+        to_mate_a(cut).wait_recv()
+
+        @pl.when(lone)
+        def _():
+            mate_a[cut] = (mine(cut, 1) + mate_a[cut].astype(F32)).astype(BF16)
+
+        @pl.when(jnp.logical_not(lone))
+        def _():
+            to_facing(cut).wait_recv()
+            both = mine(cut, part) + mate_a[cut].astype(F32) + facing[cut].astype(F32)
+            mate_a[cut] = both.astype(BF16)
+
+        to_across(cut).start()
+
+    def step_3(cut):
+        to_across(cut).wait_recv()
+        sums[cut] = mate_a[cut, :, x].astype(F32) + side[cut].astype(F32)
+
+    def lift(cut, hop):
+        at = hop - 1
+
+        @pl.when(z == at)
+        def _():
+            count = lines - hop
+            if at > 0:
+                going_up(cut, count + 1).wait_recv()
+            for ahead in range(1, count + 1):
+                value = sums[cut, at + ahead]
+                if at > 0:
+                    value = value + up_in[cut, ahead].astype(F32)
+                up_out[cut, ahead - 1] = value.astype(BF16)
+            going_up(cut, count).start()
+
+        low = lines - hop
+
+        @pl.when(z == low)
+        def _():
+            count = lines - hop
+            if low < lines - 1:
+                going_down(cut, count + 1).wait_recv()
+            for ahead in range(1, count + 1):
+                value = sums[cut, low - ahead]
+                if low < lines - 1:
+                    value = value + down_in[cut, ahead].astype(F32)
+                down_out[cut, ahead - 1] = value.astype(BF16)
+            going_down(cut, count).start()
+
+    def finish(cut):
+        for at in range(lines):
+
+            @pl.when(z == at)
+            def _(at=at):
+                value = sums[cut, at]
+                if at == lines - 1:
+                    going_up(cut, 1).wait_recv()
+                if at == 0:
+                    going_down(cut, 1).wait_recv()
+                if at > 0:
+                    value = value + up_in[cut, 0].astype(F32)
+                if at < lines - 1:
+                    value = value + down_in[cut, 0].astype(F32)
+                ending[cut] = value.astype(BF16)
+
+        pl.when(lone)(lambda: to_ending(cut).start())
+
+        @pl.when(jnp.logical_not(lone))
+        def _():
+            result[:, columns(cut, part)] = ending[cut]
+            last(cut, LAST_FACING, part, opposite).start()
+            last(cut, LAST_MATE, part, mate).start()
+
+    def share(cut):
+        @pl.when(lone)
+        def _():
+            to_ending(cut).wait_recv()
+            both = ending[cut].astype(F32) + ended[cut].astype(F32)
+            result[:, columns(cut, part)] = both.astype(BF16)
+            last(cut, LAST_MATE, part, mate).start()
+
+        @pl.when(jnp.logical_not(lone))
+        def _():
+            last(cut, LAST_FACING, 2 - part, opposite).wait_recv()
+            last(cut, LAST_SECOND, 2 - part, mate).start()
+
+    def close(cut):
+        last(cut, LAST_MATE, mate_part, mate).wait_recv()
+        pl.when(lone)(lambda: last(cut, LAST_SECOND, 2 - mate_part, mate).wait_recv())
+
+    steps = [step_0, step_1, step_2, step_3]
+    steps += [functools.partial(lambda hop, cut: lift(cut, hop), hop) for hop in range(1, lines)]
+    steps += [finish, share, close]
+    for tick in range(cuts + len(steps) - 1):
+        for number, step in enumerate(steps):
+            if 0 <= tick - number < cuts:
+                step(tick - number)
+
+    out[...] = result[...].astype(F32)
+    for cut in range(cuts):
+        to_mate_a(cut).wait_send()
+        to_across(cut).wait_send()
+        for hop in range(1, lines):
+            pl.when(z == hop - 1)(lambda hop=hop: going_up(cut, lines - hop).wait_send())
+            pl.when(z == lines - hop)(lambda hop=hop: going_down(cut, lines - hop).wait_send())
+        last(cut, LAST_MATE, part, mate).wait_send()
+
+        @pl.when(lone)
+        def _():
+            to_mate_b(cut).wait_send()
+            to_ending(cut).wait_send()
+
+        @pl.when(jnp.logical_not(lone))
+        def _():
+            to_facing(cut).wait_send()
+            last(cut, LAST_FACING, part, opposite).wait_send()
+            last(cut, LAST_SECOND, 2 - part, mate).wait_send()
+
+
+def reduce_rows(grads, fsdp_count, cuts, collective_id):
+    total, width = grads.shape
+    lines, rows = fsdp_count // 2, total // fsdp_count
+    size = width // (3 * cuts)
+    blocks = (cuts, lines, 2, rows, size)
+    return pl.pallas_call(
+        functools.partial(reduce_kernel, cuts, lines),
+        out_shape=jax.ShapeDtypeStruct((rows, width), F32),
+        in_specs=[pl.BlockSpec(memory_space=pltpu.VMEM)],
+        out_specs=pl.BlockSpec(memory_space=pltpu.VMEM),
+        scratch_shapes=[
+            pltpu.VMEM(blocks, BF16),
+            pltpu.VMEM(blocks, BF16),
+            pltpu.VMEM(blocks, BF16),
+            pltpu.VMEM((cuts, lines, rows, size), BF16),
+            pltpu.VMEM((cuts, lines, rows, size), F32),
+        ]
+        + [pltpu.VMEM((cuts, lines - 1, rows, size), BF16)] * 4
+        + [pltpu.VMEM((cuts, rows, size), BF16)] * 2
+        + [
+            pltpu.VMEM((rows, width), BF16),
+            pltpu.SemaphoreType.DMA((cuts, 10)),
+            pltpu.SemaphoreType.DMA((cuts, 10)),
+        ],
+        compiler_params=pltpu.CompilerParams(
+            collective_id=collective_id, has_side_effects=True, vmem_limit_bytes=58 << 20
+        ),
+        name="reduce_rows",
+    )(grads.reshape(lines, 2, rows, width))
+
+
+GELU_A = 0.7978845608028654
+GELU_B = 0.044715
+TAIL = 16
+
+
+def mm(left, right):
+    return lax.dot_general(left, right, (((1,), (0,)), ((), ())), preferred_element_type=F32)
+
+
+def mm_nt(left, right):
+    return lax.dot_general(left, right, (((1,), (1,)), ((), ())), preferred_element_type=F32)
+
+
+def mm_tn(left, right):
+    return lax.dot_general(left, right, (((0,), (0,)), ((), ())), preferred_element_type=F32)
+
+
+def norm_parts(x):
+    centred = x - jnp.mean(x, -1, keepdims=True)
+    lift = lax.rsqrt(jnp.mean(centred * centred, -1, keepdims=True) + 1e-06)
+    return centred * lift, lift
+
+
+def norm_back(grad, gain, unit_x, lift):
+    inner = grad * gain
+    return lift * (
+        inner
+        - jnp.mean(inner, -1, keepdims=True)
+        - unit_x * jnp.mean(inner * unit_x, -1, keepdims=True)
+    )
+
+
+def gelu(x):
+    return 0.5 * x * (1.0 + jnp.tanh(GELU_A * (x + GELU_B * (x * x * x))))
+
+
+def gelu_both(x):
+    square = x * x
+    slope = jnp.tanh(GELU_A * x * (1.0 + GELU_B * square))
+    half = 0.5 * (1.0 + slope)
+    turn = half + 0.5 * x * (1.0 - slope * slope) * GELU_A * (1.0 + 3.0 * GELU_B * square)
+    return x * half, turn
+
+
+def half_masks(width):
+    lane = lax.broadcasted_iota(jnp.int32, (1, 128), 1)
+    first = (lane < width).astype(F32)
+    return first, 1.0 - first
+
+
+def column_sum(x):
+    return jnp.sum(x, 0, keepdims=True)
+
+
+def attend(q, keys, values, valid, scale, lse_store):
+    rows, total = q.shape[0], keys.shape[0]
+    masks = half_masks(64)
+    column = lax.broadcasted_iota(jnp.int32, (rows, total), 1)
+    lane = lax.broadcasted_iota(jnp.int32, (rows, 128), 1)
+    mixed, lse = [], jnp.zeros((rows, 128), F32)
+    for pair in range(HEADS // 2):
+        span = slice(128 * pair, 128 * pair + 128)
+        halves = []
+        for side in range(2):
+            asked = q[:, span] * (masks[side] * scale).astype(BF16)
+            scores = mm_nt(asked, keys[:, span])
+            scores = jnp.where(column < valid, scores, -1e30)
+            top = jnp.max(scores, -1, keepdims=True)
+            expo = jnp.exp(scores - top)
+            total_e = jnp.sum(expo, -1, keepdims=True)
+            halves.append(mm(expo.astype(BF16), values[:, span]) / total_e)
+            if lse_store:
+                lse = jnp.where(lane == 2 * pair + side, top + jnp.log(total_e), lse)
+        mixed.append(jnp.where(lane < 64, halves[0], halves[1]))
+    return jnp.concatenate(mixed, -1).astype(BF16), lse
+
+
+def forward_kernel(
+    images, hidden, keep, patches, covered, weight_p, weight_0, weight_1, places, rows_table, *rest
+):
+    if keep:
+        (cls_out, x0_out, x1_out, x2_out, qkv_out, o0_out, lse0_out, kv_out, q1_out, lse1_out,
+         x1c_out, o1_out, cls_x, cls_o) = rest
+    else:
+        cls_out, cls_x, cls_o = rest
+    image = pl.program_id(0)
+    model = weight_0.shape[0]
+    count = patches.shape[1]
+    valid = count + 1
+    scale = (model // HEADS) ** -0.5
+
+    def vec(row):
+        return rows_table[row : row + 1, :]
+
+    @pl.when(image == 0)
+    def _():
+        cls_x[...] = jnp.zeros_like(cls_x)
+        cls_o[...] = jnp.zeros_like(cls_o)
+
+    tokens = mm_nt(patches[0], weight_p[:, : patches.shape[2]]) + vec(1)
+    if keep:
+        hide = covered[0]
+        tokens = tokens * (1.0 - hide) + vec(0) * hide
+    x = jnp.concatenate([tokens + places[:count, :], places[count:, :]], 0)
+
+    def row(layer, index):
+        return vec(2 + 6 * layer + index)
+
+    unit_x, _ = norm_parts(x)
+    low = (unit_x * row(0, 0) + row(0, 1)).astype(BF16)
+    qkv = mm(low, weight_0[:, : 3 * model]).astype(BF16)
+    mixture, lse = attend(
+        qkv[:, :model], qkv[:, model : 2 * model], qkv[:, 2 * model :], valid, scale, keep
+    )
+    x1 = x + row(0, 2) * mm(mixture, weight_0[:, 3 * model : 4 * model])
+    unit_x, _ = norm_parts(x1)
+    low = (unit_x * row(0, 3) + row(0, 4)).astype(BF16)
+    wide = gelu(mm(low, weight_0[:, 4 * model : 4 * model + hidden])).astype(BF16)
+    x2 = x1 + row(0, 5) * mm_nt(wide, weight_0[:, 4 * model + hidden :])
+
+    unit_x, _ = norm_parts(x2)
+    low = (unit_x * row(1, 0) + row(1, 1)).astype(BF16)
+    kv = mm(low, weight_1[:, model : 3 * model]).astype(BF16)
+    q1 = mm(low[count:, :], weight_1[:, :model]).astype(BF16)
+    mixture1, lse1 = attend(q1, kv[:, :model], kv[:, model:], valid, scale, keep)
+    cls_x[pl.ds(image, 1), :] = x2[count : count + 1, :]
+    cls_o[pl.ds(image, 1), :] = mixture1[:1, :].astype(F32)
+    if keep:
+        x0_out[0] = x
+        x1_out[0] = x1
+        x2_out[0] = x2
+        qkv_out[0] = qkv
+        o0_out[0] = mixture
+        lse0_out[0] = lse
+        kv_out[0] = kv
+        q1_out[0] = q1
+        lse1_out[0] = lse1
+
+    @pl.when(image == images - 1)
+    def _():
+        mixed = cls_o[...].astype(BF16)
+        x1c = cls_x[...] + row(1, 2) * mm(mixed, weight_1[:, 3 * model : 4 * model])
+        unit_c, _ = norm_parts(x1c)
+        low_c = (unit_c * row(1, 3) + row(1, 4)).astype(BF16)
+        wide_c = gelu(mm(low_c, weight_1[:, 4 * model : 4 * model + hidden])).astype(BF16)
+        cls_out[...] = x1c + row(1, 5) * mm_nt(wide_c, weight_1[:, 4 * model + hidden :])
+        if keep:
+            x1c_out[...] = x1c
+            o1_out[...] = mixed
+
+
+def fixed(shape):
+    zeros = (0,) * len(shape)
+    return pl.BlockSpec(shape, lambda i: zeros, pipeline_mode=pl.Buffered(1))
+
+
+def each(shape):
+    rest = (0,) * len(shape)
+    return pl.BlockSpec((1,) + shape, lambda i: (i,) + rest)
+
+
+def whole_out(shape):
+    zeros = (0,) * len(shape)
+    return pl.BlockSpec(shape, lambda i: zeros)
+
+
+def split_table(vecs, count):
+    places = jnp.concatenate(
+        [
+            vecs[1 : count + 1],
+            vecs[:1] + vecs[count + 1 : count + 2],
+            jnp.zeros((TAIL - 1, vecs.shape[1]), F32),
+        ]
+    )
+    rows = vecs[count + 2 :]
+    rows = jnp.concatenate([rows, jnp.zeros(((-rows.shape[0]) % 8, rows.shape[1]), F32)])
+    return places, rows
+
+
+def forward(patches, covered, weight_p, weight_0, weight_1, vecs, keep):
+    images, count, pixels = patches.shape
+    model, columns = weight_0.shape
+    hidden = (columns - 4 * model) // 2
+    total = count + TAIL
+    places, rows = split_table(vecs, count)
+    shape = jax.ShapeDtypeStruct
+    outs = [shape((TAIL, model), F32)]
+    out_specs = [whole_out((TAIL, model))]
+    if keep:
+        per_image = [
+            ((total, model), F32),
+            ((total, model), F32),
+            ((total, model), F32),
+            ((total, 3 * model), BF16),
+            ((total, model), BF16),
+            ((total, 128), F32),
+            ((total, 2 * model), BF16),
+            ((TAIL, model), BF16),
+            ((TAIL, 128), F32),
+        ]
+        outs += [shape((images,) + dims, kind) for dims, kind in per_image]
+        out_specs += [each(dims) for dims, kind in per_image]
+        outs += [shape((TAIL, model), F32), shape((TAIL, model), BF16)]
+        out_specs += [whole_out((TAIL, model))] * 2
+    return pl.pallas_call(
+        functools.partial(forward_kernel, images, hidden, keep),
+        grid=(images,),
+        out_shape=outs,
+        in_specs=[
+            each((count, pixels)),
+            each((count, 1)),
+            fixed(weight_p.shape),
+            fixed(weight_0.shape),
+            fixed(weight_1.shape),
+            fixed(places.shape),
+            fixed(rows.shape),
+        ],
+        out_specs=out_specs,
+        scratch_shapes=[pltpu.VMEM((TAIL, model), F32)] * 2,
+        compiler_params=pltpu.CompilerParams(vmem_limit_bytes=56 << 20),
+        name="backbone_forward",
+    )(patches, covered[..., None], weight_p, weight_0, weight_1, places, rows)
+
+
+def attend_back(grad_o, q, keys, values, lse, valid, scale):
+    rows, total = q.shape[0], keys.shape[0]
+    masks = half_masks(64)
+    column = lax.broadcasted_iota(jnp.int32, (rows, total), 1)
+    lane_row = lax.broadcasted_iota(jnp.int32, (rows, 128), 1)
+    grad_q, grad_k, grad_v = [], [], []
+    for pair in range(HEADS // 2):
+        span = slice(128 * pair, 128 * pair + 128)
+        out_q, out_k, out_v = [], None, None
+        for side in range(2):
+            mask = masks[side].astype(BF16)
+            asked = q[:, span] * (masks[side] * scale).astype(BF16)
+            given = grad_o[:, span] * mask
+            head = 2 * pair + side
+            scores = mm_nt(asked, keys[:, span])
+            share = jnp.where(column < valid, jnp.exp(scores - lse[:, head : head + 1]), 0.0)
+            grad_p = mm_nt(given, values[:, span])
+            inner = jnp.sum(share * grad_p, -1, keepdims=True)
+            grad_s = (share * (grad_p - inner)).astype(BF16)
+            out_q.append(mm(grad_s, keys[:, span]))
+            more_k = mm_tn(grad_s, asked)
+            more_v = mm_tn(share.astype(BF16), given)
+            out_k = more_k if out_k is None else out_k + more_k
+            out_v = more_v if out_v is None else out_v + more_v
+        grad_q.append(jnp.where(lane_row < 64, out_q[0], out_q[1]) * scale)
+        grad_k.append(out_k)
+        grad_v.append(out_v)
+    return [jnp.concatenate(part, -1).astype(BF16) for part in (grad_q, grad_k, grad_v)]
+
+
+def backward_kernel(
+    images, hidden, count_, patches, covered, weight_p, weight_0, weight_1, rows_table, ends, grad_cls,
+    x0_in, x1_in, x2_in, qkv_in, o0_in, lse0_in, kv_in, q1_in, lse1_in, x1c_in, o1_in,
+    packed, acc_p, acc_0, acc_kv, acc_q, grad_c, grad_oc, places, rows
+):
+    image = pl.program_id(0)
+    model = weight_0.shape[0]
+    count, pixels = patches.shape[1], patches.shape[2]
+    valid = count + 1
+    scale = (model // HEADS) ** -0.5
+    base_0 = packed_width_p(pixels)
+    columns = weight_0.shape[1]
+    base_1 = base_0 + columns
+    base_v = base_1 + columns
+    cut_o, cut_u, cut_d = 3 * model, 4 * model, 4 * model + hidden
+
+    def row(layer, index):
+        at = 2 + 6 * layer + index
+        return rows_table[at : at + 1, :]
+
+    def add_row(layer, index, value):
+        at = 2 + 6 * layer + index
+        rows[at : at + 1, :] += value
+
+    @pl.when(image == 0)
+    def _():
+        for ref in (acc_p, acc_0, acc_kv, acc_q, places, rows):
+            ref[...] = jnp.zeros_like(ref)
+        grad_x = grad_cls[...]
+        x1c = x1c_in[...]
+        unit_x, lift = norm_parts(x1c)
+        low = (unit_x * row(1, 3) + row(1, 4)).astype(BF16)
+        wide, slope = gelu_both(mm(low, weight_1[:, cut_u:cut_d]))
+        wide = wide.astype(BF16)
+        down = mm_nt(wide, weight_1[:, cut_d:])
+        add_row(1, 5, column_sum(grad_x * down))
+        grad_d = (grad_x * row(1, 5)).astype(BF16)
+        grad_u = (mm(grad_d, weight_1[:, cut_d:]) * slope).astype(BF16)
+        packed[:, base_1 + cut_d : base_v] = mm_tn(grad_d, wide).astype(BF16)
+        packed[:, base_1 + cut_u : base_1 + cut_d] = mm_tn(low, grad_u).astype(BF16)
+        grad_n = mm_nt(grad_u, weight_1[:, cut_u:cut_d])
+        add_row(1, 3, column_sum(grad_n * unit_x))
+        add_row(1, 4, column_sum(grad_n))
+        grad_x = grad_x + norm_back(grad_n, row(1, 3), unit_x, lift)
+        mixed = o1_in[...]
+        add_row(1, 2, column_sum(grad_x * mm(mixed, weight_1[:, cut_o:cut_u])))
+        grad_a = (grad_x * row(1, 2)).astype(BF16)
+        packed[:, base_1 + cut_o : base_1 + cut_u] = mm_tn(mixed, grad_a).astype(BF16)
+        grad_c[...] = grad_x
+        grad_oc[...] = mm_nt(grad_a, weight_1[:, cut_o:cut_u])
+
+    first_row = lax.broadcasted_iota(jnp.int32, (TAIL, 1), 0) == 0
+
+    grad_o1 = jnp.where(first_row, grad_oc[pl.ds(image, 1), :], 0.0).astype(BF16)
+    kv = kv_in[0]
+    grad_q, grad_k, grad_v = attend_back(
+        grad_o1, q1_in[0], kv[:, :model], kv[:, model:], lse1_in[0], valid, scale
+    )
+    unit_x, lift = norm_parts(x2_in[0])
+    low = (unit_x * row(1, 0) + row(1, 1)).astype(BF16)
+    grad_kv = jnp.concatenate([grad_k, grad_v], -1)
+    acc_kv[...] += mm_tn(low, grad_kv)
+    acc_q[...] += mm_tn(low[count:, :], grad_q)
+    grad_n = mm_nt(grad_kv, weight_1[:, model : 3 * model])
+    tail = grad_n[count:, :] + mm_nt(grad_q, weight_1[:, :model])
+    grad_n = jnp.concatenate([grad_n[:count, :], tail], 0)
+    add_row(1, 0, column_sum(grad_n * unit_x))
+    add_row(1, 1, column_sum(grad_n))
+    grad_x = norm_back(grad_n, row(1, 0), unit_x, lift)
+    tail = grad_x[count:, :] + jnp.where(first_row, grad_c[pl.ds(image, 1), :], 0.0)
+    grad_x = jnp.concatenate([grad_x[:count, :], tail], 0)
+
+    unit_x, lift = norm_parts(x1_in[0])
+    low = (unit_x * row(0, 3) + row(0, 4)).astype(BF16)
+    wide, slope = gelu_both(mm(low, weight_0[:, cut_u:cut_d]))
+    wide = wide.astype(BF16)
+    down = mm_nt(wide, weight_0[:, cut_d:])
+    add_row(0, 5, column_sum(grad_x * down))
+    grad_d = (grad_x * row(0, 5)).astype(BF16)
+    grad_u = (mm(grad_d, weight_0[:, cut_d:]) * slope).astype(BF16)
+    acc_0[:, cut_d:] += mm_tn(grad_d, wide)
+    acc_0[:, cut_u:cut_d] += mm_tn(low, grad_u)
+    grad_n = mm_nt(grad_u, weight_0[:, cut_u:cut_d])
+    add_row(0, 3, column_sum(grad_n * unit_x))
+    add_row(0, 4, column_sum(grad_n))
+    grad_x = grad_x + norm_back(grad_n, row(0, 3), unit_x, lift)
+    mixed = o0_in[0]
+    add_row(0, 2, column_sum(grad_x * mm(mixed, weight_0[:, cut_o:cut_u])))
+    grad_a = (grad_x * row(0, 2)).astype(BF16)
+    acc_0[:, cut_o:cut_u] += mm_tn(mixed, grad_a)
+    grad_o = mm_nt(grad_a, weight_0[:, cut_o:cut_u]).astype(BF16)
+    qkv = qkv_in[0]
+    grad_qkv = jnp.concatenate(
+        attend_back(
+            grad_o, qkv[:, :model], qkv[:, model : 2 * model], qkv[:, 2 * model :], lse0_in[0],
+            valid, scale,
+        ),
+        -1,
+    )
+    unit_x, lift = norm_parts(x0_in[0])
+    low = (unit_x * row(0, 0) + row(0, 1)).astype(BF16)
+    acc_0[:, :cut_o] += mm_tn(low, grad_qkv)
+    grad_n = mm_nt(grad_qkv, weight_0[:, :cut_o])
+    add_row(0, 0, column_sum(grad_n * unit_x))
+    add_row(0, 1, column_sum(grad_n))
+    grad_x = grad_x + norm_back(grad_n, row(0, 0), unit_x, lift)
+
+    places[...] += grad_x
+    hide = covered[0]
+    token = grad_x[:count, :]
+    rows[0:1, :] += column_sum(token * hide)
+    token = token * (1.0 - hide)
+    rows[1:2, :] += column_sum(token)
+    acc_p[...] += mm_tn(token.astype(BF16), patches[0])
+
+    @pl.when(image == images - 1)
+    def _():
+        packed[:, :base_0] = jnp.concatenate(
+            [acc_p[...], jnp.zeros((model, base_0 - pixels), F32)], -1
+        ).astype(BF16)
+        packed[:, base_0:base_1] = acc_0[...].astype(BF16)
+        packed[:, base_1 : base_1 + model] = acc_q[...].astype(BF16)
+        packed[:, base_1 + model : base_1 + cut_o] = acc_kv[...].astype(BF16)
+        used = rows_table.shape[0]
+        table = jnp.concatenate(
+            [
+                places[count : count + 1, :],
+                places[:count, :],
+                places[count : count + 1, :],
+                rows[...] + ends[...],
+            ],
+            0,
+        )
+        table = jnp.concatenate(
+            [table, jnp.zeros((model - table.shape[0], model), F32)], 0
+        )
+        packed[:, base_v : base_v + model] = table.astype(BF16)
+        spare = packed.shape[1] - base_v - model
+        if spare:
+            packed[:, base_v + model :] = jnp.zeros((model, spare), BF16)
+
+
+def packed_width_p(pixels):
+    return (pixels + 127) // 128 * 128
+
+
+def packed_width(pixels, columns, model):
+    width = packed_width_p(pixels) + 2 * columns + model
+    return (width + 1151) // 1152 * 1152
+
+
+def backward(patches, covered, weight_p, weight_0, weight_1, vecs, ends, grad_cls, saved):
+    images, count, pixels = patches.shape
+    model, columns = weight_0.shape
+    hidden = (columns - 4 * model) // 2
+    total = count + TAIL
+    _, rows = split_table(vecs, count)
+    ends = jnp.concatenate(
+        [jnp.zeros((14, model), F32), ends, jnp.zeros((rows.shape[0] - 16, model), F32)]
+    )
+    width = packed_width(pixels, columns, model)
+    return pl.pallas_call(
+        functools.partial(backward_kernel, images, hidden, count),
+        grid=(images,),
+        out_shape=jax.ShapeDtypeStruct((model, width), BF16),
+        in_specs=[
+            each((count, pixels)),
+            each((count, 1)),
+            fixed(weight_p.shape),
+            fixed(weight_0.shape),
+            fixed(weight_1.shape),
+            fixed(rows.shape),
+            fixed(ends.shape),
+            fixed(grad_cls.shape),
+        ]
+        + [each(array.shape[1:]) for array in saved[:9]]
+        + [fixed(array.shape) for array in saved[9:]],
+        out_specs=whole_out((model, width)),
+        scratch_shapes=[
+            pltpu.VMEM((model, pixels), F32),
+            pltpu.VMEM((model, columns), F32),
+            pltpu.VMEM((model, 2 * model), F32),
+            pltpu.VMEM((model, model), F32),
+            pltpu.VMEM((TAIL, model), F32),
+            pltpu.VMEM((TAIL, model), F32),
+            pltpu.VMEM((total, model), F32),
+            pltpu.VMEM(rows.shape, F32),
+        ],
+        compiler_params=pltpu.CompilerParams(vmem_limit_bytes=58 << 20),
+        name="backbone_backward",
+    )(patches, covered[..., None], weight_p, weight_0, weight_1, rows, ends, grad_cls, *saved)
 
 
 def dot(left, right, dims):
     return lax.dot_general(left, right, (dims, ((), ())), preferred_element_type=F32)
-
-
-@jax.custom_vjp
-def matmul(left, right):
-    return jnp.dot(left.astype(BF16), right.astype(BF16), preferred_element_type=F32)
-
-
-def matmul_keep(left, right):
-    left, right = left.astype(BF16), right.astype(BF16)
-    return jnp.dot(left, right, preferred_element_type=F32), (left, right)
-
-
-def matmul_pull(kept, grad):
-    left, right = kept
-    grad = grad.astype(BF16)
-    width = left.ndim - 1
-    lead = tuple(range(width))
-    return dot(grad, right, ((width,), (1,))), dot(left, grad, (lead, lead))
-
-
-matmul.defvjp(matmul_keep, matmul_pull)
-
-
-@partial(jax.custom_vjp, nondiff_argnums=(2,))
-def contract(left, right, spec):
-    return jnp.einsum(spec, left.astype(BF16), right.astype(BF16), preferred_element_type=F32)
-
-
-def contract_keep(left, right, spec):
-    left, right = left.astype(BF16), right.astype(BF16)
-    return jnp.einsum(spec, left, right, preferred_element_type=F32), (left, right)
-
-
-def contract_pull(spec, kept, grad):
-    left, right = kept
-    grad = grad.astype(BF16)
-    operands, result = spec.split("->")
-    first, second = operands.split(",")
-    return (
-        jnp.einsum(result + "," + second + "->" + first, grad, right, preferred_element_type=F32),
-        jnp.einsum(result + "," + first + "->" + second, grad, left, preferred_element_type=F32),
-    )
-
-
-contract.defvjp(contract_keep, contract_pull)
 
 
 def layer_norm(x, gain, shift):
     centred = x - jnp.mean(x, -1, keepdims=True)
     spread = jnp.mean(centred * centred, -1, keepdims=True)
     return centred * lax.rsqrt(spread + 1e-06) * gain + shift
-
-
-def embed(pixels, covered, patch_weight, vecs):
-    length = pixels.shape[1] + 1
-    tokens = matmul(pixels, patch_weight.T) + vecs[length + 2]
-    covered_col = covered[..., None]
-    tokens = tokens * (1.0 - covered_col) + vecs[length + 1] * covered_col
-    leading = jnp.broadcast_to(vecs[length], (pixels.shape[0], 1, vecs.shape[1]))
-    return jnp.concatenate([leading, tokens], 1) + vecs[:length]
-
-
-def mlp(x, layer_weight, rows):
-    model_width = x.shape[-1]
-    normed = layer_norm(x, rows[3], rows[4])
-    hidden = (layer_weight.shape[1] - 4 * model_width) // 2
-    up = layer_weight[:, 4 * model_width : 4 * model_width + hidden]
-    down = layer_weight[:, 4 * model_width + hidden :]
-    activated = jax.nn.gelu(matmul(normed, up))
-    return x + rows[5] * matmul(activated, down.T)
-
-
-def block(x, layer_weight, vecs, depth_index, last):
-    images, length, model_width = x.shape
-    rows = vecs[length + 3 + 6 * depth_index : length + 9 + 6 * depth_index]
-    head_width = model_width // HEADS
-    normed = layer_norm(x, rows[0], rows[1])
-    asking = normed[:, :1] if last else normed
-    queries = matmul(asking, layer_weight[:, :model_width])
-    pair = matmul(normed, layer_weight[:, model_width : 3 * model_width])
-    queries = queries.reshape(images, -1, HEADS, head_width)
-    pair = pair.reshape(images, length, 2, HEADS, head_width)
-    scores = contract(queries, pair[:, :, 0], "nqhe,nkhe->nhqk") * head_width ** (-0.5)
-    attention = jax.nn.softmax(scores, -1)
-    mixture = contract(attention, pair[:, :, 1], "nhqk,nkhe->nqhe")
-    mixture = mixture.reshape(images, -1, model_width)
-    kept = x[:, :1] if last else x
-    x = kept + rows[2] * matmul(mixture, layer_weight[:, 3 * model_width : 4 * model_width])
-    return mlp(x, layer_weight, rows)
-
-
-def backbone(patch_weight, layers, vecs, pixels, covered):
-    x = embed(pixels, covered, patch_weight, vecs)
-    count = len(layers)
-    for depth_index in range(count):
-        x = block(x, layers[depth_index], vecs, depth_index, depth_index == count - 1)
-    return x[:, 0]
-
-
-def gathered(owned, axis):
-    return lax.all_gather(owned.astype(BF16), "fsdp", axis=axis, tiled=True)
-
-
-def gathered_layers(owned):
-    return [gathered(owned[index], 0) for index in range(owned.shape[0])]
 
 
 def gelu_slope(x):
@@ -157,6 +951,23 @@
         moment / (1.0 - BETA_ONE**STEP) / (jnp.sqrt(second / (1.0 - BETA_TWO**STEP)) + 1e-08)
     )
     return (weight - step_rate * (direction + weight_decay * weight), moment, second)
+
+
+def small_mesh():
+    return lax.axis_size("dp") == 4 and lax.axis_size("fsdp") in (4, 8)
+
+
+def gather_all(arrays, cuts):
+    if small_mesh():
+        return gather_rows(arrays, lax.axis_size("fsdp"), cuts, 1)
+    return [lax.all_gather(array, "fsdp", axis=0, tiled=True) for array in arrays]
+
+
+def reduce_all(grads):
+    if small_mesh():
+        return reduce_rows(grads, lax.axis_size("fsdp"), 3, 2)
+    owned = lax.psum_scatter(grads, "fsdp", scatter_dimension=0, tiled=True)
+    return lax.psum(owned, "dp").astype(F32)
 
 
 def per_device(
@@ -192,23 +1003,27 @@
     counted = image_valid.astype(F32)
     counted_total = jnp.maximum(jnp.sum(counted), 1.0)
     covered = patch_mask.astype(F32)
-
-    teacher_patch_full = gathered(teacher_patch, 0)
-    teacher_layers_full = gathered_layers(teacher_layer)
-    patch_full = gathered(w_patch, 0)
-    layers_full = gathered_layers(w_layer)
-    teacher_head_full = gathered(teacher_head, 0)
-    head_full = gathered(w_head, 0)
-
-    teacher_cls = backbone(
-        teacher_patch_full, teacher_layers_full, teacher_vectors, patches, jnp.zeros_like(covered)
-    )
-    cls, pull_backbone = jax.vjp(
-        lambda pw, lw, vv: backbone(pw, lw, vv, patches, covered),
-        patch_full.astype(F32),
-        [weight.astype(F32) for weight in layers_full],
-        vectors,
-    )
+    pixels = w_patch.shape[1]
+    model_width, columns = w_layer.shape[1] * lax.axis_size("fsdp"), w_layer.shape[2]
+    pad = packed_width_p(pixels) - pixels
+
+    def low_blocks(patch, layers, weight):
+        patch = jnp.pad(patch, ((0, 0), (0, pad)))
+        return [array.astype(BF16) for array in (patch, layers[0], layers[1], weight)]
+
+    blocks = low_blocks(teacher_patch, teacher_layer, teacher_head)
+    blocks += low_blocks(w_patch, w_layer, w_head)
+    blocks = [blocks[index] for index in (0, 1, 2, 4, 5, 6, 3, 7)]
+    full = gather_all(blocks, (1, 1, 1, 1, 1, 1, 2, 2))
+    teacher_patch_full, teacher_0, teacher_1, patch_full, layer_0, layer_1 = full[:6]
+    teacher_head_full, head_full = full[6:]
+
+    teacher_cls = forward(
+        patches, jnp.zeros_like(covered), teacher_patch_full, teacher_0, teacher_1,
+        teacher_vectors, False,
+    )[0][:local]
+    cls_rows, *saved = forward(patches, covered, patch_full, layer_0, layer_1, vectors, True)
+    cls = cls_rows[:local]
 
     teacher_unit = unit(head_forward(teacher_cls, teacher_head_full, teacher_vectors)[-1])
     low_n, pre_a, low_a, pre_b, low_b, raw = head_forward(cls, head_full, vectors)
@@ -260,7 +1075,7 @@
     grad_rows = lax.dynamic_index_in_dim(grad_rows, lax.axis_index("dp"), 1, keepdims=False)
     grad_bottleneck = lax.psum_scatter(grad_rows, "fsdp", scatter_dimension=0, tiled=False)
 
-    model_width, hidden = cls.shape[1], head_full.shape[1]
+    hidden = head_full.shape[1]
     low_dz = pull_unit(grad_bottleneck)[0].astype(BF16)
     grad_b = jnp.dot(low_dz, head_full[model_width + hidden :], preferred_element_type=F32)
     low_db = (grad_b * gelu_slope(pre_b)).astype(BF16)
@@ -285,21 +1100,22 @@
     )
     grad_head = dot(left, right, ((0,), (0,)))
 
-    grad_patch, grad_layers, grad_vectors = pull_backbone(grad_cls)
-    grad_vectors = grad_vectors.at[-2].add(grad_gain).at[-1].add(grad_shift)
-    own_patch = lax.psum_scatter(
-        grad_patch.astype(BF16), "fsdp", scatter_dimension=0, tiled=True
-    )
-    own_layers = [
-        lax.psum_scatter(piece.astype(BF16), "fsdp", scatter_dimension=0, tiled=True)
-        for piece in grad_layers
-    ]
-    own_patch, own_layers = lax.psum((own_patch, jnp.stack(own_layers)), "dp")
-    own_patch, own_layers = own_patch.astype(F32), own_layers.astype(F32)
-    vector_grad = lax.psum(grad_vectors, everyone)
+    grad_rows = jnp.pad(grad_cls, ((0, TAIL - local), (0, 0)))
+    ends = jnp.stack([grad_gain, grad_shift])
+    packed_grads = backward(
+        patches, covered, patch_full, layer_0, layer_1, vectors, ends, grad_rows, saved
+    )
+    owned = reduce_all(packed_grads)
+    base = packed_width_p(pixels)
+    own_patch = owned[:, :pixels]
+    own_layers = jnp.stack(
+        [owned[:, base : base + columns], owned[:, base + columns : base + 2 * columns]]
+    )
+    own_rows_grad = owned[:, base + 2 * columns : base + 2 * columns + model_width]
+    vector_grad = lax.all_gather(own_rows_grad, "fsdp", axis=0, tiled=True)[: vectors.shape[0]]
     owned_grads = (own_patch, own_layers, grad_head, grad_proto)
     owned_squares = sum((jnp.sum(gradient * gradient) for gradient in owned_grads))
-    squares = lax.psum(owned_squares, "fsdp") + jnp.sum(vector_grad * vector_grad)
+    squares = lax.psum(owned_squares + jnp.sum(own_rows_grad * own_rows_grad), "fsdp")
     norm_value = jnp.sqrt(squares)
     factor = CLIP_NORM / jnp.maximum(norm_value, CLIP_NORM)
     updated_centre = CENTRE_KEEP * centre + (1.0 - CENTRE_KEEP) * teacher_total / counted_total

time: 1430 us -> 762 us (0.53)
  waiting for transfers between devices: 699 us -> 0.02 us
  Pallas kernels: 0 us -> 393 us
  matrix products: 189 us -> 49.3 us
  other arithmetic: 187 us -> 73.2 us
  local copies, waits for them, and re-layouts: 80 us -> 22.6 us
  blocking collectives: 238 us -> 195 us
    pallas_call x0 -> x5, Pallas kernels: none -> 393 us  [the longest x1 210 us: gather_rows(): pl.pallas_call(kernel, out_shape=[jax.ShapeDtypeStruct((fsdp_count * a.sh...]
    all_gather x6 -> x0, waiting for transfers between devices: 348 us -> none  [gathered(): return lax.all_gather(owned.astype(BF16), 'fsdp', axis=axis, tiled=True)]
    psum x2 -> x0, waiting for transfers between devices: 155 us -> none  [the longest x1 127 us: per_device(): vector_grad = lax.psum(grad_vectors, everyone)]
    reduce_scatter x3 -> x0, waiting for transfers between devices: 147 us -> none  [the longest x2 94.4 us: per_device(): lax.psum_scatter(piece.astype(BF16), 'fsdp', scatter_dimension=0, tiled=T...]
    dot_general x55 -> x0, matrix products: 137 us -> none  [the longest x11 27.6 us: matmul_keep(): return (jnp.dot(left, right, preferred_element_type=F32), (left, right))]
    all_gather x1, waiting for transfers between devices: 47.6 us -> 0.01 us  [per_device(): packed = lax.all_gather(packed, everyone, axis=0, tiled=True)]
    reduce_sum x15 -> x0, other arithmetic: 41 us -> none  [the longest x6 24.8 us: layer_norm(): return centred * lax.rsqrt(spread + 1e-06) * gain + shift]
    all_gather x2 -> x1, blocking collectives: 66.5 us -> 31.5 us  [per_device(): lax.all_gather(own_rows_grad, 'fsdp', axis=0, tiled=True)[:vectors.shape[0]]]
  transfers between devices with their start and end apart: 12 -> 1, of which waited for: 11 -> 0; matrix products, arithmetic and copies ran while one was open for 16% -> 2% of each run, Pallas kernels for 0% -> 17%
where the time goes in v2:
time: 762 us; the launch traced here: 755 us
  Pallas kernels  393 us (52%)
  blocking collectives  195 us (26%)
  other arithmetic  73.2 us (10%)
  matrix products  49.3 us (6%)
  local copies, waits for them, and re-layouts  22.6 us (3%)
  between operations  22 us (3%)
    pallas_call x1, Pallas kernels, gather_rows(): pl.pallas_call(kernel, out_shape=[jax.ShapeDtypeStruct((fsdp_count * a.sh...  210 us
    pallas_call x1, Pallas kernels, reduce_rows(): pl.pallas_call(functools.partial(reduce_kernel, cuts, lines), out_shape=j...  68.2 us
    pallas_call x1, Pallas kernels, backward(): pl.pallas_call(functools.partial(backward_kernel, images, hidden, count),...  60.1 us
    pallas_call x2, Pallas kernels, forward(): pl.pallas_call(functools.partial(forward_kernel, images, hidden, keep), g...  55.1 us
    all_gather x1, blocking collectives, per_device(): both = lax.all_gather(both, everyone, axis=0, tiled=True)  46.2 us
    add x5, other arithmetic, per_device(): TEACHER_KEEP * teachers[group] + (1.0 - TEACHER_KEEP) * updated  45.8 us
    unnamed x1, blocking collectives  33 us
    dot_general x8, matrix products, dot(): lax.dot_general(left, right, (dims, ((), ())), preferred_element_type=F32)  31.9 us
  transfers between devices with their start and end apart: 1, of which 0 were waited for; matrix products, arithmetic and copies ran while one was open for 2% of the time, Pallas kernels for 17%

profile of v2, /device:TPU:0, one launch (start us, length us, event | category | flops | bytes accessed | tf_op | source)
XLA Modules:
  0.0 754.8 jit_solution(13053709705105590622)
XLA Ops:
  7.2 1.9 slice.141
  9.1 1.6 slice_reduce_fusion.3
  10.7 1.8 slice.151
  12.5 1.4 slice.144.rows_table
  13.9 1.4 slice.154.rows_table
  15.3 1.6 convert.17
  17.0 1.3 convert_element_type.82.refs_6_
  18.2 0.9 copy-done.4
  19.1 1.3 convert_element_type.83.refs_7_
  20.4 0.6 pad.13.refs_0_
  21.1 0.6 pad.14.refs_3_
  21.7 3.4 copy.66.patches
  25.1 1.2 slice_bitcast_fusion.2
  26.4 1.0 maximum_maximum_fusion
  27.4 209.7 %gather_rows.1 = (bf16[384,640]{1,0:T(8,128)(2,1)}, bf16[384,4608]{1,0:T(8,128)(2,1)}, bf16[384,4608]{1,0:T(8,128)(2,1)}, bf16[384,640]{1,0:T(8,128)(2,1)}, bf16...) custom-call(bf16[48,640]{1,0:T(8,128)(2,1)} %pad.13.refs_0_, ...), custom_call_target="tpu_custom_call" | custom-call | tf_op jit(solution)/shard_map/gather_rows/pallas_call | solution.py:217
  237.1 0.8 broadcast_in_dim_broadcast_in_dim.3.covered
  237.9 27.0 %backbone_forward.2 = f32[16,384]{1,0:T(8,128)} custom-call(bf16[4,256,588]{2,1,0:T(8,128)(2,1)} %copy.66.patches, f32[4,256,1]{2,1,0:T(8,128)} %broadcast_in_dim_broadcast_in_dim.3.covered, bf16[384,640]{1,0:T(8,128)(2,1)} %get-tuple-element.44.weight_p, bf16[384,4608]{1,0:T(8,128)(2,1)} %get-tuple-element.45.weight_0, ...), custom_call_target="tpu_custom_call" | custom-call | tf_op jit(solution)/shard_map/backbone_forward/pallas_call | solution.py:673
  264.9 0.8 slice_reduce_fusion
  265.7 0.9 multiply_reduce_fusion.10
  266.7 5.3 fusion.88
  272.0 1.7 multiply_reduce_fusion.16
  273.8 1.0 copy.68.covered
  274.8 28.1 %backbone_forward.3 = (f32[16,384]{1,0:T(8,128)}, f32[4,272,384]{2,1,0:T(8,128)}, f32[4,272,384]{2,1,0:T(8,128)}, f32[4,272,384]{2,1,0:T(8,128)}, bf16[4,272,115...) custom-call(bf16[4,256,588]{2,1,0:T(8,128)(2,1)} %copy.66.patches, ...), custom_call_target="tpu_custom_call" | custom-call | tf_op jit(solution)/shard_map/backbone_forward/pallas_call | solution.py:673
  302.9 0.8 slice_reduce_fusion.1
  303.7 0.9 multiply_reduce_fusion.9
  304.6 0.8 constant_dynamic-update-slice_fusion.5
  305.4 1.8 constant_dynamic-update-slice_fusion.4
  307.2 4.6 fusion.5
  311.8 1.7 multiply_reduce_fusion.15
  313.7 46.2 %all-gather.1 = bf16[32,4,512]{2,1,0:T(4,128)(2,1)S(1)} all-gather(bf16[1,4,512]{2,1,0:T(4,128)(2,1)S(1)} %maximum_bitcast_fusion), channel_id=1, replica_groups=mesh['fsdp'=8,'dp'=4] {'fsdp','dp'}, dimensions={0}, use_global_device_ids=true | all-gather | bytes 135168 | tf_op jit(solution)/shard_map/all_gather | solution.py:1032
  360.0 5.0 fusion.127
  365.0 6.5 fusion.9
  371.5 2.6 multiply_reduce_fusion.2
  374.2 30.4 %all-gather.2 = f32[8,5,128]{2,1,0:T(8,128)S(1)} all-gather(f32[1,5,128]{2,1,0:T(8,128)S(1)} %bitcast.59), channel_id=2, replica_groups=mesh['fsdp'=8,'dp'=4] {'fsdp'}, dimensions={0}, use_global_device_ids=true | all-gather | bytes 23040 | tf_op jit(solution)/shard_map/all_gather | solution.py:1056
  406.0 5.4 subtract_convert_fusion
  411.4 4.1 fusion.19
  415.6 33.0 %all-reduce.3 = f32[8,4,256]{2,1,0:T(4,128)S(1)} all-reduce(f32[8,4,256]{2,1,0:T(4,128)S(1)} %dynamic-slice_bitcast_fusion), channel_id=3, replica_groups=mesh['fsdp'=8,'dp'=4] {'fsdp'}, use_global_device_ids=true, to_apply=%region_18.19.clone | all-reduce | flops 8192 | bytes 65536
  449.2 0.8 multiply_reduce_fusion.11
  450.0 0.7 constant_dynamic-update-slice_fusion.3
  450.7 1.5 fusion.17
  452.2 5.7 constant_dynamic-update-slice_fusion.2
  457.9 0.6 copy-done.22
  458.6 2.0 multiply_reduce_fusion.7
  460.9 0.6 pad.15.grad_cls
  461.5 0.7 pad_maximum_fusion.1.ends
  462.2 60.1 %backbone_backward.1 = bf16[384,10368]{1,0:T(8,128)(2,1)} custom-call(bf16[4,256,588]{2,1,0:T(8,128)(2,1)} %copy.66.patches, f32[4,256,1]{2,1,0:T(8,128)} %copy.68.covered, bf16[384,640]{1,0:T(8,128)(2,1)} %get-tuple-element.48.weight_p, bf16[384,4608]{1,0:T(8,128)(2,1)} %get-tuple-element.49.weight_0, bf16[384,4608]{1,0:T(8,128)(2,1)} %get-tuple-element.50.weight_1, ...), custom_call_target="tpu_custom_call" | custom-call | tf_op jit(solution)/shard_map/backbone_backward/pallas_call | solution.py:884
  522.3 68.2 %reduce_rows.1 = f32[48,10368]{1,0:T(8,128)} custom-call(bf16[4,2,48,10368]{3,2,1,0:T(8,128)(2,1)} %bitcast.53), custom_call_target="tpu_custom_call" | custom-call | tf_op jit(solution)/shard_map/reduce_rows/pallas_call | solution.py:443
  590.5 1.6 slice_bitcast_fusion.1
  592.1 0.9 copy-done.6
  593.0 1.1 multiply_reduce_fusion.4
  594.0 1.5 multiply_reduce_fusion.5
  596.9 31.5 %all_gather.22 = f32[65536]{0:T(1024)S(1)} all-gather(f32[8192]{0:T(1024)S(1)} %get-tuple-element.67), channel_id=1, replica_groups=mesh['fsdp'=8,'dp'=4] {'fsdp'}, dimensions={0}, use_global_device_ids=true | all-gather | bytes 294912 | tf_op jit(solution)/shard_map/all_gather | solution.py:1070
  628.4 1.5 fusion.125
  629.9 6.3 multiply_reduce_fusion
  636.2 0.8 divide_add_fusion
  636.9 2.6 reshape.162
  639.9 3.0 multiply_reduce_fusion.3
  644.9 31.5 %all_gather.23 = f32[384,384]{1,0:T(8,128)S(1)} all-gather(f32[48,384]{1,0:T(8,128)S(1)} %get-tuple-element.109), channel_id=1, replica_groups=mesh['fsdp'=8,'dp'=4] {'fsdp'}, dimensions={0}, use_global_device_ids=true | all-gather | bytes 663552 | tf_op jit(solution)/shard_map/all_gather | solution.py:1115
  676.4 22.1 %psum.7 = f32[]{:T(128)} all-reduce(f32[]{:T(128)S(6)} %add.267), channel_id=1, replica_groups=mesh['fsdp'=8,'dp'=4] {'fsdp'}, use_global_device_ids=true, to_apply=%region_29.30 | all-reduce | flops 1 | bytes 8 | tf_op jit(solution)/shard_map/psum | solution.py:1118
  699.4 7.3 multiply_add_fusion.4
  706.6 1.7 multiply_add_fusion.8
  708.4 1.4 multiply_add_fusion.6
  709.9 28.0 %multiply_add_fusion = (f32[8192,256]{1,0:T(8,128)}, f32[8192,256]{1,0:T(8,128)}, f32[8192,256]{1,0:T(8,128)}, f32[8192,256]{1,0:T(8,128)}) fusion(f32[8192,256]{1,0:T(8,128)} %param.43, f32[8192,256]{1,0:T(8,128)} %param.40, f32[8192,256]{1,0:T(8,128)} %get-tuple-element.145, f32[]{:T(128)S(6)} %div.170, f32[8192,256]{1,0:T(8,128)} %param.41, ...), kind=kLoop, calls=%fused_computation.3 | loop fusion | flops 39845888 | bytes 75497472 | tf_op jit(solution)/shard_map/add | solution.py:1143
  737.9 7.3 multiply_add_fusion.2
  (103 shorter events, 2.8 us)
Async XLA Ops:
  7.2 9.6 %copy-start.8 = (f32[2,48,4608]{2,1,0:T(8,128)S(1)}, f32[2,48,4608]{2,1,0:T(8,128)}, u32[]{:S(2)}) copy-start(f32[2,48,4608]{2,1,0:T(8,128)} %param.32) | copy-start | bytes 5308420
  7.2 629.7 %all-gather.6.cloned.1.call-start = ((), (), s32[]{:S(2)}) async-start(), calls=%async_computation | async-start | bytes 2331648 | tf_op jit(solution)/shard_map/all_gather | solution.py:1089
  9.1 7.8 %copy-start.2 = (f32[336,2048]{1,0:T(8,128)S(1)}, f32[336,2048]{1,0:T(8,128)}, u32[]{:S(2)}) copy-start(f32[336,2048]{1,0:T(8,128)} %param.39) | copy-start | bytes 8257540
  16.8 2.3 copy-start.4
  16.9 3.4 copy-start.13
  19.1 1.3 copy-start.15
  20.4 6.0 copy-start.11
  20.4 6.0 copy-start.12
  266.6 7.1 copy-start.26
  274.8 29.8 %copy-start.24 = (f32[384]{0:T(512)S(1)}, f32[384]{0:T(512)}, u32[]{:S(2)}) copy-start(f32[384]{0:T(512)} %get-tuple-element.70) | copy-start | bytes 4612
  274.8 29.8 %copy-start.25 = (f32[384]{0:T(512)S(1)}, f32[384]{0:T(512)}, u32[]{:S(2)}) copy-start(f32[384]{0:T(512)} %get-tuple-element.71) | copy-start | bytes 4612
  307.2 52.8 %copy-start.27 = (s32[128]{0:T(128)S(1)}, s32[128]{0:T(128)}, u32[]{:S(2)}) copy-start(s32[128]{0:T(128)} %param.26) | copy-start | bytes 1540
  307.2 52.8 %copy-start.19 = (f32[65536]{0:T(1024)S(1)}, f32[65536]{0:T(1024)}, u32[]{:S(2)}) copy-start(f32[65536]{0:T(1024)} %param.27) | copy-start | bytes 786436
  365.0 6.5 copy-start
  371.5 2.6 copy-start.1
  411.4 37.2 %copy-start.28 = (u32[32]{0:T(128)S(1)}, u32[32]{0:T(128)}, u32[]{:S(2)}) copy-start(u32[32]{0:T(128)} %constant.39) | copy-start | bytes 388
  452.2 6.4 copy-start.23
  457.9 0.6 copy-start.22
  592.1 0.9 copy-start.6
  639.9 59.4 %copy-start.7 = (f32[1,48,4608]{2,1,0:T(8,128)S(1)}, f32[1,48,4608]{2,1,0:T(8,128)}, u32[]{:S(2)}) copy-start(f32[1,48,4608]{2,1,0:T(8,128)} %copy-done.6) | copy-start | bytes 2654212
  699.3 7.4 copy-start.14
  699.3 7.3 copy-start.16
  699.3 7.3 copy-start.20
  699.3 7.3 copy-start.21
  699.3 9.1 %copy-start.9 = (f32[274,384]{1,0:T(8,128)S(1)}, f32[274,384]{1,0:T(8,128)}, u32[]{:S(2)}) copy-start(f32[274,384]{1,0:T(8,128)} %param.44) | copy-start | bytes 1262596
  699.3 9.1 %copy-start.10 = (f32[274,384]{1,0:T(8,128)S(1)}, f32[274,384]{1,0:T(8,128)}, u32[]{:S(2)}) copy-start(f32[274,384]{1,0:T(8,128)} %param.47) | copy-start | bytes 1262596
  699.3 9.1 %copy-start.17 = (f32[274,384]{1,0:T(8,128)S(1)}, f32[274,384]{1,0:T(8,128)}, u32[]{:S(2)}) copy-start(f32[274,384]{1,0:T(8,128)} %param.45) | copy-start | bytes 1262596
  699.4 9.0 %copy-start.18 = (f32[274,384]{1,0:T(8,128)S(1)}, f32[274,384]{1,0:T(8,128)}, u32[]{:S(2)}) copy-start(f32[274,384]{1,0:T(8,128)} %param.46) | copy-start | bytes 1262596
  709.9 28.0 %copy-start.3 = (f32[336,2048]{1,0:T(8,128)S(1)}, f32[336,2048]{1,0:T(8,128)}, u32[]{:S(2)}) copy-start(f32[336,2048]{1,0:T(8,128)} %param.39) | copy-start | bytes 8257540
  709.9 28.0 %copy-start.5 = (f32[336,2048]{1,0:T(8,128)S(1)}, f32[336,2048]{1,0:T(8,128)}, u32[]{:S(2)}) copy-start(f32[336,2048]{1,0:T(8,128)} %param.36) | copy-start | bytes 8257540
Sparse Core Ops, SparseCore 0:
  458.7 53.0 all-gather.5

commit v3 on v2

--- a/solution.py
+++ b/solution.py
@@ -33,7 +33,7 @@
     return spans
 
 
-def gather_kernel(items, lines, sources, targets, send, recv, copied):
+def gather_kernel(items, early, lines, sources, heads, targets, send, recv, copied, send_e, recv_e):
     fsdp, dp = lax.axis_index("fsdp"), lax.axis_index("dp")
     z, x = fsdp // 2, fsdp % 2
     y, core = dp // 2, dp % 2
@@ -49,13 +49,11 @@
     def when(condition, body):
         pl.when(condition)(body)
 
-    greet(across, dp)
+    for step in range(1, 2 * lines):
+        greet(lax.rem(fsdp + step, 2 * lines), dp)
     greet(fsdp, mate)
-    when(z + 1 < lines, lambda: greet(fsdp + 2, dp))
-    when(z > 0, lambda: greet(fsdp - 2, dp))
     when(core == 0, lambda: greet(fsdp, opposite))
-    ends = (z + 1 < lines).astype(jnp.int32) + (z > 0).astype(jnp.int32)
-    pl.semaphore_wait(barrier, 3 - core + ends)
+    pl.semaphore_wait(barrier, 2 * lines + 1 - core)
 
     hops = lines - 1
     UP, DOWN, ACROSS, OPPOSITE, MATE = 0, hops, 2 * hops, 4 * hops + 1, 4 * hops + 2
@@ -154,8 +152,62 @@
     def to_mate(index, part, second=0):
         return move(index, MATE + second, whole(index, part), whole(index, part), fsdp, mate)
 
+    def deal(part, act):
+        for index, (number, places) in early.items():
+            _, rows, spans = items[index]
+            at, size = spans[part]
+            target = sources[items[index][0]].at[:, pl.ds(at, size)]
+            for f, (owner, start) in enumerate(places):
+                source = heads[number].at[pl.ds(start, rows), pl.ds(at, size)]
+                act(index, f, owner, source, target)
+
+    def early_copy(index, f, source, target):
+        return pltpu.make_async_remote_copy(
+            src_ref=source,
+            dst_ref=target,
+            send_sem=send_e.at[index, f],
+            recv_sem=recv_e.at[index],
+            device_id=(f, dp),
+            device_id_type=pl.DeviceIdType.MESH,
+        )
+
+    def deal_start(index, f, owner, source, target):
+        if f == owner:
+            when(
+                fsdp == f,
+                lambda: pltpu.make_async_copy(source, target, recv_e.at[index]).start(),
+            )
+        else:
+            when(fsdp == owner, lambda: early_copy(index, f, source, target).start())
+
+    def deal_end(index, f, owner, source, target):
+        if f != owner:
+            when(fsdp == owner, lambda: early_copy(index, f, source, target).wait_send())
+
+    def dealt(index, part):
+        _, rows, spans = items[index]
+        at, size = spans[part]
+        number, places = early[index]
+        target = sources[items[index][0]].at[:, pl.ds(at, size)]
+        for f, (owner, start) in enumerate(places):
+            source = heads[number].at[pl.ds(start, rows), pl.ds(at, size)]
+            if f == owner:
+                when(
+                    fsdp == f,
+                    lambda source=source: pltpu.make_async_copy(
+                        source, target, recv_e.at[index]
+                    ).wait(),
+                )
+            else:
+                when(
+                    fsdp == f,
+                    lambda f=f, source=source: early_copy(index, f, source, target).wait_recv(),
+                )
+
     def stage(index, part, step):
         if step == 0:
+            if index in early:
+                dealt(index, part)
             keep(index, part).start()
             z_steps(index, part, 0, lambda copy: copy.start())
             x_steps(index, part, 0, lambda copy: copy.start())
@@ -183,6 +235,7 @@
                 when(y == 1, lambda: to_mate(index, 0, 1).wait_recv())
 
     def run(part):
+        deal(part, deal_start)
         steps = lines + 3
         for tick in range(len(items) + steps - 1):
             for step in range(steps):
@@ -196,39 +249,56 @@
                 to_opposite(index, part).wait_send()
                 to_mate(index, 2 - part, 1).wait_send()
             to_mate(index, part).wait_send()
+        deal(part, deal_end)
 
     roles(run)
 
 
-def gather_rows(arrays, fsdp_count, cuts, collective_id):
+def gather_rows(arrays, heads, ranges, fsdp_count, collective_id):
     lines = fsdp_count // 2
-    items = []
-    for number, array in enumerate(arrays):
-        rows, width = array.shape
-        step = width // cuts[number]
-        for cut in range(cuts[number]):
-            items.append((number, rows, third_ranges(step, cut * step)))
+    head_rows, head_width = heads[0].shape
+    shapes = [array.shape for array in arrays]
+    items = [(number, shape[0], third_ranges(shape[1], 0)) for number, shape in enumerate(shapes)]
+    early = {}
     count = len(arrays)
+    for low, high in ranges:
+        for number in range(len(heads)):
+            rows = (high - low) // fsdp_count
+            starts = [low + rows * f for f in range(fsdp_count)]
+            early[len(items)] = (
+                number,
+                [(start // head_rows, start % head_rows) for start in starts],
+            )
+            shapes.append((rows, head_width))
+            items.append((len(shapes) - 1, rows, third_ranges(head_width, 0)))
     slots = 4 * (lines - 1) + 4
+    extra = len(shapes) - count
+    heads_at = count + len(heads)
 
     def kernel(*refs):
-        gather_kernel(items, lines, refs[:count], refs[count : 2 * count], *refs[2 * count :])
-
-    return pl.pallas_call(
+        targets = refs[heads_at : heads_at + len(shapes)]
+        blocks = refs[:count] + refs[heads_at + len(shapes) : heads_at + len(shapes) + extra]
+        rest = refs[heads_at + len(shapes) + extra :]
+        gather_kernel(items, early, lines, blocks, refs[count:heads_at], targets, *rest)
+
+    anywhere = pl.BlockSpec(memory_space=pl.ANY)
+    out = pl.pallas_call(
         kernel,
-        out_shape=[
-            jax.ShapeDtypeStruct((fsdp_count * a.shape[0], a.shape[1]), a.dtype) for a in arrays
-        ],
-        in_specs=[pl.BlockSpec(memory_space=pl.ANY)] * count,
-        out_specs=[pl.BlockSpec(memory_space=pl.ANY)] * count,
+        out_shape=[jax.ShapeDtypeStruct((fsdp_count * r, c), BF16) for r, c in shapes]
+        + [jax.ShapeDtypeStruct(shape, BF16) for shape in shapes[count:]],
+        in_specs=[anywhere] * heads_at,
+        out_specs=[anywhere] * (len(shapes) + extra),
         scratch_shapes=[
             pltpu.SemaphoreType.DMA((len(items), slots)),
             pltpu.SemaphoreType.DMA((len(items), slots)),
             pltpu.SemaphoreType.DMA((len(items),)),
+            pltpu.SemaphoreType.DMA((len(items), fsdp_count)),
+            pltpu.SemaphoreType.DMA((len(items),)),
         ],
         compiler_params=pltpu.CompilerParams(collective_id=collective_id, has_side_effects=True),
         name="gather_rows",
-    )(*arrays)
+    )(*arrays, *heads)
+    return out[: len(shapes)]
 
 
 def reduce_kernel(
@@ -913,6 +983,522 @@
     )(patches, covered[..., None], weight_p, weight_0, weight_1, rows, ends, grad_cls, *saved)
 
 
+def owners_of(low, high, rows, count):
+    return [f for f in range(count) if f * rows < high and (f + 1) * rows > low]
+
+
+def two_halves(value):
+    half = value.shape[1] // 2
+    return jnp.concatenate([value[:, :half], value[:, half:]], 0).astype(BF16)
+
+
+def from_halves(slots):
+    wide = slots.astype(F32)
+    half = wide.shape[-1]
+    first = wide[:, :8, :].reshape(-1, half)
+    second = wide[:, 8:, :].reshape(-1, half)
+    return jnp.concatenate([first, second], -1)
+
+
+def student_rows(value, start=0):
+    pieces = [value[at + start : at + start + 4, :] for at in range(0, value.shape[0], 8)]
+    return jnp.concatenate(pieces, 0)
+
+
+def sixteen(value):
+    return jnp.concatenate([value, jnp.zeros_like(value)], 0).astype(BF16)
+
+
+def head_kernel(
+    sizes, cls, gains, first_s, first_t, third_s, third_t, shard_s, shard_t, centre, counted_row,
+    counted_col, proto_s, proto_t,
+    grad_cls, ends, loss_row, totals, grad_logits, unit_rows, grad_head,
+    table_s, table_t, loading, wide_s, wide_t, kept, left, acts, parts_out, parts_in, units,
+    stats, pulls, pulled, backs, pieces, pieced, extra_1, extra_3, lefts, rights, tall,
+    send, recv, send_z, recv_z, send_x, recv_x, send_d, recv_d,
+):
+    count, dp_count, rows, chunk = sizes
+    fsdp, dp = lax.axis_index("fsdp"), lax.axis_index("dp")
+    model, hidden = first_s.shape
+    width = third_s.shape[0]
+    top_2, top_3 = model, model + hidden
+    top_4 = top_3 + width
+    span = kept.shape[0] // 2
+    base = fsdp * rows // 128 * 128
+    offset = fsdp * rows - base
+    slot_rows = 8 * count
+    is_student = lax.broadcasted_iota(jnp.int32, (8, 1), 0) < 4
+    owners_1 = owners_of(0, top_2, rows, count)
+    owners_2 = owners_of(top_2, top_3, rows, count)
+    owners_3 = owners_of(top_3, top_4, rows, count)
+
+    load_s = pltpu.make_async_copy(proto_s, table_s, loading.at[0])
+    load_t = pltpu.make_async_copy(proto_t, table_t, loading.at[1])
+    load_s.start()
+    load_t.start()
+
+    barrier = pltpu.get_barrier_semaphore()
+    for f_step in range(count):
+        for d_step in range(dp_count):
+            if f_step or d_step:
+                peer_f = lax.rem(fsdp + f_step, count)
+                peer_d = lax.rem(dp + d_step, dp_count)
+                pl.semaphore_signal(barrier, 1, device_id=(peer_f, peer_d), device_id_type=MESH)
+    pl.semaphore_wait(barrier, count * dp_count - 1)
+
+    ACTS, PARTS, STATS, PULLS, BACKS, PIECES, TOTALS = range(7)
+
+    def swap(kind, step, source_of, target):
+        peer = lax.rem(fsdp + step, count)
+        return pltpu.make_async_remote_copy(
+            src_ref=source_of(peer),
+            dst_ref=target.at[fsdp],
+            send_sem=send.at[kind, step - 1],
+            recv_sem=recv.at[kind, fsdp],
+            device_id=(peer, dp),
+            device_id_type=MESH,
+        )
+
+    def begin(kind, source_of, target):
+        for step in range(1, count):
+            swap(kind, step, source_of, target).start()
+
+    def arrive(kind, target):
+        for step in range(1, count):
+            peer = lax.rem(fsdp + step, count)
+            pltpu.make_async_remote_copy(
+                src_ref=target.at[peer],
+                dst_ref=target.at[peer],
+                send_sem=send.at[kind, step - 1],
+                recv_sem=recv.at[kind, peer],
+                device_id=(peer, dp),
+                device_id_type=MESH,
+            ).wait_recv()
+
+    def end(kind, source_of, target):
+        for step in range(1, count):
+            swap(kind, step, source_of, target).wait_send()
+
+    def each_net(value, first, second, product):
+        low = sixteen(value)
+        return jnp.where(is_student, product(low, first)[:8, :], product(low, second)[:8, :])
+
+    unit_c, lift_c = norm_parts(cls[...])
+    normed = unit_c * gains[:8, :] + gains[8:, :]
+    pre_a = each_net(normed, first_s[...], first_t[...], mm)
+    act_a, slope_a = gelu_both(pre_a)
+    acts[fsdp] = two_halves(act_a)
+    begin(ACTS, lambda peer: acts.at[fsdp], acts)
+
+    row = fsdp * rows + lax.broadcasted_iota(jnp.int32, (rows, 1), 0)
+    inside = (row >= top_2) & (row < top_3)
+    kept[...] = jnp.zeros_like(kept)
+    place = pl.multiple_of(offset, 16)
+    kept[pl.ds(place, rows), :] = jnp.where(inside, shard_s[...], 0.0).astype(BF16)
+    kept[pl.ds(pl.multiple_of(span + offset, 16), rows), :] = jnp.where(
+        inside, shard_t[...], 0.0
+    ).astype(BF16)
+    left[...] = jnp.zeros_like(left)
+    columns = pl.ds(pl.multiple_of(base, 128), span)
+
+    arrive(ACTS, acts)
+    left[:, top_2:top_3] = from_halves(acts[...])
+    asked = left[:, columns].astype(BF16)
+    net = lax.broadcasted_iota(jnp.int32, (slot_rows, 1), 0) % 8 < 4
+    product = jnp.where(net, mm(asked, kept[:span, :]), mm(asked, kept[span:, :]))
+    for f in range(count):
+        parts_out[f] = two_halves(product[8 * f : 8 * f + 8, :])
+    parts_in[fsdp] = parts_out[fsdp]
+    begin(PARTS, lambda peer: parts_out.at[peer], parts_in)
+    arrive(PARTS, parts_in)
+    summed = from_halves(parts_in[...])
+    pre_b = summed[:8, :]
+    for f in range(1, count):
+        pre_b = pre_b + summed[8 * f : 8 * f + 8, :]
+    act_b, slope_b = gelu_both(pre_b)
+    raw = each_net(act_b, third_s[...], third_t[...], mm_nt)
+    lift_z = lax.rsqrt(jnp.sum(raw * raw, -1, keepdims=True) + 1e-06)
+    unit_z = raw * lift_z
+
+    me = fsdp * dp_count + dp
+    everyone = count * dp_count
+    units[me] = two_halves(unit_z)
+
+    def unit_copy(step):
+        peer = lax.rem(me + step, everyone)
+        return pltpu.make_async_remote_copy(
+            src_ref=units.at[me],
+            dst_ref=units.at[me],
+            send_sem=send_z.at[step - 1],
+            recv_sem=recv_z.at[me],
+            device_id=(peer // dp_count, lax.rem(peer, dp_count)),
+            device_id_type=MESH,
+        )
+
+    for step in range(1, everyone):
+        unit_copy(step).start()
+
+    def owner_copy(kind, owner, source, target):
+        return pltpu.make_async_remote_copy(
+            src_ref=source,
+            dst_ref=target.at[fsdp],
+            send_sem=send_x.at[kind, owner],
+            recv_sem=recv_x.at[kind, fsdp],
+            device_id=(owner, dp),
+            device_id_type=MESH,
+        )
+
+    def owners_begin(kind, owners, target, value):
+        target[fsdp] = value
+        for owner in owners:
+            pl.when(fsdp != owner)(
+                lambda owner=owner: owner_copy(kind, owner, target.at[fsdp], target).start()
+            )
+
+    def owners_end(kind, owners, target):
+        for owner in owners:
+            pl.when(fsdp != owner)(
+                lambda owner=owner: owner_copy(kind, owner, target.at[fsdp], target).wait_send()
+            )
+
+    def owners_arrive(kind, owners, target):
+        for owner in owners:
+
+            @pl.when(fsdp == owner)
+            def _(owner=owner):
+                for f in range(count):
+                    if f != owner:
+                        pltpu.make_async_remote_copy(
+                            src_ref=target.at[f],
+                            dst_ref=target.at[f],
+                            send_sem=send_x.at[kind, owner],
+                            recv_sem=recv_x.at[kind, f],
+                            device_id=(f, dp),
+                            device_id_type=MESH,
+                        ).wait_recv()
+
+    for step in range(1, everyone):
+        peer = lax.rem(me + step, everyone)
+        pltpu.make_async_remote_copy(
+            src_ref=units.at[peer],
+            dst_ref=units.at[peer],
+            send_sem=send_z.at[step - 1],
+            recv_sem=recv_z.at[peer],
+            device_id=(peer // dp_count, lax.rem(peer, dp_count)),
+            device_id_type=MESH,
+        ).wait_recv()
+    all_units = from_halves(units[...])
+    rows_s = student_rows(all_units).astype(BF16)
+    rows_t = student_rows(all_units, 4).astype(BF16)
+    unit_rows[...] = rows_s
+
+    load_s.wait()
+    load_t.wait()
+    images = rows_s.shape[0]
+    chunks = table_s.shape[0] // chunk
+    low_start = jnp.full((images, 128), -3.0e38, F32)
+
+    def lanes(op, value):
+        out = value[:, :128]
+        for at in range(128, value.shape[1], 128):
+            out = op(out, value[:, at : at + 128])
+        return out
+
+    def logits_pass(index, tops):
+        top_t, top_s = tops
+        at = pl.ds(pl.multiple_of(index * chunk, chunk), chunk)
+        raw_t = mm_nt(rows_t, table_t[at, :].astype(BF16))
+        totals[fsdp, pl.ds(index, 1), :] = column_sum(counted_col[...] * raw_t)
+        scaled_t = (raw_t - centre[:, at]) * (1.0 / TEACHER_TEMP)
+        scaled_s = mm_nt(rows_s, table_s[at, :].astype(BF16)) * (1.0 / STUDENT_TEMP)
+        wide_t[:, at] = scaled_t
+        wide_s[:, at] = scaled_s
+        return (
+            jnp.maximum(top_t, lanes(jnp.maximum, scaled_t)),
+            jnp.maximum(top_s, lanes(jnp.maximum, scaled_s)),
+        )
+
+    top_t, top_s = lax.fori_loop(0, chunks, logits_pass, (low_start, low_start))
+    top_t = jnp.max(top_t, -1, keepdims=True)
+    top_s = jnp.max(top_s, -1, keepdims=True)
+    begin(TOTALS, lambda peer: totals.at[fsdp], totals)
+
+    def expo_pass(index, sums):
+        sum_t, sum_s, cross = sums
+        at = pl.ds(pl.multiple_of(index * chunk, chunk), chunk)
+        shifted_s = wide_s[:, at] - top_s
+        expo_t = jnp.exp(wide_t[:, at] - top_t)
+        expo_s = jnp.exp(shifted_s)
+        wide_t[:, at] = expo_t
+        wide_s[:, at] = expo_s
+        return (
+            sum_t + lanes(jnp.add, expo_t),
+            sum_s + lanes(jnp.add, expo_s),
+            cross + lanes(jnp.add, expo_t * shifted_s),
+        )
+
+    zero = jnp.zeros((images, 128), F32)
+    sum_t, sum_s, cross = lax.fori_loop(0, chunks, expo_pass, (zero, zero, zero))
+    lane = lax.broadcasted_iota(jnp.int32, (images, 128), 1)
+    columns_of = zero
+    values = (top_t, jnp.sum(sum_t, -1, keepdims=True), top_s, jnp.sum(sum_s, -1, keepdims=True),
+              jnp.sum(cross, -1, keepdims=True))
+    for number, value in enumerate(values):
+        columns_of = jnp.where(lane == number, value, columns_of)
+    stats[fsdp] = columns_of.T[:8, :]
+    begin(STATS, lambda peer: stats.at[fsdp], stats)
+    arrive(STATS, stats)
+    gathered = [stats[f] for f in range(count)]
+    high_t, high_s = gathered[0][0:1, :], gathered[0][2:3, :]
+    for part in gathered[1:]:
+        high_t = jnp.maximum(high_t, part[0:1, :])
+        high_s = jnp.maximum(high_s, part[2:3, :])
+    total_t = total_s = crossed = jnp.zeros_like(high_t)
+    for part in gathered:
+        lift_t = jnp.exp(part[0:1, :] - high_t)
+        total_t = total_t + part[1:2, :] * lift_t
+        total_s = total_s + part[3:4, :] * jnp.exp(part[2:3, :] - high_s)
+        crossed = crossed + lift_t * (part[4:5, :] + (part[2:3, :] - high_s) * part[1:2, :])
+    counted = counted_row[...]
+    loss_row[...] = counted * (jnp.log(total_s) - crossed / total_t)
+    weighting = counted / jnp.maximum(jnp.sum(counted, -1, keepdims=True), 1.0) / STUDENT_TEMP
+    mine = stats[fsdp]
+    share_s = weighting * jnp.exp(mine[2:3, :] - high_s) / total_s
+    share_t = weighting * jnp.exp(mine[0:1, :] - high_t) / total_t
+    turned = jnp.concatenate([share_s, share_t, jnp.zeros((126, images), F32)], 0).T
+    share_s, share_t = turned[:, 0:1], turned[:, 1:2]
+
+    def grad_pass(index, total):
+        at = pl.ds(pl.multiple_of(index * chunk, chunk), chunk)
+        low = (wide_s[:, at] * share_s - wide_t[:, at] * share_t).astype(BF16)
+        grad_logits[:, at] = low
+        return total + mm(low, table_s[at, :].astype(BF16))
+
+    partial = lax.fori_loop(0, chunks, grad_pass, jnp.zeros((images, width), F32))
+    for slot in range(0, everyone, 2):
+        pair = partial[4 * slot : 4 * slot + 8, :]
+        pulls[slot] = pair
+        pulls[slot + 1] = jnp.concatenate([pair[4:, :], pair[:4, :]], 0)
+    pulled[fsdp] = pulls[me]
+    begin(PULLS, lambda peer: pulls.at[peer * dp_count + dp], pulled)
+    arrive(PULLS, pulled)
+    grad_z = pulled[0]
+    for f in range(1, count):
+        grad_z = grad_z + pulled[f]
+    grad_z = jnp.where(is_student, grad_z, 0.0)
+    grad_raw = lift_z * (grad_z - unit_z * jnp.sum(unit_z * grad_z, -1, keepdims=True))
+    grad_b = mm(sixteen(grad_raw), third_s[...])[:8, :]
+    pre_grad_b = jnp.where(is_student, grad_b * slope_b, 0.0)
+    backs[fsdp] = two_halves(pre_grad_b)
+    begin(BACKS, lambda peer: backs.at[fsdp], backs)
+    arrive(BACKS, backs)
+    grads_b = from_halves(backs[...])
+    piece = mm_nt(grads_b.astype(BF16), kept[:span, :])
+    for f in range(count):
+        pieces[f] = piece[8 * f : 8 * f + 8, :]
+    pieced[fsdp] = pieces[fsdp]
+    begin(PIECES, lambda peer: pieces.at[peer], pieced)
+
+    owned = [
+        (fsdp >= owners[0]) & (fsdp <= owners[-1]) for owners in (owners_1, owners_2, owners_3)
+    ]
+
+    def group_copy(kind, step, place):
+        peer = lax.rem(dp + step, dp_count)
+        return pltpu.make_async_remote_copy(
+            src_ref=place(dp),
+            dst_ref=place(dp),
+            send_sem=send_d.at[kind, step - 1],
+            recv_sem=recv_d.at[kind, dp],
+            device_id=(fsdp, peer),
+            device_id_type=MESH,
+        )
+
+    def group_arrive(kind, place):
+        for step in range(1, dp_count):
+            peer = lax.rem(dp + step, dp_count)
+            pltpu.make_async_remote_copy(
+                src_ref=place(peer),
+                dst_ref=place(peer),
+                send_sem=send_d.at[kind, step - 1],
+                recv_sem=recv_d.at[kind, peer],
+                device_id=(fsdp, peer),
+                device_id_type=MESH,
+            ).wait_recv()
+
+    def right_at(number):
+        return lambda group: rights.at[group, number]
+
+    def left_at(group):
+        return lefts.at[group]
+
+    def group_begin(kind, place):
+        for step in range(1, dp_count):
+            group_copy(kind, step, place).start()
+
+    def group_end(kind, place):
+        for step in range(1, dp_count):
+            group_copy(kind, step, place).wait_send()
+
+    @pl.when(owned[1])
+    def _():
+        rights[dp, 1] = student_rows(grads_b).astype(BF16)
+        group_begin(2, right_at(1))
+
+    owners_begin(1, owners_3, extra_3, two_halves(jnp.concatenate([act_b, grad_raw], -1)))
+    arrive(PIECES, pieced)
+    back_a = jnp.zeros((8, left.shape[1]), F32)
+    for f in range(count):
+        at = f * rows // 128 * 128
+        value = [pieced[f]]
+        if at:
+            value = [jnp.zeros((8, at), F32)] + value
+        if left.shape[1] - at - span:
+            value = value + [jnp.zeros((8, left.shape[1] - at - span), F32)]
+        back_a = back_a + jnp.concatenate(value, -1)
+    pre_grad_a = jnp.where(is_student, back_a[:, top_2:top_3] * slope_a, 0.0)
+    spare = jnp.zeros((8, 2 * extra_1.shape[2] - model - hidden), F32)
+    owners_begin(
+        0, owners_1, extra_1, two_halves(jnp.concatenate([normed, pre_grad_a, spare], -1))
+    )
+    grad_n = jnp.where(is_student, mm_nt(sixteen(pre_grad_a), first_s[...])[:8, :], 0.0)
+    grad_cls[...] = norm_back(grad_n, gains[:8, :], unit_c, lift_c)
+    ends[...] = jnp.concatenate(
+        [column_sum(grad_n * unit_c), column_sum(grad_n), jnp.zeros((6, model), F32)], 0
+    )
+
+    owners_arrive(1, owners_3, extra_3)
+
+    @pl.when(owned[2])
+    def _():
+        extra = from_halves(extra_3[...])
+        left[:, top_3:top_4] = extra[:, hidden:]
+        rights[dp, 2] = student_rows(extra[:, :hidden]).astype(BF16)
+        group_begin(3, right_at(2))
+
+    owners_arrive(0, owners_1, extra_1)
+
+    @pl.when(owned[0])
+    def _():
+        extra = from_halves(extra_1[...])
+        left[:, :top_2] = extra[:, :model]
+        rights[dp, 0] = student_rows(extra[:, model : model + hidden]).astype(BF16)
+        group_begin(1, right_at(0))
+
+    lefts[dp] = student_rows(left[:, columns]).astype(BF16)
+    group_begin(0, left_at)
+    group_arrive(0, left_at)
+    tall[...] = jnp.zeros_like(tall)
+    column = base + lax.broadcasted_iota(jnp.int32, (1, span), 1)
+    for number, (low, high) in enumerate(((0, top_2), (top_2, top_3), (top_3, top_4))):
+
+        @pl.when(owned[number])
+        def _(number=number, low=low, high=high):
+            group_arrive(1 + number, right_at(number))
+            own_side = jnp.concatenate([lefts[group] for group in range(dp_count)], 0)
+            keep_columns = ((column >= low) & (column < high)).astype(F32)
+            own_side = (own_side.astype(F32) * keep_columns).astype(BF16)
+            other = jnp.concatenate([rights[group, number] for group in range(dp_count)], 0)
+            tall[...] += mm_tn(own_side, other)
+            group_end(1 + number, right_at(number))
+
+    grad_head[...] = tall[pl.ds(place, rows), :]
+    group_end(0, left_at)
+    arrive(TOTALS, totals)
+    end(ACTS, lambda peer: acts.at[fsdp], acts)
+    end(PARTS, lambda peer: parts_out.at[peer], parts_in)
+    end(STATS, lambda peer: stats.at[fsdp], stats)
+    end(PULLS, lambda peer: pulls.at[peer * dp_count + dp], pulled)
+    end(BACKS, lambda peer: backs.at[fsdp], backs)
+    end(PIECES, lambda peer: pieces.at[peer], pieced)
+    end(TOTALS, lambda peer: totals.at[fsdp], totals)
+    for step in range(1, everyone):
+        unit_copy(step).wait_send()
+    owners_end(0, owners_1, extra_1)
+    owners_end(1, owners_3, extra_3)
+
+
+def head_step(
+    cls_s, cls_t, vecs_s, vecs_t, weights, shards, centre, counted, protos, counts, collective_id
+):
+    count, dp_count = counts
+    model, hidden = weights[0].shape
+    width = weights[2].shape[0]
+    rows = shards[0].shape[0]
+    owned_k = protos[0].shape[0]
+    images = counted.shape[0]
+    everyone = count * dp_count
+    span = max(f * rows % 128 + rows for f in range(count))
+    span = (span + 127) // 128 * 128
+    extent = max(f * rows // 128 * 128 + span for f in range(count))
+    chunk = 1024
+    cls = jnp.concatenate([cls_s[:4], cls_t[:4]])
+    gains = jnp.concatenate(
+        [
+            jnp.broadcast_to(vecs[vecs.shape[0] + row][None], (4, model))
+            for row in (-2, -1)
+            for vecs in (vecs_s, vecs_t)
+        ]
+    )
+    shape = jax.ShapeDtypeStruct
+    vmem = pl.BlockSpec(memory_space=pltpu.VMEM)
+    anywhere = pl.BlockSpec(memory_space=pl.ANY)
+    extra_width = (model + hidden + 255) // 256 * 128
+    sems = pltpu.SemaphoreType.DMA
+    return pl.pallas_call(
+        functools.partial(head_kernel, (count, dp_count, rows, chunk)),
+        out_shape=[
+            shape((8, model), F32),
+            shape((8, model), F32),
+            shape((1, images), F32),
+            shape((count, owned_k // chunk, chunk), F32),
+            shape((images, owned_k), BF16),
+            shape((images, width), BF16),
+            shape((rows, hidden), F32),
+        ],
+        in_specs=[vmem] * 11 + [anywhere] * 2,
+        out_specs=[vmem] * 7,
+        scratch_shapes=[
+            pltpu.VMEM((owned_k, width), F32),
+            pltpu.VMEM((owned_k, width), F32),
+            sems((2,)),
+            pltpu.VMEM((images, owned_k), F32),
+            pltpu.VMEM((images, owned_k), F32),
+            pltpu.VMEM((2 * span, hidden), BF16),
+            pltpu.VMEM((8 * count, extent), F32),
+            pltpu.VMEM((count, 16, hidden // 2), BF16),
+            pltpu.VMEM((count, 16, hidden // 2), BF16),
+            pltpu.VMEM((count, 16, hidden // 2), BF16),
+            pltpu.VMEM((everyone, 16, width // 2), BF16),
+            pltpu.VMEM((count, 8, 128), F32),
+            pltpu.VMEM((everyone, 8, width), F32),
+            pltpu.VMEM((count, 8, width), F32),
+            pltpu.VMEM((count, 16, hidden // 2), BF16),
+            pltpu.VMEM((count, 8, span), F32),
+            pltpu.VMEM((count, 8, span), F32),
+            pltpu.VMEM((count, 16, extra_width), BF16),
+            pltpu.VMEM((count, 16, (hidden + width) // 2), BF16),
+            pltpu.VMEM((dp_count, 4 * count, span), BF16),
+            pltpu.VMEM((dp_count, 3, 4 * count, hidden), BF16),
+            pltpu.VMEM((span, hidden), F32),
+            sems((7, count - 1)),
+            sems((7, count)),
+            sems((everyone - 1,)),
+            sems((everyone,)),
+            sems((2, count)),
+            sems((2, count)),
+            sems((4, dp_count - 1)),
+            sems((4, dp_count)),
+        ],
+        compiler_params=pltpu.CompilerParams(
+            collective_id=collective_id, has_side_effects=True, vmem_limit_bytes=60 << 20
+        ),
+        name="head_step",
+    )(
+        cls, gains, *weights, *shards, centre[None], counted[None], counted[:, None], *protos
+    )
+
+
 def dot(left, right, dims):
     return lax.dot_general(left, right, (dims, ((), ())), preferred_element_type=F32)
 
@@ -953,21 +1539,102 @@
     return (weight - step_rate * (direction + weight_decay * weight), moment, second)
 
 
-def small_mesh():
-    return lax.axis_size("dp") == 4 and lax.axis_size("fsdp") in (4, 8)
-
-
-def gather_all(arrays, cuts):
-    if small_mesh():
-        return gather_rows(arrays, lax.axis_size("fsdp"), cuts, 1)
-    return [lax.all_gather(array, "fsdp", axis=0, tiled=True) for array in arrays]
-
-
-def reduce_all(grads):
-    if small_mesh():
+def own_kernels(local, head_rows, model, hidden, total):
+    count = lax.axis_size("fsdp")
+    if lax.axis_size("dp") != 4 or count not in (4, 8) or local != 4 or head_rows % 16:
+        return False
+    for low, high in ((0, model), (hidden + model, total)):
+        rows = (high - low) // count
+        if rows % 16 or any((low + rows * f) % head_rows + rows > head_rows for f in range(count)):
+            return False
+    return True
+
+
+def reduce_all(grads, own):
+    if own:
         return reduce_rows(grads, lax.axis_size("fsdp"), 3, 2)
     owned = lax.psum_scatter(grads, "fsdp", scatter_dimension=0, tiled=True)
     return lax.psum(owned, "dp").astype(F32)
+
+
+def head_plain(
+    cls, teacher_cls, vectors, teacher_vectors, head_full, teacher_head_full, own_centre, counted,
+    counted_total, w_proto, teacher_proto, own_rows,
+):
+    teacher_unit = unit(head_forward(teacher_cls, teacher_head_full, teacher_vectors)[-1])
+    low_n, pre_a, low_a, pre_b, low_b, raw = head_forward(cls, head_full, vectors)
+    bottleneck, pull_unit = jax.vjp(unit, raw)
+    both = jnp.concatenate([teacher_unit.astype(BF16), bottleneck.astype(BF16)], -1)
+    both = lax.all_gather(both, ("fsdp", "dp"), axis=0, tiled=True)
+    width = raw.shape[1]
+    teacher_rows, student_rows = both[:, :width], both[:, width:]
+
+    low_proto = w_proto.astype(BF16)
+    teacher_logits = dot(teacher_rows, teacher_proto.astype(BF16), ((1,), (1,)))
+    logits = dot(student_rows, low_proto, ((1,), (1,)))
+    scaled_t = (teacher_logits - own_centre) / TEACHER_TEMP
+    scaled_s = logits / STUDENT_TEMP
+    max_t = jnp.max(scaled_t, -1)
+    max_s = jnp.max(scaled_s, -1)
+    expo_t = jnp.exp(scaled_t - max_t[:, None])
+    expo_s = jnp.exp(scaled_s - max_s[:, None])
+    parts = jnp.stack(
+        [
+            max_t,
+            jnp.sum(expo_t, -1),
+            max_s,
+            jnp.sum(expo_s, -1),
+            jnp.sum(expo_t * (scaled_s - max_s[:, None]), -1),
+        ]
+    )
+    parts = lax.all_gather(parts, "fsdp", axis=0)
+    top_t = jnp.max(parts[:, 0], 0)
+    lift_t = jnp.exp(parts[:, 0] - top_t)
+    total_t = jnp.sum(parts[:, 1] * lift_t, 0)
+    top_s = jnp.max(parts[:, 2], 0)
+    total_s = jnp.sum(parts[:, 3] * jnp.exp(parts[:, 2] - top_s), 0)
+    crossed = jnp.sum(lift_t * (parts[:, 4] + (parts[:, 2] - top_s) * parts[:, 1]), 0) / total_t
+    losses = jnp.log(total_s) - crossed
+    loss_total = jnp.sum(counted * losses)
+    weighting = counted / counted_total / STUDENT_TEMP
+    share_s = weighting * jnp.exp(max_s - top_s) / total_s
+    share_t = weighting * jnp.exp(max_t - top_t) / total_t
+    grad_logits = (expo_s * share_s[:, None] - expo_t * share_t[:, None]).astype(BF16)
+    teacher_sum = jnp.sum(counted[:, None] * teacher_logits, 0)
+    teacher_total = lax.all_gather(teacher_sum, "fsdp", axis=0, tiled=True)
+    grad_proto = dot(grad_logits, student_rows, ((0,), (0,)))
+    grad_rows = jnp.dot(grad_logits, low_proto, preferred_element_type=F32)
+    dp_count = lax.axis_size("dp")
+    grad_rows = grad_rows.reshape(-1, dp_count, cls.shape[0], width)
+    grad_rows = lax.dynamic_index_in_dim(grad_rows, lax.axis_index("dp"), 1, keepdims=False)
+    grad_bottleneck = lax.psum_scatter(grad_rows, "fsdp", scatter_dimension=0, tiled=False)
+
+    model_width, hidden = cls.shape[1], head_full.shape[1]
+    local = cls.shape[0]
+    low_dz = pull_unit(grad_bottleneck)[0].astype(BF16)
+    grad_b = jnp.dot(low_dz, head_full[model_width + hidden :], preferred_element_type=F32)
+    low_db = (grad_b * gelu_slope(pre_b)).astype(BF16)
+    grad_a = dot(low_db, head_full[model_width : model_width + hidden], ((1,), (1,)))
+    low_da = (grad_a * gelu_slope(pre_a)).astype(BF16)
+    grad_n = dot(low_da, head_full[:model_width], ((1,), (1,)))
+    _, pull_norm = jax.vjp(layer_norm, cls, vectors[-2], vectors[-1])
+    grad_cls, grad_gain, grad_shift = pull_norm(grad_n)
+
+    packed = jnp.concatenate([low_n, low_a, low_dz, low_da, low_db, low_b], -1)
+    packed = lax.all_gather(packed, ("fsdp", "dp"), axis=0, tiled=True)
+    total_rows = model_width + hidden + width
+    lefts, rights = packed[:, :total_rows], packed[:, total_rows:]
+    start = lax.axis_index("fsdp") * own_rows
+    left = lax.dynamic_slice_in_dim(lefts, start, own_rows, 1)
+    row = start + lax.broadcasted_iota(jnp.int32, (1, own_rows), 1)
+    kind = jnp.where(row < model_width, 0, jnp.where(row < model_width + hidden, 1, 2))
+    left = jnp.concatenate([jnp.where(kind == index, left, 0) for index in range(3)], 0)
+    right = jnp.concatenate(
+        [rights[:, index * hidden : (index + 1) * hidden] for index in range(3)], 0
+    )
+    grad_head = dot(left, right, ((0,), (0,)))
+    ends = jnp.stack([grad_gain, grad_shift])
+    return grad_cls, ends, loss_total, teacher_total, grad_proto, grad_head
 
 
 def per_device(
@@ -1007,105 +1674,52 @@
     model_width, columns = w_layer.shape[1] * lax.axis_size("fsdp"), w_layer.shape[2]
     pad = packed_width_p(pixels) - pixels
 
-    def low_blocks(patch, layers, weight):
+    def low_blocks(patch, layers):
         patch = jnp.pad(patch, ((0, 0), (0, pad)))
-        return [array.astype(BF16) for array in (patch, layers[0], layers[1], weight)]
-
-    blocks = low_blocks(teacher_patch, teacher_layer, teacher_head)
-    blocks += low_blocks(w_patch, w_layer, w_head)
-    blocks = [blocks[index] for index in (0, 1, 2, 4, 5, 6, 3, 7)]
-    full = gather_all(blocks, (1, 1, 1, 1, 1, 1, 2, 2))
+        return [array.astype(BF16) for array in (patch, layers[0], layers[1])]
+
+    head_s, head_t = w_head.astype(BF16), teacher_head.astype(BF16)
+    blocks = low_blocks(teacher_patch, teacher_layer) + low_blocks(w_patch, w_layer)
+    hidden = w_head.shape[1]
+    fsdp_count = lax.axis_size("fsdp")
+    own_rows, own_k = w_head.shape[0], w_proto.shape[0]
+    total_rows = own_rows * fsdp_count
+    own = own_kernels(local, own_rows, model_width, hidden, total_rows)
+    if own:
+        ranges = ((0, model_width), (model_width + hidden, total_rows))
+        full = gather_rows(blocks, (head_s, head_t), ranges, fsdp_count, 1)
+    else:
+        full = [
+            lax.all_gather(block, "fsdp", axis=0, tiled=True)
+            for block in blocks + [head_s, head_t]
+        ]
     teacher_patch_full, teacher_0, teacher_1, patch_full, layer_0, layer_1 = full[:6]
-    teacher_head_full, head_full = full[6:]
-
-    teacher_cls = forward(
+
+    teacher_rows = forward(
         patches, jnp.zeros_like(covered), teacher_patch_full, teacher_0, teacher_1,
         teacher_vectors, False,
-    )[0][:local]
+    )[0]
     cls_rows, *saved = forward(patches, covered, patch_full, layer_0, layer_1, vectors, True)
-    cls = cls_rows[:local]
-
-    teacher_unit = unit(head_forward(teacher_cls, teacher_head_full, teacher_vectors)[-1])
-    low_n, pre_a, low_a, pre_b, low_b, raw = head_forward(cls, head_full, vectors)
-    bottleneck, pull_unit = jax.vjp(unit, raw)
-    both = jnp.concatenate([teacher_unit.astype(BF16), bottleneck.astype(BF16)], -1)
-    both = lax.all_gather(both, everyone, axis=0, tiled=True)
-    width = raw.shape[1]
-    teacher_rows, student_rows = both[:, :width], both[:, width:]
-
-    owned_k = w_proto.shape[0]
-    low_proto = w_proto.astype(BF16)
-    teacher_logits = dot(teacher_rows, teacher_proto.astype(BF16), ((1,), (1,)))
-    logits = dot(student_rows, low_proto, ((1,), (1,)))
-    own_centre = lax.dynamic_slice_in_dim(centre, fsdp_index * owned_k, owned_k)
-    scaled_t = (teacher_logits - own_centre) / TEACHER_TEMP
-    scaled_s = logits / STUDENT_TEMP
-    max_t = jnp.max(scaled_t, -1)
-    max_s = jnp.max(scaled_s, -1)
-    expo_t = jnp.exp(scaled_t - max_t[:, None])
-    expo_s = jnp.exp(scaled_s - max_s[:, None])
-    parts = jnp.stack(
-        [
-            max_t,
-            jnp.sum(expo_t, -1),
-            max_s,
-            jnp.sum(expo_s, -1),
-            jnp.sum(expo_t * (scaled_s - max_s[:, None]), -1),
-        ]
-    )
-    parts = lax.all_gather(parts, "fsdp", axis=0)
-    top_t = jnp.max(parts[:, 0], 0)
-    lift_t = jnp.exp(parts[:, 0] - top_t)
-    total_t = jnp.sum(parts[:, 1] * lift_t, 0)
-    top_s = jnp.max(parts[:, 2], 0)
-    total_s = jnp.sum(parts[:, 3] * jnp.exp(parts[:, 2] - top_s), 0)
-    crossed = jnp.sum(lift_t * (parts[:, 4] + (parts[:, 2] - top_s) * parts[:, 1]), 0) / total_t
-    losses = jnp.log(total_s) - crossed
-    loss_total = jnp.sum(counted * losses)
-    weighting = counted / counted_total / STUDENT_TEMP
-    share_s = weighting * jnp.exp(max_s - top_s) / total_s
-    share_t = weighting * jnp.exp(max_t - top_t) / total_t
-    grad_logits = (expo_s * share_s[:, None] - expo_t * share_t[:, None]).astype(BF16)
-    teacher_sum = jnp.sum(counted[:, None] * teacher_logits, 0)
-    teacher_total = lax.all_gather(teacher_sum, "fsdp", axis=0, tiled=True)
-    grad_proto = dot(grad_logits, student_rows, ((0,), (0,)))
-    grad_rows = jnp.dot(grad_logits, low_proto, preferred_element_type=F32)
-    dp_count = lax.axis_size("dp")
-    grad_rows = grad_rows.reshape(-1, dp_count, local, width)
-    grad_rows = lax.dynamic_index_in_dim(grad_rows, lax.axis_index("dp"), 1, keepdims=False)
-    grad_bottleneck = lax.psum_scatter(grad_rows, "fsdp", scatter_dimension=0, tiled=False)
-
-    hidden = head_full.shape[1]
-    low_dz = pull_unit(grad_bottleneck)[0].astype(BF16)
-    grad_b = jnp.dot(low_dz, head_full[model_width + hidden :], preferred_element_type=F32)
-    low_db = (grad_b * gelu_slope(pre_b)).astype(BF16)
-    grad_a = dot(low_db, head_full[model_width : model_width + hidden], ((1,), (1,)))
-    low_da = (grad_a * gelu_slope(pre_a)).astype(BF16)
-    grad_n = dot(low_da, head_full[:model_width], ((1,), (1,)))
-    _, pull_norm = jax.vjp(layer_norm, cls, vectors[-2], vectors[-1])
-    grad_cls, grad_gain, grad_shift = pull_norm(grad_n)
-
-    packed = jnp.concatenate([low_n, low_a, low_dz, low_da, low_db, low_b], -1)
-    packed = lax.all_gather(packed, everyone, axis=0, tiled=True)
-    total_rows = model_width + hidden + width
-    lefts, rights = packed[:, :total_rows], packed[:, total_rows:]
-    own_rows = w_head.shape[0]
-    start = fsdp_index * own_rows
-    left = lax.dynamic_slice_in_dim(lefts, start, own_rows, 1)
-    row = start + lax.broadcasted_iota(jnp.int32, (1, own_rows), 1)
-    kind = jnp.where(row < model_width, 0, jnp.where(row < model_width + hidden, 1, 2))
-    left = jnp.concatenate([jnp.where(kind == index, left, 0) for index in range(3)], 0)
-    right = jnp.concatenate(
-        [rights[:, index * hidden : (index + 1) * hidden] for index in range(3)], 0
-    )
-    grad_head = dot(left, right, ((0,), (0,)))
-
-    grad_rows = jnp.pad(grad_cls, ((0, TAIL - local), (0, 0)))
-    ends = jnp.stack([grad_gain, grad_shift])
+    own_centre = lax.dynamic_slice_in_dim(centre, fsdp_index * own_k, own_k)
+    if own:
+        grad_cls, ends, loss_row, totals, grad_logits, unit_rows, grad_head = head_step(
+            cls_rows, teacher_rows, vectors, teacher_vectors, full[6:], (head_s, head_t),
+            own_centre, counted, (w_proto, teacher_proto), (fsdp_count, lax.axis_size("dp")), 3,
+        )
+        ends = ends[:2]
+        loss_total = jnp.sum(loss_row)
+        teacher_total = totals.reshape(-1)
+        grad_proto = dot(grad_logits, unit_rows, ((0,), (0,)))
+    else:
+        grad_cls, ends, loss_total, teacher_total, grad_proto, grad_head = head_plain(
+            cls_rows[:local], teacher_rows[:local], vectors, teacher_vectors, full[6], full[7],
+            own_centre, counted, counted_total, w_proto, teacher_proto, own_rows,
+        )
+    grad_rows = jnp.pad(grad_cls, ((0, TAIL - grad_cls.shape[0]), (0, 0)))
     packed_grads = backward(
         patches, covered, patch_full, layer_0, layer_1, vectors, ends, grad_rows, saved
     )
-    owned = reduce_all(packed_grads)
+    owned = reduce_all(packed_grads, own)
     base = packed_width_p(pixels)
     own_patch = owned[:, :pixels]
     own_layers = jnp.stack(

time: 762 us -> 558 us (0.73)
  blocking collectives: 195 us -> 56.3 us
  matrix products: 49.3 us -> 7.88 us
  between operations: 22 us -> 8.32 us
  other arithmetic: 73.2 us -> 62.3 us
    all_gather x3 -> x0, blocking collectives: 108 us -> none  [the longest x1 46.2 us: per_device(): both = lax.all_gather(both, everyone, axis=0, tiled=True)]
    unnamed x1 -> x0, blocking collectives: 33 us -> none
    dot_general x8 -> x1, matrix products: 31.9 us -> 7.88 us  [dot(): lax.dot_general(left, right, (dims, ((), ())), preferred_element_type=F32)]
    dot_general x5 -> x0, matrix products: 17.3 us -> none  [the longest x2 9.96 us: head_forward(): jnp.dot(low_a, weight[width:width + hidden], preferred_element_type=F32)]
    pallas_call x1 -> x2, Pallas kernels: 210 us -> 208 us  [the longest x1 128 us: gather_rows(): pl.pallas_call(kernel, out_shape=[jax.ShapeDtypeStruct((fsdp_count * r, c...]
  transfers between devices with their start and end apart: 1 -> 0, of which waited for: 0 -> 0; matrix products, arithmetic and copies ran while one was open for 2% -> 0% of each run, Pallas kernels for 17% -> 0%
where the time goes in v3:
time: 558 us; the launch traced here: 551 us
  Pallas kernels  394 us (71%)
  other arithmetic  62.3 us (11%)
  blocking collectives  56.3 us (10%)
  local copies, waits for them, and re-layouts  22.1 us (4%)
  between operations  8.32 us (1%)
  matrix products  7.88 us (1%)
    pallas_call x1, Pallas kernels, gather_rows(): pl.pallas_call(kernel, out_shape=[jax.ShapeDtypeStruct((fsdp_count * r, c...  128 us
    pallas_call x1, Pallas kernels, head_step(): pl.pallas_call(functools.partial(head_kernel, (count, dp_count, rows, chu...  79.8 us
    pallas_call x1, Pallas kernels, reduce_rows(): pl.pallas_call(functools.partial(reduce_kernel, cuts, lines), out_shape=j...  71.3 us
    pallas_call x1, Pallas kernels, backward(): pl.pallas_call(functools.partial(backward_kernel, images, hidden, count),...  60.1 us
    pallas_call x2, Pallas kernels, forward(): pl.pallas_call(functools.partial(forward_kernel, images, hidden, keep), g...  54.8 us
    add x5, other arithmetic, per_device(): TEACHER_KEEP * teachers[group] + (1.0 - TEACHER_KEEP) * updated  45.2 us
    all_gather x1, blocking collectives, per_device(): lax.all_gather(own_rows_grad, 'fsdp', axis=0, tiled=True)[:vectors.shape[0]]  31.6 us
    psum x1, blocking collectives, per_device(): lax.psum(owned_squares + jnp.sum(own_rows_grad * own_rows_grad), 'fsdp')  24.7 us

profile of v3, /device:TPU:0, one launch (start us, length us, event | category | flops | bytes accessed | tf_op | source)
XLA Modules:
  0.0 551.2 jit_solution(15344594172620408478)
XLA Ops:
  0.7 0.0 copy-start.7
  0.7 1.7 convert.17
  2.4 0.3 copy-done.7
  2.7 0.1 convert.19
  2.8 1.2 slice_bitcast_fusion.2
  4.0 1.1 copy-done
  5.1 1.3 convert_element_type.36.refs_6_.shard_s
  6.4 1.3 convert_element_type.37.refs_7_.shard_t
  7.7 0.6 pad.14.refs_0_
  8.3 0.0 copy-done.14
  8.3 0.6 pad.15.refs_3_
  8.9 128.3 %gather_rows.1 = (bf16[384,640]{1,0:T(8,128)(2,1)}, bf16[384,4608]{1,0:T(8,128)(2,1)}, bf16[384,4608]{1,0:T(8,128)(2,1)}, bf16[384,640]{1,0:T(8,128)(2,1)}, bf16...) custom-call(bf16[48,640]{1,0:T(8,128)(2,1)} %pad.14.refs_0_, ...), custom_call_target="tpu_custom_call" | custom-call | tf_op jit(solution)/shard_map/gather_rows/pallas_call | solution.py:285
  137.3 0.8 slice_reduce_fusion.2
  138.1 0.0 copy-start.20
  138.1 1.0 slice.81
  139.2 0.1 pad.30.clone
  139.2 1.0 maximum_maximum_fusion
  140.3 3.9 copy.52.patches
  144.2 1.0 copy.53.covered
  145.2 1.4 slice.84.rows_table
  146.6 28.1 %backbone_forward.2 = (f32[16,384]{1,0:T(8,128)}, f32[4,272,384]{2,1,0:T(8,128)}, f32[4,272,384]{2,1,0:T(8,128)}, f32[4,272,384]{2,1,0:T(8,128)}, bf16[4,272,115...) custom-call(bf16[4,256,588]{2,1,0:T(8,128)(2,1)} %copy.52.patches, ...), custom_call_target="tpu_custom_call" | custom-call | tf_op jit(solution)/shard_map/backbone_forward/pallas_call | solution.py:743
  174.7 0.7 slice.85
  175.4 0.6 slice.89.rows_table
  176.0 0.8 broadcast_in_dim_broadcast_in_dim.3.covered
  176.8 26.8 %backbone_forward.3 = f32[16,384]{1,0:T(8,128)} custom-call(bf16[4,256,588]{2,1,0:T(8,128)(2,1)} %copy.52.patches, f32[4,256,1]{2,1,0:T(8,128)} %broadcast_in_dim_broadcast_in_dim.3.covered, bf16[384,640]{1,0:T(8,128)(2,1)} %get-tuple-element.57.weight_p, bf16[384,4608]{1,0:T(8,128)(2,1)} %get-tuple-element.58.weight_0, ...), custom_call_target="tpu_custom_call" | custom-call | tf_op jit(solution)/shard_map/backbone_forward/pallas_call | solution.py:743
  203.6 0.7 slice.105
  204.3 0.6 pad_maximum_fusion.2.cls
  204.9 0.6 pad_maximum_fusion.1.gains
  205.5 1.4 dynamic_slice.3
  206.9 0.5 convert_bitcast_fusion.1
  207.4 0.7 copy.55.counted_col
  208.2 79.8 %head_step.1 = (f32[8,384]{1,0:T(8,128)}, f32[8,384]{1,0:T(8,128)}, f32[1,128]{1,0:T(1,128)}, f32[8,8,1024]{2,1,0:T(8,128)}, bf16[128,8192]{1,0:T(8,128)(2,1)}, ...) custom-call(f32[8,384]{1,0:T(8,128)} %pad_maximum_fusion.2.cls, f32[16,384]{1,0:T(8,128)} %pad_maximum_fusion.1.gains, ...), custom_call_target="tpu_custom_call" | custom-call | tf_op jit(solution)/shard_map/head_step/pallas_call | solution.py:1448
  288.0 7.9 %multiply_reduce_fusion = (f32[]{:T(128)}, f32[8192,256]{1,0:T(8,128)}) fusion(bf16[128,8192]{1,0:T(8,128)(2,1)} %get-tuple-element.79, bf16[128,256]{1,0:T(8,128)(2,1)} %get-tuple-element.80), kind=kOutput, calls=%fused_computation.5 | convolution fusion | flops 541065216 | bytes 10551300 | tf_op jit(solution)/shard_map/dot_general | solution.py:1503
  295.9 0.7 slice.95
  296.6 0.6 concatenate.19.ends
  297.2 0.6 pad.16.grad_cls
  297.8 60.1 %backbone_backward.1 = bf16[384,10368]{1,0:T(8,128)(2,1)} custom-call(bf16[4,256,588]{2,1,0:T(8,128)(2,1)} %copy.52.patches, f32[4,256,1]{2,1,0:T(8,128)} %copy.53.covered, bf16[384,640]{1,0:T(8,128)(2,1)} %get-tuple-element.53.weight_p, bf16[384,4608]{1,0:T(8,128)(2,1)} %get-tuple-element.54.weight_0, bf16[384,4608]{1,0:T(8,128)(2,1)} %get-tuple-element.55.weight_1, ...), custom_call_target="tpu_custom_call" | custom-call | tf_op jit(solution)/shard_map/backbone_backward/pallas_call | solution.py:954
  358.0 71.3 %reduce_rows.1 = f32[48,10368]{1,0:T(8,128)} custom-call(bf16[4,2,48,10368]{3,2,1,0:T(8,128)(2,1)} %bitcast.25), custom_call_target="tpu_custom_call" | custom-call | tf_op jit(solution)/shard_map/reduce_rows/pallas_call | solution.py:513
  429.2 1.6 slice_bitcast_fusion.1
  430.8 0.0 copy-start.3
  430.8 0.0 copy-start.5
  430.8 0.9 copy-done.3
  431.7 1.1 multiply_reduce_fusion.2
  432.8 1.5 multiply_reduce_fusion.3
  435.6 3.1 multiply_reduce_fusion.1
  440.0 1.5 fusion.10
  442.2 24.7 %psum.7 = f32[]{:T(128)} all-reduce(f32[]{:T(128)S(6)} %add.130), channel_id=1, replica_groups=mesh['fsdp'=8,'dp'=4] {'fsdp'}, use_global_device_ids=true, to_apply=%region_7.8 | all-reduce | flops 1 | bytes 8 | tf_op jit(solution)/shard_map/psum | solution.py:1732
  467.5 31.6 %all_gather.3 = f32[384,384]{1,0:T(8,128)S(1)} all-gather(f32[48,384]{1,0:T(8,128)S(1)} %get-tuple-element.106), channel_id=1, replica_groups=mesh['fsdp'=8,'dp'=4] {'fsdp'}, dimensions={0}, use_global_device_ids=true | all-gather | bytes 663552 | tf_op jit(solution)/shard_map/all_gather | solution.py:1729
  499.2 2.7 multiply_add_fusion.6
  501.9 28.1 %multiply_add_fusion = (f32[8192,256]{1,0:T(8,128)}, f32[8192,256]{1,0:T(8,128)}, f32[8192,256]{1,0:T(8,128)}, f32[8192,256]{1,0:T(8,128)}) fusion(f32[8192,256]{1,0:T(8,128)} %proto_t.1, f32[8192,256]{1,0:T(8,128)} %proto_s.1, f32[8192,256]{1,0:T(8,128)} %get-tuple-element.121, f32[]{:T(128)S(6)} %div.90, f32[8192,256]{1,0:T(8,128)} %param.41, ...), kind=kLoop, calls=%fused_computation.2 | loop fusion | flops 39845888 | bytes 75497472 | tf_op jit(solution)/shard_map/add | solution.py:1757
  530.0 0.0 copy-start.4
  530.0 0.0 copy-start.6
  530.0 0.0 copy-start.8
  530.0 0.0 copy-start.9
  530.0 0.0 copy-start.10
  530.0 0.0 copy-start.11
  530.1 8.5 %multiply_add_fusion.2 = (f32[336,2048]{1,0:T(8,128)}, f32[336,2048]{1,0:T(8,128)}, f32[336,2048]{1,0:T(8,128)}, f32[336,2048]{1,0:T(8,128)}) fusion(f32[336,2048]{1,0:T(8,128)S(1)} %copy-done.2, f32[336,2048]{1,0:T(8,128)S(1)} %copy-done, f32[336,2048]{1,0:T(8,128)} %get-tuple-element.78, f32[]{:T(128)S(6)} %div.90, f32[336,2048]{1,0:T(8,128)} %param.37, ...), kind=kLoop, calls=%fused_computation.8 | loop fusion | flops 13074432 | bytes 24772612 | tf_op jit(solution)/shard_map/add | solution.py:1757
  538.6 0.2 copy-done.10
  538.8 1.1 copy-done.11
  539.8 4.1 multiply_add_fusion.4
  544.0 1.7 multiply_add_fusion.9
  545.7 0.6 convert_reduce_fusion
  547.1 0.7 multiply_add_fusion.8
  547.9 0.6 reduce_sum.63
  (41 shorter events, 0.2 us)
Async XLA Ops:
  0.7 2.0 copy-start.7
  2.7 2.4 copy-start
  4.0 2.4 copy-start.1
  6.4 1.3 copy-start.13
  6.4 1.9 copy-start.14
  7.6 129.6 %copy-start.12 = (f32[274,384]{1,0:T(8,128)S(1)}, f32[274,384]{1,0:T(8,128)}, u32[]{:S(2)}) copy-start(f32[274,384]{1,0:T(8,128)} %param.47) | copy-start | bytes 1262596
  138.1 6.1 %copy-start.20 = (s32[4,256]{1,0:T(4,128)S(1)}, s32[4,256]{1,0:T(4,128)}, u32[]{:S(2)}) copy-start(s32[4,256]{1,0:T(4,128)} %param.25) | copy-start | bytes 12292
  176.8 30.1 %copy-start.21 = (s32[128]{0:T(128)S(1)}, s32[128]{0:T(128)}, u32[]{:S(2)}) copy-start(s32[128]{0:T(128)} %param.26) | copy-start | bytes 1540
  288.0 9.2 %copy-start.19 = (f32[8,384]{1,0:T(8,128)S(1)}, f32[8,384]{1,0:T(8,128)}, u32[]{:S(2)}) copy-start(f32[8,384]{1,0:T(8,128)} %get-tuple-element.66) | copy-start | bytes 36868
  430.8 0.9 copy-start.3
  430.8 2.0 copy-start.5
  501.9 28.1 %copy-start.2 = (f32[336,2048]{1,0:T(8,128)S(1)}, f32[336,2048]{1,0:T(8,128)}, u32[]{:S(2)}) copy-start(f32[336,2048]{1,0:T(8,128)} %param.39) | copy-start | bytes 8257540
  530.0 8.6 %copy-start.4 = (f32[1,48,4608]{2,1,0:T(8,128)S(1)}, f32[1,48,4608]{2,1,0:T(8,128)}, u32[]{:S(2)}) copy-start(f32[1,48,4608]{2,1,0:T(8,128)} %copy-done.3) | copy-start | bytes 2654212
  530.0 8.6 %copy-start.6 = (f32[1,48,4608]{2,1,0:T(8,128)S(1)}, f32[1,48,4608]{2,1,0:T(8,128)}, u32[]{:S(2)}) copy-start(f32[1,48,4608]{2,1,0:T(8,128)} %copy-done.5) | copy-start | bytes 2654212
  530.0 8.6 %copy-start.8 = (f32[2,48,4608]{2,1,0:T(8,128)S(1)}, f32[2,48,4608]{2,1,0:T(8,128)}, u32[]{:S(2)}) copy-start(f32[2,48,4608]{2,1,0:T(8,128)} %param.32) | copy-start | bytes 5308420
  530.0 8.6 %copy-start.9 = (f32[2,48,4608]{2,1,0:T(8,128)S(1)}, f32[2,48,4608]{2,1,0:T(8,128)}, u32[]{:S(2)}) copy-start(f32[2,48,4608]{2,1,0:T(8,128)} %param.35) | copy-start | bytes 5308420
  530.0 8.7 %copy-start.10 = (f32[2,48,4608]{2,1,0:T(8,128)S(1)}, f32[2,48,4608]{2,1,0:T(8,128)}, u32[]{:S(2)}) copy-start(f32[2,48,4608]{2,1,0:T(8,128)} %param.33) | copy-start | bytes 5308420
  530.0 9.8 %copy-start.11 = (f32[2,48,4608]{2,1,0:T(8,128)S(1)}, f32[2,48,4608]{2,1,0:T(8,128)}, u32[]{:S(2)}) copy-start(f32[2,48,4608]{2,1,0:T(8,128)} %param.34) | copy-start | bytes 5308420
  539.8 4.2 copy-start.17
  539.8 4.2 copy-start.18
  539.8 7.2 %copy-start.16 = (f32[8,8,1024]{2,1,0:T(8,128)S(1)}, f32[8,8,1024]{2,1,0:T(8,128)}, u32[]{:S(2)}) copy-start(f32[8,8,1024]{2,1,0:T(8,128)} %get-tuple-element.81) | copy-start | bytes 786436
  539.8 7.3 %copy-start.15 = (f32[65536]{0:T(1024)S(1)}, f32[65536]{0:T(1024)}, u32[]{:S(2)}) copy-start(f32[65536]{0:T(1024)} %param.27) | copy-start | bytes 786436
  544.0 3.9 copy-start.22

commit v4 on v3

--- a/solution.py
+++ b/solution.py
@@ -33,7 +33,7 @@
     return spans
 
 
-def gather_kernel(items, early, lines, sources, heads, targets, send, recv, copied, send_e, recv_e):
+def gather_kernel(items, early, lines, sources, heads, targets, between, send, recv, copied, send_e, recv_e):
     fsdp, dp = lax.axis_index("fsdp"), lax.axis_index("dp")
     z, x = fsdp // 2, fsdp % 2
     y, core = dp // 2, dp % 2
@@ -234,13 +234,14 @@
                 when(y == 1, lambda: to_mate(index, 2).wait_recv())
                 when(y == 1, lambda: to_mate(index, 0, 1).wait_recv())
 
-    def run(part):
-        deal(part, deal_start)
-        steps = lines + 3
-        for tick in range(len(items) + steps - 1):
-            for step in range(steps):
-                if 0 <= tick - step < len(items):
-                    stage(tick - step, part, step)
+    steps = lines + 3
+
+    def run(tick, part):
+        for step in range(steps):
+            if 0 <= tick - step < len(items):
+                stage(tick - step, part, step)
+
+    def close(part):
         for index in range(len(items)):
             for hop in range(lines):
                 z_steps(index, part, hop, lambda copy: copy.wait_send())
@@ -251,10 +252,16 @@
             to_mate(index, part).wait_send()
         deal(part, deal_end)
 
-    roles(run)
-
-
-def gather_rows(arrays, heads, ranges, fsdp_count, collective_id):
+    roles(lambda part: deal(part, deal_start))
+    for tick in range(len(items) + steps - 1):
+        roles(functools.partial(run, tick))
+        between(tick - steps + 1)
+    roles(close)
+
+
+def gather_forward(
+    arrays, heads, ranges, fsdp_count, patches, covered, vecs, teacher_vecs, collective_id
+):
     lines = fsdp_count // 2
     head_rows, head_width = heads[0].shape
     shapes = [array.shape for array in arrays]
@@ -273,37 +280,131 @@
             items.append((len(shapes) - 1, rows, third_ranges(head_width, 0)))
     slots = 4 * (lines - 1) + 4
     extra = len(shapes) - count
-    heads_at = count + len(heads)
+    full = [(fsdp_count * r, c) for r, c in shapes]
+    images, pixel_rows, pixels = patches.shape
+    model, columns = full[1]
+    hidden = (columns - 4 * model) // 2
+    tables = split_table(teacher_vecs, pixel_rows) + split_table(vecs, pixel_rows)
+    per_image = saved_shapes(pixel_rows + TAIL, model)
+    saved = len(per_image)
 
     def kernel(*refs):
-        targets = refs[heads_at : heads_at + len(shapes)]
-        blocks = refs[:count] + refs[heads_at + len(shapes) : heads_at + len(shapes) + extra]
-        rest = refs[heads_at + len(shapes) + extra :]
-        gather_kernel(items, early, lines, blocks, refs[count:heads_at], targets, *rest)
+        refs = list(refs)
+
+        def take(number):
+            taken = refs[:number]
+            del refs[:number]
+            return taken
+
+        sources, head_refs = take(count), take(len(heads))
+        patches_ref, covered_ref = take(2)
+        table_refs = take(4)
+        targets, dealt = take(len(shapes)), take(extra)
+        cls_t, cls_s, x1c_out, o1_out = take(4)
+        saved_out = take(saved)
+        weights, kept = take(6), take(saved)
+        cls_x, cls_o, load_sem, save_sem = take(4)
+
+        def load(number):
+            return pltpu.make_async_copy(targets[number], weights[number], load_sem.at[number])
+
+        def save(number, image):
+            return pltpu.make_async_copy(
+                kept[number].at[image], saved_out[number].at[image], save_sem.at[number, image]
+            )
+
+        def run_image(net, image):
+            places, rows = table_refs[2 * net : 2 * net + 2]
+            values = image_forward(
+                patches_ref[image],
+                covered_ref[image] if net else None,
+                weights[3 * net : 3 * net + 3],
+                places,
+                rows,
+                hidden,
+            )
+            for number in range(saved if net else 0):
+                kept[number][image] = values[number]
+                save(number, image).start()
+            x2, mixture = values[2], values[-1]
+            cls_x[net, image : image + 1, :] = x2[pixel_rows : pixel_rows + 1, :]
+            cls_o[net, image : image + 1, :] = mixture[:1, :].astype(F32)
+
+        def run_class(net):
+            out, x1c, mixed = class_forward(
+                cls_x[net], cls_o[net], weights[3 * net + 2], table_refs[2 * net + 1], hidden
+            )
+            if net:
+                cls_s[...] = out
+                x1c_out[...] = x1c
+                o1_out[...] = mixed
+            else:
+                cls_t[...] = out
+
+        after = {item: [] for item in range(-lines - 3, len(items))}
+        last = len(items) - 1
+        for net in range(2):
+            for image in range(images):
+                at = min(3 * net + 2 + image + (net * max(0, images - 3)), last)
+                after[at].append(functools.partial(run_image, net, image))
+            after[at].append(functools.partial(run_class, net))
+
+        def between(item):
+            if item == -1:
+                cls_x[...] = jnp.zeros_like(cls_x)
+                cls_o[...] = jnp.zeros_like(cls_o)
+            if 0 <= item < 6:
+                load(item).start()
+            if item in (2, 5):
+                for number in range(item - 2, item + 1):
+                    load(number).wait()
+            for work in after[item]:
+                work()
+
+        gather_kernel(
+            items, early, lines, sources + dealt, head_refs, targets, between, *refs
+        )
+        for number in range(saved):
+            for image in range(images):
+                save(number, image).wait()
 
     anywhere = pl.BlockSpec(memory_space=pl.ANY)
+    vmem = pl.BlockSpec(memory_space=pltpu.VMEM)
+    shape = jax.ShapeDtypeStruct
+    sems = pltpu.SemaphoreType.DMA
     out = pl.pallas_call(
         kernel,
-        out_shape=[jax.ShapeDtypeStruct((fsdp_count * r, c), BF16) for r, c in shapes]
-        + [jax.ShapeDtypeStruct(shape, BF16) for shape in shapes[count:]],
-        in_specs=[anywhere] * heads_at,
-        out_specs=[anywhere] * (len(shapes) + extra),
-        scratch_shapes=[
-            pltpu.SemaphoreType.DMA((len(items), slots)),
-            pltpu.SemaphoreType.DMA((len(items), slots)),
-            pltpu.SemaphoreType.DMA((len(items),)),
-            pltpu.SemaphoreType.DMA((len(items), fsdp_count)),
-            pltpu.SemaphoreType.DMA((len(items),)),
+        out_shape=[shape(dims, BF16) for dims in full]
+        + [shape(dims, BF16) for dims in shapes[count:]]
+        + [shape((TAIL, model), kind) for kind in (F32, F32, F32, BF16)]
+        + [shape((images,) + dims, kind) for dims, kind in per_image],
+        in_specs=[anywhere] * (count + len(heads)) + [vmem] * 6,
+        out_specs=[anywhere] * (len(shapes) + extra) + [vmem] * 4 + [anywhere] * saved,
+        scratch_shapes=[pltpu.VMEM(dims, BF16) for dims in full[:6]]
+        + [pltpu.VMEM((images,) + dims, kind) for dims, kind in per_image]
+        + [pltpu.VMEM((2, TAIL, model), F32)] * 2
+        + [
+            sems((6,)),
+            sems((saved, images)),
+            sems((len(items), slots)),
+            sems((len(items), slots)),
+            sems((len(items),)),
+            sems((len(items), fsdp_count)),
+            sems((len(items),)),
         ],
-        compiler_params=pltpu.CompilerParams(collective_id=collective_id, has_side_effects=True),
-        name="gather_rows",
-    )(*arrays, *heads)
-    return out[: len(shapes)]
+        compiler_params=pltpu.CompilerParams(
+            collective_id=collective_id, has_side_effects=True, vmem_limit_bytes=60 << 20
+        ),
+        name="gather_forward",
+    )(*arrays, *heads, patches, covered[..., None], *tables)
+    at = len(shapes) + extra
+    cls_t, cls_s, x1c, o1 = out[at : at + 4]
+    return out[: len(shapes)], cls_t, cls_s, list(out[at + 4 :]) + [x1c, o1]
 
 
 def reduce_kernel(
-    cuts, lines, grads, out, mate_a, mate_b, facing, side, sums, up_out, up_in, down_out, down_in,
-    ending, ended, result, send, recv
+    cuts, lines, places, grads, squares, patch_out, layers_out, vectors_out, norm_out, mate_a, mate_b, facing, side, sums, up_out, up_in, down_out, down_in,
+    ending, ended, result, vectors, norms, send, recv, send_f, recv_f
 ):
     fsdp, dp = lax.axis_index("fsdp"), lax.axis_index("dp")
     z, x = fsdp // 2, fsdp % 2
@@ -321,13 +422,12 @@
     def greet(f, d):
         pl.semaphore_signal(barrier, 1, device_id=(f, d), device_id_type=MESH)
 
-    greet(across, dp)
+    count = 2 * lines
+    for step in range(1, count):
+        greet(lax.rem(fsdp + step, count), dp)
     greet(fsdp, mate)
     greet(fsdp, opposite)
-    pl.when(z + 1 < lines)(lambda: greet(fsdp + 2, dp))
-    pl.when(z > 0)(lambda: greet(fsdp - 2, dp))
-    ends = (z + 1 < lines).astype(jnp.int32) + (z > 0).astype(jnp.int32)
-    pl.semaphore_wait(barrier, 3 + ends)
+    pl.semaphore_wait(barrier, count + 1)
 
     MATE_A, MATE_B, FACING, ACROSS, UP, DOWN, ENDING, LAST_MATE, LAST_SECOND, LAST_FACING = range(10)
 
@@ -484,7 +584,54 @@
             if 0 <= tick - number < cuts:
                 step(tick - number)
 
-    out[...] = result[...].astype(F32)
+    cut_0, cut_1, cut_2, width = places
+    vectors[fsdp] = result[:, cut_2 : cut_2 + width]
+    total = squares[...]
+    for at in range(0, result.shape[1], 128):
+        value = result[:, at : at + 128].astype(F32)
+        value = value * value
+        for row in range(0, value.shape[0], 8):
+            total = total + value[row : row + 8, :]
+    norms[fsdp] = total
+
+    def tell(kind, ref, step):
+        return pltpu.make_async_remote_copy(
+            src_ref=ref.at[fsdp],
+            dst_ref=ref.at[fsdp],
+            send_sem=send_f.at[kind, step - 1],
+            recv_sem=recv_f.at[kind, fsdp],
+            device_id=(lax.rem(fsdp + step, count), dp),
+            device_id_type=MESH,
+        )
+
+    def told(kind, ref, step):
+        peer = lax.rem(fsdp + step, count)
+        return pltpu.make_async_remote_copy(
+            src_ref=ref.at[peer],
+            dst_ref=ref.at[peer],
+            send_sem=send_f.at[kind, step - 1],
+            recv_sem=recv_f.at[kind, peer],
+            device_id=(peer, dp),
+            device_id_type=MESH,
+        )
+
+    for kind, ref in enumerate((norms, vectors)):
+        for step in range(1, count):
+            tell(kind, ref, step).start()
+    patch_out[...] = result[:, :cut_0].astype(F32)
+    layers_out[0] = result[:, cut_0:cut_1].astype(F32)
+    layers_out[1] = result[:, cut_1:cut_2].astype(F32)
+    for kind, ref in enumerate((norms, vectors)):
+        for step in range(1, count):
+            told(kind, ref, step).wait_recv()
+    vectors_out[...] = vectors[...].astype(F32)
+    total = norms[0]
+    for f in range(1, count):
+        total = total + norms[f]
+    norm_out[...] = total
+    for kind, ref in enumerate((norms, vectors)):
+        for step in range(1, count):
+            tell(kind, ref, step).wait_send()
     for cut in range(cuts):
         to_mate_a(cut).wait_send()
         to_across(cut).wait_send()
@@ -505,16 +652,24 @@
             last(cut, LAST_SECOND, 2 - part, mate).wait_send()
 
 
-def reduce_rows(grads, fsdp_count, cuts, collective_id):
+def reduce_rows(grads, squares, places, fsdp_count, cuts, collective_id):
     total, width = grads.shape
     lines, rows = fsdp_count // 2, total // fsdp_count
     size = width // (3 * cuts)
     blocks = (cuts, lines, 2, rows, size)
+    cut_0, cut_1, cut_2, table = places
+    shape = jax.ShapeDtypeStruct
+    sems = pltpu.SemaphoreType.DMA
     return pl.pallas_call(
-        functools.partial(reduce_kernel, cuts, lines),
-        out_shape=jax.ShapeDtypeStruct((rows, width), F32),
-        in_specs=[pl.BlockSpec(memory_space=pltpu.VMEM)],
-        out_specs=pl.BlockSpec(memory_space=pltpu.VMEM),
+        functools.partial(reduce_kernel, cuts, lines, places),
+        out_shape=[
+            shape((rows, cut_0), F32),
+            shape((2, rows, cut_1 - cut_0), F32),
+            shape((fsdp_count, rows, table), F32),
+            shape((8, 128), F32),
+        ],
+        in_specs=[pl.BlockSpec(memory_space=pltpu.VMEM)] * 2,
+        out_specs=[pl.BlockSpec(memory_space=pltpu.VMEM)] * 4,
         scratch_shapes=[
             pltpu.VMEM(blocks, BF16),
             pltpu.VMEM(blocks, BF16),
@@ -526,14 +681,18 @@
         + [pltpu.VMEM((cuts, rows, size), BF16)] * 2
         + [
             pltpu.VMEM((rows, width), BF16),
-            pltpu.SemaphoreType.DMA((cuts, 10)),
-            pltpu.SemaphoreType.DMA((cuts, 10)),
+            pltpu.VMEM((fsdp_count, rows, table), BF16),
+            pltpu.VMEM((fsdp_count, 8, 128), F32),
+            sems((cuts, 10)),
+            sems((cuts, 10)),
+            sems((2, fsdp_count - 1)),
+            sems((2, fsdp_count)),
         ],
         compiler_params=pltpu.CompilerParams(
-            collective_id=collective_id, has_side_effects=True, vmem_limit_bytes=58 << 20
+            collective_id=collective_id, has_side_effects=True, vmem_limit_bytes=32 << 20
         ),
         name="reduce_rows",
-    )(grads.reshape(lines, 2, rows, width))
+    )(grads.reshape(lines, 2, rows, width), squares)
 
 
 GELU_A = 0.7978845608028654
@@ -613,37 +772,24 @@
     return jnp.concatenate(mixed, -1).astype(BF16), lse
 
 
-def forward_kernel(
-    images, hidden, keep, patches, covered, weight_p, weight_0, weight_1, places, rows_table, *rest
-):
-    if keep:
-        (cls_out, x0_out, x1_out, x2_out, qkv_out, o0_out, lse0_out, kv_out, q1_out, lse1_out,
-         x1c_out, o1_out, cls_x, cls_o) = rest
-    else:
-        cls_out, cls_x, cls_o = rest
-    image = pl.program_id(0)
+def image_forward(pixel_rows, hide, weights, places, rows_table, hidden):
+    weight_p, weight_0, weight_1 = weights
     model = weight_0.shape[0]
-    count = patches.shape[1]
+    count, pixels = pixel_rows.shape
     valid = count + 1
     scale = (model // HEADS) ** -0.5
+    keep = hide is not None
 
     def vec(row):
         return rows_table[row : row + 1, :]
 
-    @pl.when(image == 0)
-    def _():
-        cls_x[...] = jnp.zeros_like(cls_x)
-        cls_o[...] = jnp.zeros_like(cls_o)
-
-    tokens = mm_nt(patches[0], weight_p[:, : patches.shape[2]]) + vec(1)
+    def row(layer, index):
+        return vec(2 + 6 * layer + index)
+
+    tokens = mm_nt(pixel_rows, weight_p[:, :pixels]) + vec(1)
     if keep:
-        hide = covered[0]
         tokens = tokens * (1.0 - hide) + vec(0) * hide
     x = jnp.concatenate([tokens + places[:count, :], places[count:, :]], 0)
-
-    def row(layer, index):
-        return vec(2 + 6 * layer + index)
-
     unit_x, _ = norm_parts(x)
     low = (unit_x * row(0, 0) + row(0, 1)).astype(BF16)
     qkv = mm(low, weight_0[:, : 3 * model]).astype(BF16)
@@ -661,30 +807,70 @@
     kv = mm(low, weight_1[:, model : 3 * model]).astype(BF16)
     q1 = mm(low[count:, :], weight_1[:, :model]).astype(BF16)
     mixture1, lse1 = attend(q1, kv[:, :model], kv[:, model:], valid, scale, keep)
-    cls_x[pl.ds(image, 1), :] = x2[count : count + 1, :]
-    cls_o[pl.ds(image, 1), :] = mixture1[:1, :].astype(F32)
+    return x, x1, x2, qkv, mixture, lse, kv, q1, lse1, mixture1
+
+
+def class_forward(cls_x, cls_o, weight_1, rows_table, hidden):
+    model = weight_1.shape[0]
+
+    def row(index):
+        return rows_table[8 + index : 9 + index, :]
+
+    mixed = cls_o.astype(BF16)
+    x1c = cls_x + row(2) * mm(mixed, weight_1[:, 3 * model : 4 * model])
+    unit_c, _ = norm_parts(x1c)
+    low_c = (unit_c * row(3) + row(4)).astype(BF16)
+    wide_c = gelu(mm(low_c, weight_1[:, 4 * model : 4 * model + hidden])).astype(BF16)
+    return x1c + row(5) * mm_nt(wide_c, weight_1[:, 4 * model + hidden :]), x1c, mixed
+
+
+def saved_shapes(total, model):
+    return [
+        ((total, model), F32),
+        ((total, model), F32),
+        ((total, model), F32),
+        ((total, 3 * model), BF16),
+        ((total, model), BF16),
+        ((total, 128), F32),
+        ((total, 2 * model), BF16),
+        ((TAIL, model), BF16),
+        ((TAIL, 128), F32),
+    ]
+
+
+def forward_kernel(
+    images, hidden, keep, patches, covered, weight_p, weight_0, weight_1, places, rows_table, *rest
+):
+    outs, (cls_x, cls_o) = rest[:-2], rest[-2:]
+    image = pl.program_id(0)
+    count = patches.shape[1]
+
+    @pl.when(image == 0)
+    def _():
+        cls_x[...] = jnp.zeros_like(cls_x)
+        cls_o[...] = jnp.zeros_like(cls_o)
+
+    values = image_forward(
+        patches[0],
+        covered[0] if keep else None,
+        (weight_p, weight_0, weight_1),
+        places,
+        rows_table,
+        hidden,
+    )
+    cls_x[pl.ds(image, 1), :] = values[2][count : count + 1, :]
+    cls_o[pl.ds(image, 1), :] = values[-1][:1, :].astype(F32)
     if keep:
-        x0_out[0] = x
-        x1_out[0] = x1
-        x2_out[0] = x2
-        qkv_out[0] = qkv
-        o0_out[0] = mixture
-        lse0_out[0] = lse
-        kv_out[0] = kv
-        q1_out[0] = q1
-        lse1_out[0] = lse1
+        for number, value in enumerate(values[:-1]):
+            outs[1 + number][0] = value
 
     @pl.when(image == images - 1)
     def _():
-        mixed = cls_o[...].astype(BF16)
-        x1c = cls_x[...] + row(1, 2) * mm(mixed, weight_1[:, 3 * model : 4 * model])
-        unit_c, _ = norm_parts(x1c)
-        low_c = (unit_c * row(1, 3) + row(1, 4)).astype(BF16)
-        wide_c = gelu(mm(low_c, weight_1[:, 4 * model : 4 * model + hidden])).astype(BF16)
-        cls_out[...] = x1c + row(1, 5) * mm_nt(wide_c, weight_1[:, 4 * model + hidden :])
+        out, x1c, mixed = class_forward(cls_x[...], cls_o[...], weight_1, rows_table, hidden)
+        outs[0][...] = out
         if keep:
-            x1c_out[...] = x1c
-            o1_out[...] = mixed
+            outs[-2][...] = x1c
+            outs[-1][...] = mixed
 
 
 def fixed(shape):
@@ -725,17 +911,7 @@
     outs = [shape((TAIL, model), F32)]
     out_specs = [whole_out((TAIL, model))]
     if keep:
-        per_image = [
-            ((total, model), F32),
-            ((total, model), F32),
-            ((total, model), F32),
-            ((total, 3 * model), BF16),
-            ((total, model), BF16),
-            ((total, 128), F32),
-            ((total, 2 * model), BF16),
-            ((TAIL, model), BF16),
-            ((TAIL, 128), F32),
-        ]
+        per_image = saved_shapes(total, model)
         outs += [shape((images,) + dims, kind) for dims, kind in per_image]
         out_specs += [each(dims) for dims, kind in per_image]
         outs += [shape((TAIL, model), F32), shape((TAIL, model), BF16)]
@@ -938,7 +1114,7 @@
 
 def packed_width(pixels, columns, model):
     width = packed_width_p(pixels) + 2 * columns + model
-    return (width + 1151) // 1152 * 1152
+    return (width + 3455) // 3456 * 3456
 
 
 def backward(patches, covered, weight_p, weight_0, weight_1, vecs, ends, grad_cls, saved):
@@ -1012,7 +1188,7 @@
 def head_kernel(
     sizes, cls, gains, first_s, first_t, third_s, third_t, shard_s, shard_t, centre, counted_row,
     counted_col, proto_s, proto_t,
-    grad_cls, ends, loss_row, totals, grad_logits, unit_rows, grad_head,
+    grad_cls, ends, loss_row, totals, grad_logits, unit_rows, grad_head, squares,
     table_s, table_t, loading, wide_s, wide_t, kept, left, acts, parts_out, parts_in, units,
     stats, pulls, pulled, backs, pieces, pieced, extra_1, extra_3, lefts, rights, tall,
     send, recv, send_z, recv_z, send_x, recv_x, send_d, recv_d,
@@ -1188,7 +1364,8 @@
             device_id_type=MESH,
         ).wait_recv()
     all_units = from_halves(units[...])
-    rows_s = student_rows(all_units).astype(BF16)
+    all_units_s = student_rows(all_units)
+    rows_s = all_units_s.astype(BF16)
     rows_t = student_rows(all_units, 4).astype(BF16)
     unit_rows[...] = rows_s
 
@@ -1268,10 +1445,21 @@
     turned = jnp.concatenate([share_s, share_t, jnp.zeros((126, images), F32)], 0).T
     share_s, share_t = turned[:, 0:1], turned[:, 1:2]
 
+    turned_rows = all_units_s.T.astype(BF16)
+    squares[...] = jnp.zeros_like(squares)
+
+    def add_squares(value):
+        total = squares[...]
+        for row in range(0, value.shape[0], 8):
+            strip = value[row : row + 8, :]
+            total = total + lanes(jnp.add, strip * strip)
+        squares[...] = total
+
     def grad_pass(index, total):
         at = pl.ds(pl.multiple_of(index * chunk, chunk), chunk)
         low = (wide_s[:, at] * share_s - wide_t[:, at] * share_t).astype(BF16)
         grad_logits[:, at] = low
+        add_squares(mm(turned_rows, low))
         return total + mm(low, table_s[at, :].astype(BF16))
 
     partial = lax.fori_loop(0, chunks, grad_pass, jnp.zeros((images, width), F32))
@@ -1403,6 +1591,12 @@
             group_end(1 + number, right_at(number))
 
     grad_head[...] = tall[pl.ds(place, rows), :]
+
+    def square_pass(index, carry):
+        add_squares(grad_head[pl.ds(pl.multiple_of(index * 16, 16), 16), :])
+        return carry
+
+    lax.fori_loop(0, rows // 16, square_pass, 0)
     group_end(0, left_at)
     arrive(TOTALS, totals)
     end(ACTS, lambda peer: acts.at[fsdp], acts)
@@ -1455,9 +1649,10 @@
             shape((images, owned_k), BF16),
             shape((images, width), BF16),
             shape((rows, hidden), F32),
+            shape((8, 128), F32),
         ],
         in_specs=[vmem] * 11 + [anywhere] * 2,
-        out_specs=[vmem] * 7,
+        out_specs=[vmem] * 8,
         scratch_shapes=[
             pltpu.VMEM((owned_k, width), F32),
             pltpu.VMEM((owned_k, width), F32),
@@ -1550,13 +1745,6 @@
     return True
 
 
-def reduce_all(grads, own):
-    if own:
-        return reduce_rows(grads, lax.axis_size("fsdp"), 3, 2)
-    owned = lax.psum_scatter(grads, "fsdp", scatter_dimension=0, tiled=True)
-    return lax.psum(owned, "dp").astype(F32)
-
-
 def head_plain(
     cls, teacher_cls, vectors, teacher_vectors, head_full, teacher_head_full, own_centre, counted,
     counted_total, w_proto, teacher_proto, own_rows,
@@ -1687,22 +1875,23 @@
     own = own_kernels(local, own_rows, model_width, hidden, total_rows)
     if own:
         ranges = ((0, model_width), (model_width + hidden, total_rows))
-        full = gather_rows(blocks, (head_s, head_t), ranges, fsdp_count, 1)
+        full, teacher_rows, cls_rows, saved = gather_forward(
+            blocks, (head_s, head_t), ranges, fsdp_count, patches, covered, vectors,
+            teacher_vectors, 1,
+        )
     else:
         full = [
             lax.all_gather(block, "fsdp", axis=0, tiled=True)
             for block in blocks + [head_s, head_t]
         ]
-    teacher_patch_full, teacher_0, teacher_1, patch_full, layer_0, layer_1 = full[:6]
-
-    teacher_rows = forward(
-        patches, jnp.zeros_like(covered), teacher_patch_full, teacher_0, teacher_1,
-        teacher_vectors, False,
-    )[0]
-    cls_rows, *saved = forward(patches, covered, patch_full, layer_0, layer_1, vectors, True)
+        teacher_rows = forward(
+            patches, jnp.zeros_like(covered), *full[:3], teacher_vectors, False
+        )[0]
+        cls_rows, *saved = forward(patches, covered, *full[3:6], vectors, True)
+    patch_full, layer_0, layer_1 = full[3:6]
     own_centre = lax.dynamic_slice_in_dim(centre, fsdp_index * own_k, own_k)
     if own:
-        grad_cls, ends, loss_row, totals, grad_logits, unit_rows, grad_head = head_step(
+        grad_cls, ends, loss_row, totals, grad_logits, unit_rows, grad_head, part = head_step(
             cls_rows, teacher_rows, vectors, teacher_vectors, full[6:], (head_s, head_t),
             own_centre, counted, (w_proto, teacher_proto), (fsdp_count, lax.axis_size("dp")), 3,
         )
@@ -1719,17 +1908,27 @@
     packed_grads = backward(
         patches, covered, patch_full, layer_0, layer_1, vectors, ends, grad_rows, saved
     )
-    owned = reduce_all(packed_grads, own)
-    base = packed_width_p(pixels)
-    own_patch = owned[:, :pixels]
-    own_layers = jnp.stack(
-        [owned[:, base : base + columns], owned[:, base + columns : base + 2 * columns]]
-    )
-    own_rows_grad = owned[:, base + 2 * columns : base + 2 * columns + model_width]
-    vector_grad = lax.all_gather(own_rows_grad, "fsdp", axis=0, tiled=True)[: vectors.shape[0]]
+    cut_0 = packed_width_p(pixels)
+    cut_1, cut_2 = cut_0 + columns, cut_0 + 2 * columns
+    if own:
+        places = (cut_0, cut_1, cut_2, model_width)
+        own_patch, own_layers, table, sums = reduce_rows(
+            packed_grads, part, places, fsdp_count, 9, 2
+        )
+        vector_grad = table.reshape(model_width, model_width)[: vectors.shape[0]]
+        own_patch = own_patch[:, :pixels]
+        squares = jnp.sum(sums)
+    else:
+        owned = lax.psum_scatter(packed_grads, "fsdp", scatter_dimension=0, tiled=True)
+        owned = lax.psum(owned, "dp").astype(F32)
+        own_patch = owned[:, :pixels]
+        own_layers = jnp.stack([owned[:, cut_0:cut_1], owned[:, cut_1:cut_2]])
+        own_table = owned[:, cut_2 : cut_2 + model_width]
+        table = lax.all_gather(own_table, "fsdp", axis=0, tiled=True)
+        vector_grad = table[: vectors.shape[0]]
+        parts = (own_patch, own_layers, grad_head, grad_proto, own_table)
+        squares = lax.psum(sum(jnp.sum(value * value) for value in parts), "fsdp")
     owned_grads = (own_patch, own_layers, grad_head, grad_proto)
-    owned_squares = sum((jnp.sum(gradient * gradient) for gradient in owned_grads))
-    squares = lax.psum(owned_squares + jnp.sum(own_rows_grad * own_rows_grad), "fsdp")
     norm_value = jnp.sqrt(squares)
     factor = CLIP_NORM / jnp.maximum(norm_value, CLIP_NORM)
     updated_centre = CENTRE_KEEP * centre + (1.0 - CENTRE_KEEP) * teacher_total / counted_total

time: 558 us -> 443 us (0.79)
  blocking collectives: 56.3 us -> 0 us
  Pallas kernels: 394 us -> 358 us
  other arithmetic: 62.3 us -> 29.2 us
  matrix products: 7.88 us -> 22.9 us
    pallas_call x4 -> x2, Pallas kernels: 254 us -> 218 us  [the longest x1 151 us: gather_forward(): pl.pallas_call(kernel, out_shape=[shape(dims, BF16) for dims in full] + [...]
    all_gather x1 -> x0, blocking collectives: 31.6 us -> none  [per_device(): lax.all_gather(own_rows_grad, 'fsdp', axis=0, tiled=True)[:vectors.shape[0]]]
    add x5 -> x4, other arithmetic: 45.2 us -> 16.2 us  [per_device(): TEACHER_KEEP * teachers[group] + (1.0 - TEACHER_KEEP) * updated]
    psum x1 -> x0, blocking collectives: 24.7 us -> none  [per_device(): lax.psum(owned_squares + jnp.sum(own_rows_grad * own_rows_grad), 'fsdp')]
    dot_general x1, matrix products: 7.88 us -> 22.9 us  [dot(): lax.dot_general(left, right, (dims, ((), ())), preferred_element_type=F32)]
where the time goes in v4:
time: 443 us; the launch traced here: 434 us
  Pallas kernels  358 us (81%)
  other arithmetic  29.2 us (7%)
  matrix products  22.9 us (5%)
  local copies, waits for them, and re-layouts  19.6 us (4%)
  between operations  4.72 us (1%)
    pallas_call x1, Pallas kernels, gather_forward(): pl.pallas_call(kernel, out_shape=[shape(dims, BF16) for dims in full] + [...  151 us
    pallas_call x1, Pallas kernels, head_step(): pl.pallas_call(functools.partial(head_kernel, (count, dp_count, rows, chu...  79 us
    pallas_call x1, Pallas kernels, reduce_rows(): pl.pallas_call(functools.partial(reduce_kernel, cuts, lines, places), out...  67.8 us
    pallas_call x1, Pallas kernels, backward(): pl.pallas_call(functools.partial(backward_kernel, images, hidden, count),...  60.3 us
    dot_general x1, matrix products, dot(): lax.dot_general(left, right, (dims, ((), ())), preferred_element_type=F32)  22.9 us
    add x4, other arithmetic, per_device(): TEACHER_KEEP * teachers[group] + (1.0 - TEACHER_KEEP) * updated  16.2 us

profile of v4, /device:TPU:0, one launch (start us, length us, event | category | flops | bytes accessed | tf_op | source)
XLA Modules:
  0.0 434.2 jit_solution(10507035294302460617)
XLA Ops:
  0.7 0.0 copy-start.6
  0.7 1.0 convert.16
  1.7 0.6 pad.14.refs_0_
  2.3 1.6 convert.19
  3.9 0.0 copy-done.6
  3.9 0.0 copy-start.15
  3.9 0.0 copy-start.2
  3.9 0.1 convert.17
  4.0 1.2 slice_bitcast_fusion
  5.3 0.0 copy-done.15
  5.3 0.6 pad.15.refs_3_
  5.9 0.5 copy-done.2
  6.4 1.3 convert_element_type.35.refs_6_.shard_s
  7.7 0.0 copy-done.4
  7.7 0.0 copy-start.12
  7.7 1.3 convert_element_type.36.refs_7_.shard_t
  9.0 0.3 copy-done.13
  9.3 2.3 copy.51.refs_8_.patches
  11.6 0.0 copy-done.19
  11.6 1.0 copy.52.refs_9_.covered
  12.7 0.0 copy-done.11
  12.7 0.0 copy-done.12
  12.7 0.1 pad.28.clone
  12.8 1.0 maximum_maximum_fusion.1
  13.9 0.6 slice.75.refs_11_
  14.5 0.6 slice.79.refs_13_.rows_table
  15.1 150.6 %gather_forward.1 = (bf16[384,640]{1,0:T(8,128)(2,1)}, bf16[384,4608]{1,0:T(8,128)(2,1)}, bf16[384,4608]{1,0:T(8,128)(2,1)}, bf16[384,640]{1,0:T(8,128)(2,1)}, b...) custom-call(bf16[48,640]{1,0:T(8,128)(2,1)} %pad.14.refs_0_, ...), custom_call_target="tpu_custom_call" | custom-call | tf_op jit(solution)/shard_map/gather_forward/pallas_call | solution.py:375
  165.7 0.7 slice.81
  166.4 0.7 slice.80
  167.1 0.6 pad_maximum_fusion.1.cls
  167.8 0.6 pad_maximum_fusion.gains
  168.4 1.4 dynamic_slice.3
  169.7 0.0 copy-done.20
  169.8 0.5 convert_bitcast_fusion.1
  170.3 0.7 copy.53.counted_col
  171.0 79.0 %head_step.1 = (f32[8,384]{1,0:T(8,128)}, f32[8,384]{1,0:T(8,128)}, f32[1,128]{1,0:T(1,128)}, f32[8,8,1024]{2,1,0:T(8,128)}, bf16[128,8192]{1,0:T(8,128)(2,1)}, ...) custom-call(f32[8,384]{1,0:T(8,128)} %pad_maximum_fusion.1.cls, f32[16,384]{1,0:T(8,128)} %pad_maximum_fusion.gains, ...), custom_call_target="tpu_custom_call" | custom-call | tf_op jit(solution)/shard_map/head_step/pallas_call | solution.py:1642
  250.0 1.2 reduce_sum.27
  251.2 0.6 convert_reduce_fusion
  252.4 0.7 slice.86
  253.2 0.6 concatenate.19.ends
  253.8 1.3 pad.16.grad_cls
  255.1 60.3 %backbone_backward.1 = bf16[384,10368]{1,0:T(8,128)(2,1)} custom-call(bf16[4,256,588]{2,1,0:T(8,128)(2,1)} %copy.51.refs_8_.patches, f32[4,256,1]{2,1,0:T(8,128)} %copy.52.refs_9_.covered, bf16[384,640]{1,0:T(8,128)(2,1)} %get-tuple-element.63.weight_p, bf16[384,4608]{1,0:T(8,128)(2,1)} %get-tuple-element.64.weight_0, ...), custom_call_target="tpu_custom_call" | custom-call | tf_op jit(solution)/shard_map/backbone_backward/pallas_call | solution.py:1130
  315.4 0.0 copy-done.1
  315.4 0.0 copy-start
  315.4 3.3 copy-done
  318.7 67.8 %reduce_rows.1 = (f32[48,640]{1,0:T(8,128)S(1)}, f32[2,48,4608]{2,1,0:T(8,128)S(1)}, f32[8,48,384]{2,1,0:T(8,128)S(1)}, f32[8,128]{1,0:T(8,128)S(1)}) custom-call(bf16[4,2,48,10368]{3,2,1,0:T(8,128)(2,1)S(1)} %bitcast.22, f32[8,128]{1,0:T(8,128)S(1)} %copy-done.1), custom_call_target="tpu_custom_call" | custom-call | tf_op jit(solution)/shard_map/reduce_rows/pallas_call | solution.py:663
  386.5 0.6 reduce_sum.29
  387.8 1.0 divide_bitcast_fusion
  388.8 1.7 multiply_add_fusion.8
  390.6 0.0 copy-done.14
  390.6 1.9 multiply_add_fusion.9
  392.4 0.0 copy-start.8
  392.5 0.0 copy-start.9
  392.5 7.6 %multiply_add_fusion.4 = (f32[2,48,4608]{2,1,0:T(8,128)}, f32[2,48,4608]{2,1,0:T(8,128)}, f32[2,48,4608]{2,1,0:T(8,128)}, f32[2,48,4608]{2,1,0:T(8,128)}) fusion(f32[2,48,4608]{2,1,0:T(8,128)} %param.35, f32[2,48,4608]{2,1,0:T(8,128)} %param.32, f32[2,48,4608]{2,1,0:T(8,128)S(1)} %get-tuple-element.83, f32[]{:T(128)S(6)} %div.90, f32[2,48,4608]{2,1,0:T(8,128)} %param.33, ...), kind=kLoop, calls=%fused_computation.13 | loop fusion | flops 8404992 | bytes 15925252 | tf_op jit(solution)/shard_map/add | solution.py:1956
  400.1 0.0 copy-done.3
  400.1 0.0 copy-done.7
  400.1 1.2 copy-done.8
  401.3 0.8 copy-done.9
  402.1 5.3 %multiply_add_fusion.2 = (f32[336,2048]{1,0:T(8,128)}, f32[336,2048]{1,0:T(8,128)}, f32[336,2048]{1,0:T(8,128)}, f32[336,2048]{1,0:T(8,128)}) fusion(f32[336,2048]{1,0:T(8,128)S(1)} %copy-done.5, f32[336,2048]{1,0:T(8,128)S(1)} %copy-done.3, f32[336,2048]{1,0:T(8,128)S(1)} %copy-done.9, f32[]{:T(128)S(6)} %div.90, f32[336,2048]{1,0:T(8,128)S(1)} %copy-done.7, ...), kind=kLoop, calls=%fused_computation.8 | loop fusion | flops 13074432 | bytes 24772612 | tf_op jit(solution)/shard_map/add | solution.py:1956
  407.3 0.0 copy-done.18
  407.4 0.0 copy-start.17
  407.4 22.9 %multiply_add_fusion = (f32[8192,256]{1,0:T(8,128)}, f32[8192,256]{1,0:T(8,128)}, f32[8192,256]{1,0:T(8,128)}, f32[8192,256]{1,0:T(8,128)}) fusion(f32[8192,256]{1,0:T(8,128)} %proto_t.1, f32[8192,256]{1,0:T(8,128)} %proto_s.1, f32[8192,256]{1,0:T(8,128)} %param.41, f32[8192,256]{1,0:T(8,128)} %param.42, f32[]{:T(128)S(6)} %div.90, ...), kind=kOutput, calls=%fused_computation.3 | convolution fusion | flops 576716800 | bytes 69271552 | tf_op jit(solution)/shard_map/dot_general | solution.py:1698
  430.3 0.0 copy-done.16
  430.3 1.4 multiply_add_fusion.6
  (27 shorter events, 0.2 us)
Async XLA Ops:
  0.7 3.3 copy-start.6
  3.9 1.4 copy-start.15
  3.9 2.5 copy-start.2
  5.3 2.4 copy-start.4
  7.7 1.6 copy-start.13
  7.7 3.9 copy-start.19
  7.7 4.9 %copy-start.11 = (f32[274,384]{1,0:T(8,128)S(1)}, f32[274,384]{1,0:T(8,128)}, u32[]{:S(2)}) copy-start(f32[274,384]{1,0:T(8,128)} %param.47) | copy-start | bytes 1262596
  7.7 4.9 %copy-start.12 = (f32[274,384]{1,0:T(8,128)S(1)}, f32[274,384]{1,0:T(8,128)}, u32[]{:S(2)}) copy-start(f32[274,384]{1,0:T(8,128)} %param.44) | copy-start | bytes 1262596
  15.1 154.7 %copy-start.20 = (s32[128]{0:T(128)S(1)}, s32[128]{0:T(128)}, u32[]{:S(2)}) copy-start(s32[128]{0:T(128)} %param.26) | copy-start | bytes 1540
  255.1 60.3 %copy-start.1 = (f32[8,128]{1,0:T(8,128)S(1)}, f32[8,128]{1,0:T(8,128)}, u32[]{:S(2)}) copy-start(f32[8,128]{1,0:T(8,128)} %get-tuple-element.79.squares) | copy-start | bytes 12292
  315.4 3.3 copy-start
  318.7 71.9 %copy-start.14 = (f32[48,588]{1,0:T(8,128)S(1)}, f32[48,588]{1,0:T(8,128)}, u32[]{:S(2)}) copy-start(f32[48,588]{1,0:T(8,128)} %param.31) | copy-start | bytes 338692
  392.4 7.6 %copy-start.3 = (f32[336,2048]{1,0:T(8,128)S(1)}, f32[336,2048]{1,0:T(8,128)}, u32[]{:S(2)}) copy-start(f32[336,2048]{1,0:T(8,128)} %param.36) | copy-start | bytes 8257540
  392.4 7.6 %copy-start.5 = (f32[336,2048]{1,0:T(8,128)S(1)}, f32[336,2048]{1,0:T(8,128)}, u32[]{:S(2)}) copy-start(f32[336,2048]{1,0:T(8,128)} %param.39) | copy-start | bytes 8257540
  392.4 7.6 %copy-start.7 = (f32[336,2048]{1,0:T(8,128)S(1)}, f32[336,2048]{1,0:T(8,128)}, u32[]{:S(2)}) copy-start(f32[336,2048]{1,0:T(8,128)} %param.37) | copy-start | bytes 8257540
  392.4 8.8 %copy-start.8 = (f32[336,2048]{1,0:T(8,128)S(1)}, f32[336,2048]{1,0:T(8,128)}, u32[]{:S(2)}) copy-start(f32[336,2048]{1,0:T(8,128)} %param.38) | copy-start | bytes 8257540
  392.5 9.6 %copy-start.9 = (f32[336,2048]{1,0:T(8,128)S(1)}, f32[336,2048]{1,0:T(8,128)}, u32[]{:S(2)}) copy-start(f32[336,2048]{1,0:T(8,128)} %get-tuple-element.84) | copy-start | bytes 8257540
  402.1 5.3 %copy-start.10 = (bf16[128,8192]{1,0:T(8,128)(2,1)S(1)}, bf16[128,8192]{1,0:T(8,128)(2,1)}, u32[]{:S(2)}) copy-start(bf16[128,8192]{1,0:T(8,128)(2,1)} %get-tuple-element.85) | copy-start | bytes 6291460
  402.1 5.3 %copy-start.18 = (bf16[128,256]{1,0:T(8,128)(2,1)S(1)}, bf16[128,256]{1,0:T(8,128)(2,1)}, u32[]{:S(2)}) copy-start(bf16[128,256]{1,0:T(8,128)(2,1)} %get-tuple-element.86) | copy-start | bytes 196612
  407.3 23.0 %copy-start.16 = (f32[274,384]{1,0:T(8,128)S(1)}, f32[274,384]{1,0:T(8,128)}, u32[]{:S(2)}) copy-start(f32[274,384]{1,0:T(8,128)} %param.45) | copy-start | bytes 1262596
  407.4 22.9 %copy-start.17 = (f32[274,384]{1,0:T(8,128)S(1)}, f32[274,384]{1,0:T(8,128)}, u32[]{:S(2)}) copy-start(f32[274,384]{1,0:T(8,128)} %param.46) | copy-start | bytes 1262596

commit v5 on v4

--- a/solution.py
+++ b/solution.py
@@ -265,9 +265,15 @@
     lines = fsdp_count // 2
     head_rows, head_width = heads[0].shape
     shapes = [array.shape for array in arrays]
-    items = [(number, shape[0], third_ranges(shape[1], 0)) for number, shape in enumerate(shapes)]
+    count = len(arrays)
+    items, whole_at = [], {}
+    for number in (0, 1, 3, 4, 2, 5):
+        rows, width = shapes[number]
+        cuts = 2 if width % 256 == 0 and width > 1024 else 1
+        for cut in range(cuts):
+            items.append((number, rows, third_ranges(width // cuts, cut * (width // cuts))))
+        whole_at[number] = len(items) - 1
     early = {}
-    count = len(arrays)
     for low, high in ranges:
         for number in range(len(heads)):
             rows = (high - low) // fsdp_count
@@ -303,7 +309,7 @@
         cls_t, cls_s, x1c_out, o1_out = take(4)
         saved_out = take(saved)
         weights, kept = take(6), take(saved)
-        cls_x, cls_o, load_sem, save_sem = take(4)
+        cls_x, cls_o, teacher_x, load_sem, save_sem = take(5)
 
         def load(number):
             return pltpu.make_async_copy(targets[number], weights[number], load_sem.at[number])
@@ -313,24 +319,44 @@
                 kept[number].at[image], saved_out[number].at[image], save_sem.at[number, image]
             )
 
-        def run_image(net, image):
-            places, rows = table_refs[2 * net : 2 * net + 2]
-            values = image_forward(
+        def keep_values(first, image, values):
+            for number, value in enumerate(values):
+                kept[first + number][image] = value
+                save(first + number, image).start()
+
+        def run_first(net, image):
+            if image == 0:
+                load(3 * net).wait()
+                load(3 * net + 1).wait()
+            values = image_first(
                 patches_ref[image],
                 covered_ref[image] if net else None,
-                weights[3 * net : 3 * net + 3],
-                places,
-                rows,
+                weights[3 * net],
+                weights[3 * net + 1],
+                table_refs[2 * net],
+                table_refs[2 * net + 1],
                 hidden,
             )
-            for number in range(saved if net else 0):
-                kept[number][image] = values[number]
-                save(number, image).start()
-            x2, mixture = values[2], values[-1]
+            x2 = values[2]
+            if net:
+                keep_values(0, image, values)
+            else:
+                teacher_x[image] = x2
             cls_x[net, image : image + 1, :] = x2[pixel_rows : pixel_rows + 1, :]
-            cls_o[net, image : image + 1, :] = mixture[:1, :].astype(F32)
-
-        def run_class(net):
+
+        def run_second(net):
+            load(3 * net + 2).wait()
+            for image in range(images):
+                values = image_second(
+                    kept[2][image] if net else teacher_x[image],
+                    weights[3 * net + 2],
+                    table_refs[2 * net + 1],
+                    pixel_rows,
+                    net == 1,
+                )
+                if net:
+                    keep_values(6, image, values[:-1])
+                cls_o[net, image : image + 1, :] = values[-1][:1, :].astype(F32)
             out, x1c, mixed = class_forward(
                 cls_x[net], cls_o[net], weights[3 * net + 2], table_refs[2 * net + 1], hidden
             )
@@ -341,25 +367,27 @@
             else:
                 cls_t[...] = out
 
-        after = {item: [] for item in range(-lines - 3, len(items))}
-        last = len(items) - 1
-        for net in range(2):
-            for image in range(images):
-                at = min(3 * net + 2 + image + (net * max(0, images - 3)), last)
-                after[at].append(functools.partial(run_image, net, image))
-            after[at].append(functools.partial(run_class, net))
+        waiting = [
+            (whole_at[3 * net + 1] + 1, functools.partial(run_first, net, image))
+            for net in range(2)
+            for image in range(images)
+        ]
+        waiting += [
+            (whole_at[3 * net + 2] + 1, functools.partial(run_second, net)) for net in range(2)
+        ]
 
         def between(item):
             if item == -1:
                 cls_x[...] = jnp.zeros_like(cls_x)
                 cls_o[...] = jnp.zeros_like(cls_o)
-            if 0 <= item < 6:
-                load(item).start()
-            if item in (2, 5):
-                for number in range(item - 2, item + 1):
-                    load(number).wait()
-            for work in after[item]:
-                work()
+            if waiting and waiting[0][0] <= item:
+                waiting.pop(0)[1]()
+            for number in range(6):
+                if whole_at[number] == item:
+                    load(number).start()
+            if item == len(items) - 1:
+                while waiting:
+                    waiting.pop(0)[1]()
 
         gather_kernel(
             items, early, lines, sources + dealt, head_refs, targets, between, *refs
@@ -384,6 +412,7 @@
         + [pltpu.VMEM((images,) + dims, kind) for dims, kind in per_image]
         + [pltpu.VMEM((2, TAIL, model), F32)] * 2
         + [
+            pltpu.VMEM((images, pixel_rows + TAIL, model), F32),
             sems((6,)),
             sems((saved, images)),
             sems((len(items), slots)),
@@ -403,9 +432,11 @@
 
 
 def reduce_kernel(
-    cuts, lines, places, grads, squares, patch_out, layers_out, vectors_out, norm_out, mate_a, mate_b, facing, side, sums, up_out, up_in, down_out, down_in,
-    ending, ended, result, vectors, norms, send, recv, send_f, recv_f
+    cuts, lines, places, part_of, squares, outs, work, mate_a, mate_b, facing, side,
+    spread, landed, halves, result, vectors, norms, send, recv, send_z, recv_z, send_l, recv_l,
+    send_f, recv_f
 ):
+    patch_out, layers_out, vectors_out, norm_out = outs
     fsdp, dp = lax.axis_index("fsdp"), lax.axis_index("dp")
     z, x = fsdp // 2, fsdp % 2
     y, core = dp // 2, dp % 2
@@ -425,11 +456,11 @@
     count = 2 * lines
     for step in range(1, count):
         greet(lax.rem(fsdp + step, count), dp)
-    greet(fsdp, mate)
-    greet(fsdp, opposite)
-    pl.semaphore_wait(barrier, count + 1)
-
-    MATE_A, MATE_B, FACING, ACROSS, UP, DOWN, ENDING, LAST_MATE, LAST_SECOND, LAST_FACING = range(10)
+    for step in range(1, 4):
+        greet(fsdp, lax.rem(dp + step, 4))
+    pl.semaphore_wait(barrier, count + 2)
+
+    MATE_A, MATE_B, FACING, ACROSS = range(4)
 
     def move(cut, slot, source, target, f, d):
         return pltpu.make_async_remote_copy(
@@ -445,14 +476,14 @@
         return pl.ds(pl.multiple_of((3 * cut + which) * size, 128), size)
 
     def mine(cut, which):
-        return grads[:, :, :, columns(cut, which)].astype(F32)
+        return part_of(cut, which, size)[...].astype(F32)
 
     def to_mate_a(cut):
-        return move(cut, MATE_A, grads.at[:, :, :, columns(cut, mate_part)], mate_a.at[cut], fsdp, mate)
+        return move(cut, MATE_A, part_of(cut, mate_part, size), mate_a.at[cut], fsdp, mate)
 
     def to_mate_b(cut):
         return move(
-            cut, MATE_B, grads.at[:, :, :, columns(cut, 2 - mate_part)], mate_b.at[cut], fsdp, mate
+            cut, MATE_B, part_of(cut, 2 - mate_part, size), mate_b.at[cut], fsdp, mate
         )
 
     def to_facing(cut):
@@ -461,20 +492,31 @@
     def to_across(cut):
         return move(cut, ACROSS, mate_a.at[cut, :, 1 - x], side.at[cut], across, dp)
 
-    def going_up(cut, count):
-        blocks = pl.ds(0, count)
-        return move(cut, UP, up_out.at[cut, blocks], up_in.at[cut, blocks], fsdp + 2, dp)
-
-    def going_down(cut, count):
-        blocks = pl.ds(0, count)
-        return move(cut, DOWN, down_out.at[cut, blocks], down_in.at[cut, blocks], fsdp - 2, dp)
-
-    def to_ending(cut):
-        return move(cut, ENDING, ending.at[cut], ended.at[cut], fsdp, opposite)
-
-    def last(cut, slot, which, d):
-        place = result.at[:, columns(cut, which)]
-        return move(cut, slot, place, place, fsdp, d)
+    def along(cut, to, source):
+        return pltpu.make_async_remote_copy(
+            src_ref=spread.at[cut, to],
+            dst_ref=landed.at[cut, source],
+            send_sem=send_z.at[cut, to],
+            recv_sem=recv_z.at[cut, source],
+            device_id=(2 * to + x, dp),
+            device_id_type=MESH,
+        )
+
+    def share_of(cut, group):
+        if group % 2:
+            return halves.at[cut, group // 2]
+        return result.at[:, columns(cut, group)]
+
+    def hand(cut, group, to):
+        place = share_of(cut, group)
+        return pltpu.make_async_remote_copy(
+            src_ref=place,
+            dst_ref=place,
+            send_sem=send_l.at[cut, to],
+            recv_sem=recv_l.at[cut, group],
+            device_id=(fsdp, to),
+            device_id_type=MESH,
+        )
 
     def step_0(cut):
         to_mate_a(cut).start()
@@ -504,88 +546,50 @@
 
     def step_3(cut):
         to_across(cut).wait_recv()
-        sums[cut] = mate_a[cut, :, x].astype(F32) + side[cut].astype(F32)
-
-    def lift(cut, hop):
-        at = hop - 1
-
-        @pl.when(z == at)
-        def _():
-            count = lines - hop
-            if at > 0:
-                going_up(cut, count + 1).wait_recv()
-            for ahead in range(1, count + 1):
-                value = sums[cut, at + ahead]
-                if at > 0:
-                    value = value + up_in[cut, ahead].astype(F32)
-                up_out[cut, ahead - 1] = value.astype(BF16)
-            going_up(cut, count).start()
-
-        low = lines - hop
-
-        @pl.when(z == low)
-        def _():
-            count = lines - hop
-            if low < lines - 1:
-                going_down(cut, count + 1).wait_recv()
-            for ahead in range(1, count + 1):
-                value = sums[cut, low - ahead]
-                if low < lines - 1:
-                    value = value + down_in[cut, ahead].astype(F32)
-                down_out[cut, ahead - 1] = value.astype(BF16)
-            going_down(cut, count).start()
-
-    def finish(cut):
-        for at in range(lines):
-
-            @pl.when(z == at)
-            def _(at=at):
-                value = sums[cut, at]
-                if at == lines - 1:
-                    going_up(cut, 1).wait_recv()
-                if at == 0:
-                    going_down(cut, 1).wait_recv()
-                if at > 0:
-                    value = value + up_in[cut, 0].astype(F32)
-                if at < lines - 1:
-                    value = value + down_in[cut, 0].astype(F32)
-                ending[cut] = value.astype(BF16)
-
-        pl.when(lone)(lambda: to_ending(cut).start())
-
-        @pl.when(jnp.logical_not(lone))
-        def _():
-            result[:, columns(cut, part)] = ending[cut]
-            last(cut, LAST_FACING, part, opposite).start()
-            last(cut, LAST_MATE, part, mate).start()
-
-    def share(cut):
-        @pl.when(lone)
-        def _():
-            to_ending(cut).wait_recv()
-            both = ending[cut].astype(F32) + ended[cut].astype(F32)
-            result[:, columns(cut, part)] = both.astype(BF16)
-            last(cut, LAST_MATE, part, mate).start()
-
-        @pl.when(jnp.logical_not(lone))
-        def _():
-            last(cut, LAST_FACING, 2 - part, opposite).wait_recv()
-            last(cut, LAST_SECOND, 2 - part, mate).start()
-
-    def close(cut):
-        last(cut, LAST_MATE, mate_part, mate).wait_recv()
-        pl.when(lone)(lambda: last(cut, LAST_SECOND, 2 - mate_part, mate).wait_recv())
-
-    steps = [step_0, step_1, step_2, step_3]
-    steps += [functools.partial(lambda hop, cut: lift(cut, hop), hop) for hop in range(1, lines)]
-    steps += [finish, share, close]
-    for tick in range(cuts + len(steps) - 1):
-        for number, step in enumerate(steps):
-            if 0 <= tick - number < cuts:
-                step(tick - number)
-
-    cut_0, cut_1, cut_2, width = places
-    vectors[fsdp] = result[:, cut_2 : cut_2 + width]
+        total = mate_a[cut, :, x].astype(F32) + side[cut].astype(F32)
+        spread[cut] = total.astype(BF16)
+        landed[cut, z] = spread[cut, z]
+        for to in range(lines):
+            pl.when(z != to)(lambda to=to: along(cut, to, z).start())
+
+    def step_4(cut):
+        for source in range(lines):
+            pl.when(z != source)(lambda source=source: along(cut, source, source).wait_recv())
+        total = landed[cut, 0].astype(F32)
+        for source in range(1, lines):
+            total = total + landed[cut, source].astype(F32)
+        total = total.astype(BF16)
+        for group in range(4):
+
+            @pl.when(dp == group)
+            def _(group=group):
+                share_of(cut, group)[...] = total
+                for to in range(4):
+                    if to != group:
+                        hand(cut, group, to).start()
+
+    def step_5(cut):
+        for group in range(4):
+            pl.when(dp != group)(lambda group=group: hand(cut, group, group).wait_recv())
+        both = halves[cut, 0].astype(F32) + halves[cut, 1].astype(F32)
+        result[:, columns(cut, 1)] = both.astype(BF16)
+
+    steps = [step_0, step_1, step_2, step_3, step_4, step_5]
+    due, done, tick = [], [], 0
+    while len(due) < cuts or min(done) < len(steps):
+        ready, pause = work(tick)
+        if len(due) < ready:
+            due.append(tick)
+            done.append(0)
+        for cut in reversed(range(len(due))):
+            if done[cut] < len(steps) and due[cut] <= tick:
+                steps[done[cut]](cut)
+                done[cut] += 1
+                due[cut] = tick + pause
+        tick += 1
+
+    patch_at, patch_width, table_at, width, layer_spans = places
+    vectors[fsdp] = result[:, table_at : table_at + width]
     total = squares[...]
     for at in range(0, result.shape[1], 128):
         value = result[:, at : at + 128].astype(F32)
@@ -618,9 +622,9 @@
     for kind, ref in enumerate((norms, vectors)):
         for step in range(1, count):
             tell(kind, ref, step).start()
-    patch_out[...] = result[:, :cut_0].astype(F32)
-    layers_out[0] = result[:, cut_0:cut_1].astype(F32)
-    layers_out[1] = result[:, cut_1:cut_2].astype(F32)
+    patch_out[...] = result[:, patch_at : patch_at + patch_width].astype(F32)
+    for layer, to, start, span in layer_spans:
+        layers_out[layer, :, to : to + span] = result[:, start : start + span].astype(F32)
     for kind, ref in enumerate((norms, vectors)):
         for step in range(1, count):
             told(kind, ref, step).wait_recv()
@@ -635,64 +639,18 @@
     for cut in range(cuts):
         to_mate_a(cut).wait_send()
         to_across(cut).wait_send()
-        for hop in range(1, lines):
-            pl.when(z == hop - 1)(lambda hop=hop: going_up(cut, lines - hop).wait_send())
-            pl.when(z == lines - hop)(lambda hop=hop: going_down(cut, lines - hop).wait_send())
-        last(cut, LAST_MATE, part, mate).wait_send()
-
-        @pl.when(lone)
-        def _():
-            to_mate_b(cut).wait_send()
-            to_ending(cut).wait_send()
-
-        @pl.when(jnp.logical_not(lone))
-        def _():
-            to_facing(cut).wait_send()
-            last(cut, LAST_FACING, part, opposite).wait_send()
-            last(cut, LAST_SECOND, 2 - part, mate).wait_send()
-
-
-def reduce_rows(grads, squares, places, fsdp_count, cuts, collective_id):
-    total, width = grads.shape
-    lines, rows = fsdp_count // 2, total // fsdp_count
-    size = width // (3 * cuts)
-    blocks = (cuts, lines, 2, rows, size)
-    cut_0, cut_1, cut_2, table = places
-    shape = jax.ShapeDtypeStruct
-    sems = pltpu.SemaphoreType.DMA
-    return pl.pallas_call(
-        functools.partial(reduce_kernel, cuts, lines, places),
-        out_shape=[
-            shape((rows, cut_0), F32),
-            shape((2, rows, cut_1 - cut_0), F32),
-            shape((fsdp_count, rows, table), F32),
-            shape((8, 128), F32),
-        ],
-        in_specs=[pl.BlockSpec(memory_space=pltpu.VMEM)] * 2,
-        out_specs=[pl.BlockSpec(memory_space=pltpu.VMEM)] * 4,
-        scratch_shapes=[
-            pltpu.VMEM(blocks, BF16),
-            pltpu.VMEM(blocks, BF16),
-            pltpu.VMEM(blocks, BF16),
-            pltpu.VMEM((cuts, lines, rows, size), BF16),
-            pltpu.VMEM((cuts, lines, rows, size), F32),
-        ]
-        + [pltpu.VMEM((cuts, lines - 1, rows, size), BF16)] * 4
-        + [pltpu.VMEM((cuts, rows, size), BF16)] * 2
-        + [
-            pltpu.VMEM((rows, width), BF16),
-            pltpu.VMEM((fsdp_count, rows, table), BF16),
-            pltpu.VMEM((fsdp_count, 8, 128), F32),
-            sems((cuts, 10)),
-            sems((cuts, 10)),
-            sems((2, fsdp_count - 1)),
-            sems((2, fsdp_count)),
-        ],
-        compiler_params=pltpu.CompilerParams(
-            collective_id=collective_id, has_side_effects=True, vmem_limit_bytes=32 << 20
-        ),
-        name="reduce_rows",
-    )(grads.reshape(lines, 2, rows, width), squares)
+        for to in range(lines):
+            pl.when(z != to)(lambda to=to: along(cut, to, z).wait_send())
+        for group in range(4):
+
+            @pl.when(dp == group)
+            def _(group=group):
+                for to in range(4):
+                    if to != group:
+                        hand(cut, group, to).wait_send()
+
+        pl.when(lone)(lambda: to_mate_b(cut).wait_send())
+        pl.when(jnp.logical_not(lone))(lambda: to_facing(cut).wait_send())
 
 
 GELU_A = 0.7978845608028654
@@ -772,42 +730,42 @@
     return jnp.concatenate(mixed, -1).astype(BF16), lse
 
 
-def image_forward(pixel_rows, hide, weights, places, rows_table, hidden):
-    weight_p, weight_0, weight_1 = weights
+def image_first(pixel_rows, hide, weight_p, weight_0, places, rows_table, hidden):
     model = weight_0.shape[0]
     count, pixels = pixel_rows.shape
-    valid = count + 1
     scale = (model // HEADS) ** -0.5
     keep = hide is not None
 
     def vec(row):
         return rows_table[row : row + 1, :]
-
-    def row(layer, index):
-        return vec(2 + 6 * layer + index)
 
     tokens = mm_nt(pixel_rows, weight_p[:, :pixels]) + vec(1)
     if keep:
         tokens = tokens * (1.0 - hide) + vec(0) * hide
     x = jnp.concatenate([tokens + places[:count, :], places[count:, :]], 0)
     unit_x, _ = norm_parts(x)
-    low = (unit_x * row(0, 0) + row(0, 1)).astype(BF16)
+    low = (unit_x * vec(2) + vec(3)).astype(BF16)
     qkv = mm(low, weight_0[:, : 3 * model]).astype(BF16)
     mixture, lse = attend(
-        qkv[:, :model], qkv[:, model : 2 * model], qkv[:, 2 * model :], valid, scale, keep
+        qkv[:, :model], qkv[:, model : 2 * model], qkv[:, 2 * model :], count + 1, scale, keep
     )
-    x1 = x + row(0, 2) * mm(mixture, weight_0[:, 3 * model : 4 * model])
+    x1 = x + vec(4) * mm(mixture, weight_0[:, 3 * model : 4 * model])
     unit_x, _ = norm_parts(x1)
-    low = (unit_x * row(0, 3) + row(0, 4)).astype(BF16)
+    low = (unit_x * vec(5) + vec(6)).astype(BF16)
     wide = gelu(mm(low, weight_0[:, 4 * model : 4 * model + hidden])).astype(BF16)
-    x2 = x1 + row(0, 5) * mm_nt(wide, weight_0[:, 4 * model + hidden :])
-
+    x2 = x1 + vec(7) * mm_nt(wide, weight_0[:, 4 * model + hidden :])
+    return x, x1, x2, qkv, mixture, lse
+
+
+def image_second(x2, weight_1, rows_table, count, keep):
+    model = weight_1.shape[0]
+    scale = (model // HEADS) ** -0.5
     unit_x, _ = norm_parts(x2)
-    low = (unit_x * row(1, 0) + row(1, 1)).astype(BF16)
+    low = (unit_x * rows_table[8:9, :] + rows_table[9:10, :]).astype(BF16)
     kv = mm(low, weight_1[:, model : 3 * model]).astype(BF16)
     q1 = mm(low[count:, :], weight_1[:, :model]).astype(BF16)
-    mixture1, lse1 = attend(q1, kv[:, :model], kv[:, model:], valid, scale, keep)
-    return x, x1, x2, qkv, mixture, lse, kv, q1, lse1, mixture1
+    mixture1, lse1 = attend(q1, kv[:, :model], kv[:, model:], count + 1, scale, keep)
+    return kv, q1, lse1, mixture1
 
 
 def class_forward(cls_x, cls_o, weight_1, rows_table, hidden):
@@ -850,14 +808,9 @@
         cls_x[...] = jnp.zeros_like(cls_x)
         cls_o[...] = jnp.zeros_like(cls_o)
 
-    values = image_forward(
-        patches[0],
-        covered[0] if keep else None,
-        (weight_p, weight_0, weight_1),
-        places,
-        rows_table,
-        hidden,
-    )
+    hide = covered[0] if keep else None
+    values = image_first(patches[0], hide, weight_p, weight_0, places, rows_table, hidden)
+    values += image_second(values[2], weight_1, rows_table, count, keep)
     cls_x[pl.ds(image, 1), :] = values[2][count : count + 1, :]
     cls_o[pl.ds(image, 1), :] = values[-1][:1, :].astype(F32)
     if keep:
@@ -966,197 +919,368 @@
     return [jnp.concatenate(part, -1).astype(BF16) for part in (grad_q, grad_k, grad_v)]
 
 
-def backward_kernel(
-    images, hidden, count_, patches, covered, weight_p, weight_0, weight_1, rows_table, ends, grad_cls,
-    x0_in, x1_in, x2_in, qkv_in, o0_in, lse0_in, kv_in, q1_in, lse1_in, x1c_in, o1_in,
-    packed, acc_p, acc_0, acc_kv, acc_q, grad_c, grad_oc, places, rows
+def last_back_kernel(
+    images, hidden, weight_1, rows_table, grad_cls, x2_in, kv_in, q1_in, lse1_in, x1c_in, o1_in,
+    packed, grad_out, rows, acc_kv, acc_q, grad_c, grad_oc
 ):
     image = pl.program_id(0)
-    model = weight_0.shape[0]
-    count, pixels = patches.shape[1], patches.shape[2]
+    model = weight_1.shape[0]
+    count = x2_in.shape[1] - TAIL
     valid = count + 1
     scale = (model // HEADS) ** -0.5
-    base_0 = packed_width_p(pixels)
-    columns = weight_0.shape[1]
-    base_1 = base_0 + columns
-    base_v = base_1 + columns
     cut_o, cut_u, cut_d = 3 * model, 4 * model, 4 * model + hidden
 
-    def row(layer, index):
-        at = 2 + 6 * layer + index
-        return rows_table[at : at + 1, :]
-
-    def add_row(layer, index, value):
-        at = 2 + 6 * layer + index
-        rows[at : at + 1, :] += value
+    def row(index):
+        return rows_table[8 + index : 9 + index, :]
+
+    def add_row(index, value):
+        rows[8 + index : 9 + index, :] += value
 
     @pl.when(image == 0)
     def _():
-        for ref in (acc_p, acc_0, acc_kv, acc_q, places, rows):
+        for ref in (acc_kv, acc_q, rows):
             ref[...] = jnp.zeros_like(ref)
         grad_x = grad_cls[...]
         x1c = x1c_in[...]
         unit_x, lift = norm_parts(x1c)
-        low = (unit_x * row(1, 3) + row(1, 4)).astype(BF16)
+        low = (unit_x * row(3) + row(4)).astype(BF16)
         wide, slope = gelu_both(mm(low, weight_1[:, cut_u:cut_d]))
         wide = wide.astype(BF16)
         down = mm_nt(wide, weight_1[:, cut_d:])
-        add_row(1, 5, column_sum(grad_x * down))
-        grad_d = (grad_x * row(1, 5)).astype(BF16)
+        add_row(5, column_sum(grad_x * down))
+        grad_d = (grad_x * row(5)).astype(BF16)
         grad_u = (mm(grad_d, weight_1[:, cut_d:]) * slope).astype(BF16)
-        packed[:, base_1 + cut_d : base_v] = mm_tn(grad_d, wide).astype(BF16)
-        packed[:, base_1 + cut_u : base_1 + cut_d] = mm_tn(low, grad_u).astype(BF16)
+        packed[:, cut_d:] = mm_tn(grad_d, wide).astype(BF16)
+        packed[:, cut_u:cut_d] = mm_tn(low, grad_u).astype(BF16)
         grad_n = mm_nt(grad_u, weight_1[:, cut_u:cut_d])
-        add_row(1, 3, column_sum(grad_n * unit_x))
-        add_row(1, 4, column_sum(grad_n))
-        grad_x = grad_x + norm_back(grad_n, row(1, 3), unit_x, lift)
+        add_row(3, column_sum(grad_n * unit_x))
+        add_row(4, column_sum(grad_n))
+        grad_x = grad_x + norm_back(grad_n, row(3), unit_x, lift)
         mixed = o1_in[...]
-        add_row(1, 2, column_sum(grad_x * mm(mixed, weight_1[:, cut_o:cut_u])))
-        grad_a = (grad_x * row(1, 2)).astype(BF16)
-        packed[:, base_1 + cut_o : base_1 + cut_u] = mm_tn(mixed, grad_a).astype(BF16)
+        add_row(2, column_sum(grad_x * mm(mixed, weight_1[:, cut_o:cut_u])))
+        grad_a = (grad_x * row(2)).astype(BF16)
+        packed[:, cut_o:cut_u] = mm_tn(mixed, grad_a).astype(BF16)
         grad_c[...] = grad_x
         grad_oc[...] = mm_nt(grad_a, weight_1[:, cut_o:cut_u])
 
     first_row = lax.broadcasted_iota(jnp.int32, (TAIL, 1), 0) == 0
-
     grad_o1 = jnp.where(first_row, grad_oc[pl.ds(image, 1), :], 0.0).astype(BF16)
     kv = kv_in[0]
     grad_q, grad_k, grad_v = attend_back(
         grad_o1, q1_in[0], kv[:, :model], kv[:, model:], lse1_in[0], valid, scale
     )
     unit_x, lift = norm_parts(x2_in[0])
-    low = (unit_x * row(1, 0) + row(1, 1)).astype(BF16)
+    low = (unit_x * row(0) + row(1)).astype(BF16)
     grad_kv = jnp.concatenate([grad_k, grad_v], -1)
     acc_kv[...] += mm_tn(low, grad_kv)
     acc_q[...] += mm_tn(low[count:, :], grad_q)
     grad_n = mm_nt(grad_kv, weight_1[:, model : 3 * model])
     tail = grad_n[count:, :] + mm_nt(grad_q, weight_1[:, :model])
     grad_n = jnp.concatenate([grad_n[:count, :], tail], 0)
-    add_row(1, 0, column_sum(grad_n * unit_x))
-    add_row(1, 1, column_sum(grad_n))
-    grad_x = norm_back(grad_n, row(1, 0), unit_x, lift)
+    add_row(0, column_sum(grad_n * unit_x))
+    add_row(1, column_sum(grad_n))
+    grad_x = norm_back(grad_n, row(0), unit_x, lift)
     tail = grad_x[count:, :] + jnp.where(first_row, grad_c[pl.ds(image, 1), :], 0.0)
-    grad_x = jnp.concatenate([grad_x[:count, :], tail], 0)
-
-    unit_x, lift = norm_parts(x1_in[0])
-    low = (unit_x * row(0, 3) + row(0, 4)).astype(BF16)
-    wide, slope = gelu_both(mm(low, weight_0[:, cut_u:cut_d]))
-    wide = wide.astype(BF16)
-    down = mm_nt(wide, weight_0[:, cut_d:])
-    add_row(0, 5, column_sum(grad_x * down))
-    grad_d = (grad_x * row(0, 5)).astype(BF16)
-    grad_u = (mm(grad_d, weight_0[:, cut_d:]) * slope).astype(BF16)
-    acc_0[:, cut_d:] += mm_tn(grad_d, wide)
-    acc_0[:, cut_u:cut_d] += mm_tn(low, grad_u)
-    grad_n = mm_nt(grad_u, weight_0[:, cut_u:cut_d])
-    add_row(0, 3, column_sum(grad_n * unit_x))
-    add_row(0, 4, column_sum(grad_n))
-    grad_x = grad_x + norm_back(grad_n, row(0, 3), unit_x, lift)
-    mixed = o0_in[0]
-    add_row(0, 2, column_sum(grad_x * mm(mixed, weight_0[:, cut_o:cut_u])))
-    grad_a = (grad_x * row(0, 2)).astype(BF16)
-    acc_0[:, cut_o:cut_u] += mm_tn(mixed, grad_a)
-    grad_o = mm_nt(grad_a, weight_0[:, cut_o:cut_u]).astype(BF16)
-    qkv = qkv_in[0]
-    grad_qkv = jnp.concatenate(
-        attend_back(
-            grad_o, qkv[:, :model], qkv[:, model : 2 * model], qkv[:, 2 * model :], lse0_in[0],
-            valid, scale,
-        ),
-        -1,
-    )
-    unit_x, lift = norm_parts(x0_in[0])
-    low = (unit_x * row(0, 0) + row(0, 1)).astype(BF16)
-    acc_0[:, :cut_o] += mm_tn(low, grad_qkv)
-    grad_n = mm_nt(grad_qkv, weight_0[:, :cut_o])
-    add_row(0, 0, column_sum(grad_n * unit_x))
-    add_row(0, 1, column_sum(grad_n))
-    grad_x = grad_x + norm_back(grad_n, row(0, 0), unit_x, lift)
-
-    places[...] += grad_x
-    hide = covered[0]
-    token = grad_x[:count, :]
-    rows[0:1, :] += column_sum(token * hide)
-    token = token * (1.0 - hide)
-    rows[1:2, :] += column_sum(token)
-    acc_p[...] += mm_tn(token.astype(BF16), patches[0])
+    grad_out[0] = jnp.concatenate([grad_x[:count, :], tail], 0)
 
     @pl.when(image == images - 1)
     def _():
-        packed[:, :base_0] = jnp.concatenate(
-            [acc_p[...], jnp.zeros((model, base_0 - pixels), F32)], -1
-        ).astype(BF16)
-        packed[:, base_0:base_1] = acc_0[...].astype(BF16)
-        packed[:, base_1 : base_1 + model] = acc_q[...].astype(BF16)
-        packed[:, base_1 + model : base_1 + cut_o] = acc_kv[...].astype(BF16)
-        used = rows_table.shape[0]
-        table = jnp.concatenate(
-            [
-                places[count : count + 1, :],
-                places[:count, :],
-                places[count : count + 1, :],
-                rows[...] + ends[...],
-            ],
-            0,
-        )
-        table = jnp.concatenate(
-            [table, jnp.zeros((model - table.shape[0], model), F32)], 0
-        )
-        packed[:, base_v : base_v + model] = table.astype(BF16)
-        spare = packed.shape[1] - base_v - model
-        if spare:
-            packed[:, base_v + model :] = jnp.zeros((model, spare), BF16)
-
-
-def packed_width_p(pixels):
-    return (pixels + 127) // 128 * 128
-
-
-def packed_width(pixels, columns, model):
-    width = packed_width_p(pixels) + 2 * columns + model
-    return (width + 3455) // 3456 * 3456
-
-
-def backward(patches, covered, weight_p, weight_0, weight_1, vecs, ends, grad_cls, saved):
-    images, count, pixels = patches.shape
-    model, columns = weight_0.shape
+        packed[:, :model] = acc_q[...].astype(BF16)
+        packed[:, model:cut_o] = acc_kv[...].astype(BF16)
+
+
+def last_back(weight_1, rows, grad_cls, saved):
+    x2, kv, q1, lse1, x1c, o1 = [saved[index] for index in (2, 6, 7, 8, 9, 10)]
+    images = x2.shape[0]
+    model, columns = weight_1.shape
     hidden = (columns - 4 * model) // 2
-    total = count + TAIL
-    _, rows = split_table(vecs, count)
-    ends = jnp.concatenate(
-        [jnp.zeros((14, model), F32), ends, jnp.zeros((rows.shape[0] - 16, model), F32)]
-    )
-    width = packed_width(pixels, columns, model)
+    shape = jax.ShapeDtypeStruct
     return pl.pallas_call(
-        functools.partial(backward_kernel, images, hidden, count),
+        functools.partial(last_back_kernel, images, hidden),
         grid=(images,),
-        out_shape=jax.ShapeDtypeStruct((model, width), BF16),
-        in_specs=[
-            each((count, pixels)),
-            each((count, 1)),
-            fixed(weight_p.shape),
-            fixed(weight_0.shape),
-            fixed(weight_1.shape),
-            fixed(rows.shape),
-            fixed(ends.shape),
-            fixed(grad_cls.shape),
-        ]
-        + [each(array.shape[1:]) for array in saved[:9]]
-        + [fixed(array.shape) for array in saved[9:]],
-        out_specs=whole_out((model, width)),
+        out_shape=[shape(weight_1.shape, BF16), shape(x2.shape, F32), shape(rows.shape, F32)],
+        in_specs=[fixed(weight_1.shape), fixed(rows.shape), fixed(grad_cls.shape)]
+        + [each(array.shape[1:]) for array in (x2, kv, q1, lse1)]
+        + [fixed(x1c.shape), fixed(o1.shape)],
+        out_specs=[whole_out(weight_1.shape), each(x2.shape[1:]), whole_out(rows.shape)],
         scratch_shapes=[
-            pltpu.VMEM((model, pixels), F32),
-            pltpu.VMEM((model, columns), F32),
             pltpu.VMEM((model, 2 * model), F32),
             pltpu.VMEM((model, model), F32),
             pltpu.VMEM((TAIL, model), F32),
             pltpu.VMEM((TAIL, model), F32),
-            pltpu.VMEM((total, model), F32),
-            pltpu.VMEM(rows.shape, F32),
         ],
+        compiler_params=pltpu.CompilerParams(vmem_limit_bytes=48 << 20),
+        name="last_layer_backward",
+    )(weight_1, rows, grad_cls, x2, kv, q1, lse1, x1c, o1)
+
+
+def first_back(refs, image, hidden, work, rows, store_mlp, store_mix, store_rest):
+    patches, covered, weight_0, rows_table, grad_in, x0_in, x1_in, qkv_in, o0_in, lse0_in = refs
+    model = weight_0.shape[0]
+    images, count, pixels = patches.shape
+    valid = count + 1
+    scale = (model // HEADS) ** -0.5
+    cut_o, cut_u, cut_d = 3 * model, 4 * model, 4 * model + hidden
+    acc, acc_p, grad_s, grad_t, places = work
+
+    def row(index):
+        return rows_table[2 + index : 3 + index, :]
+
+    def add_row(index, value):
+        rows[2 + index : 3 + index, :] += value
+
+    def add(ref, at, value):
+        span = slice(at, at + value.shape[1])
+        if image == 0:
+            ref[:, span] = value
+        else:
+            ref[:, span] += value
+
+    def mlp():
+        grad_x = grad_in[image]
+        unit_x, lift = norm_parts(x1_in[image])
+        low = (unit_x * row(3) + row(4)).astype(BF16)
+        wide, slope = gelu_both(mm(low, weight_0[:, cut_u:cut_d]))
+        wide = wide.astype(BF16)
+        down = mm_nt(wide, weight_0[:, cut_d:])
+        add_row(5, column_sum(grad_x * down))
+        grad_d = (grad_x * row(5)).astype(BF16)
+        grad_u = (mm(grad_d, weight_0[:, cut_d:]) * slope).astype(BF16)
+        add(acc, 0, mm_tn(low, grad_u))
+        add(acc, hidden, mm_tn(grad_d, wide))
+        grad_n = mm_nt(grad_u, weight_0[:, cut_u:cut_d])
+        add_row(3, column_sum(grad_n * unit_x))
+        add_row(4, column_sum(grad_n))
+        grad_s[image] = grad_x + norm_back(grad_n, row(3), unit_x, lift)
+        if image == images - 1:
+            store_mlp()
+
+    def attention():
+        grad_x = grad_s[image]
+        mixed = o0_in[image]
+        add_row(2, column_sum(grad_x * mm(mixed, weight_0[:, cut_o:cut_u])))
+        grad_a = (grad_x * row(2)).astype(BF16)
+        add(acc, cut_o, mm_tn(mixed, grad_a))
+        grad_o = mm_nt(grad_a, weight_0[:, cut_o:cut_u]).astype(BF16)
+        qkv = qkv_in[image]
+        grad_qkv = attend_back(
+            grad_o, qkv[:, :model], qkv[:, model : 2 * model], qkv[:, 2 * model :],
+            lse0_in[image], valid, scale,
+        )
+        grad_qkv = jnp.concatenate(grad_qkv, -1)
+        grad_t[image] = grad_qkv
+        unit_x, _ = norm_parts(x0_in[image])
+        low = (unit_x * row(0) + row(1)).astype(BF16)
+        add(acc, 0, mm_tn(low, grad_qkv))
+        if image == images - 1:
+            store_mix()
+
+    def rest():
+        grad_qkv = grad_t[image]
+        unit_x, lift = norm_parts(x0_in[image])
+        grad_n = mm_nt(grad_qkv, weight_0[:, :cut_o])
+        add_row(0, column_sum(grad_n * unit_x))
+        add_row(1, column_sum(grad_n))
+        grad_x = grad_s[image] + norm_back(grad_n, row(0), unit_x, lift)
+        places[...] += grad_x
+        hide = covered[image]
+        token = grad_x[:count, :]
+        rows[0:1, :] += column_sum(token * hide)
+        token = token * (1.0 - hide)
+        rows[1:2, :] += column_sum(token)
+        add(acc_p, 0, mm_tn(token.astype(BF16), patches[image]))
+        if image == images - 1:
+            store_rest()
+
+    return mlp, attention, rest
+
+
+def table_of(places, rows, count, total):
+    table = jnp.concatenate(
+        [places[count : count + 1, :], places[:count, :], places[count : count + 1, :], rows[...]],
+        0,
+    )
+    return jnp.concatenate(
+        [table, jnp.zeros((total - table.shape[0], table.shape[1]), F32)], 0
+    )
+
+
+def plan_of(pixels, columns, model, size):
+    hidden = (columns - 4 * model) // 2
+    patch_width = packed_width_p(pixels)
+    patch_at = 2 * columns
+    table_at = patch_at + patch_width
+    width = (table_at + model + 3 * size - 1) // (3 * size) * 3 * size
+    spans = (
+        (1, 0, 0, columns),
+        (0, 0, columns + 2 * hidden, 4 * model),
+        (0, 4 * model, columns, 2 * hidden),
+    )
+    return (patch_at, patch_width, table_at, model, spans), width
+
+
+def first_back_kernel(images, hidden, *refs):
+    ins, (rows_in, tail, *work, rows) = refs[:10], refs[10:]
+    start_sums(work[-1], rows, rows_in)
+    run = back_pieces(ins, images, hidden, work, rows, tail, lambda value: value.astype(BF16))
+    for piece, _ in run:
+        piece()
+
+
+def back_pieces(ins, images, hidden, work, rows, tail, shaped):
+    acc, acc_p, _, _, places = work
+    model = acc.shape[0]
+    _, count, pixels = ins[0].shape
+    mix = 2 * hidden
+    patch_at = mix + 4 * model
+    table_at = patch_at + packed_width_p(pixels)
+
+    def store_mlp():
+        tail[..., :mix] = shaped(acc[:, :mix])
+
+    def store_mix():
+        tail[..., mix:patch_at] = shaped(acc[:, : 4 * model])
+
+    def store_rest():
+        spare = tail.shape[-1] - table_at - model
+        ends = [acc_p[...], jnp.zeros((model, packed_width_p(pixels) - pixels), F32)]
+        ends.append(table_of(places, rows, count, model))
+        if spare:
+            ends.append(jnp.zeros((model, spare), F32))
+        tail[..., patch_at:] = shaped(jnp.concatenate(ends, -1))
+
+    blocks = [
+        first_back(ins, image, hidden, work, rows, store_mlp, store_mix, store_rest)
+        for image in range(images)
+    ]
+    return [
+        (blocks[image][phase], phase + (image == images - 1))
+        for phase in range(3)
+        for image in range(images)
+    ]
+
+
+def start_sums(places, rows, rows_in):
+    places[...] = jnp.zeros_like(places)
+    rows[...] = rows_in[...]
+
+
+def back_scratch(images, total, model, hidden, pixels, rows_shape):
+    return [
+        pltpu.VMEM((model, max(2 * hidden, 4 * model)), F32),
+        pltpu.VMEM((model, pixels), F32),
+        pltpu.VMEM((images, total, model), F32),
+        pltpu.VMEM((images, total, 3 * model), BF16),
+        pltpu.VMEM((total, model), F32),
+        pltpu.VMEM(rows_shape, F32),
+    ]
+
+
+def first_back_plain(patches, covered, weight_0, rows, grad_in, saved, rows_in, width):
+    images, count, pixels = patches.shape
+    model, columns = weight_0.shape
+    hidden = (columns - 4 * model) // 2
+    ins = [patches, covered[..., None], weight_0, rows, grad_in]
+    ins += [saved[index] for index in (0, 1, 3, 4, 5)] + [rows_in]
+    vmem = pl.BlockSpec(memory_space=pltpu.VMEM)
+    return pl.pallas_call(
+        functools.partial(first_back_kernel, images, hidden),
+        out_shape=jax.ShapeDtypeStruct((model, width), BF16),
+        in_specs=[vmem] * len(ins),
+        out_specs=vmem,
+        scratch_shapes=back_scratch(images, count + TAIL, model, hidden, pixels, rows.shape),
         compiler_params=pltpu.CompilerParams(vmem_limit_bytes=58 << 20),
-        name="backbone_backward",
-    )(patches, covered[..., None], weight_p, weight_0, weight_1, rows, ends, grad_cls, *saved)
+        name="first_layer_backward",
+    )(*ins)
+
+
+def back_reduce(
+    patches, covered, weight_0, rows, grad_in, saved, rows_in, grads_1, squares, fsdp_count,
+    collective_id
+):
+    images, count, pixels = patches.shape
+    model, columns = weight_0.shape
+    hidden = (columns - 4 * model) // 2
+    size = model
+    places, width = plan_of(pixels, columns, model, size)
+    lines, own = fsdp_count // 2, model // fsdp_count
+    cuts = width // (3 * size)
+    last_cuts = columns // (3 * size)
+    mlp_cuts = last_cuts + 2 * hidden // (3 * size)
+    mix_cuts = 2 * last_cuts
+    split = (lines, 2, own)
+    ins = [patches, covered[..., None], weight_0, rows, grad_in]
+    ins += [saved[index] for index in (0, 1, 3, 4, 5)]
+    ins += [rows_in, grads_1.reshape(split + (columns,)), squares]
+    blocks = (cuts,) + split + (size,)
+
+    def kernel(*refs):
+        parts, (rows_ref, grads_ref, squares_ref) = refs[:10], refs[10:13]
+        outs, tail = refs[13:17], refs[17]
+        work, rows_s, rest = refs[18:23], refs[23], refs[24:]
+        whole = [last_cuts, mlp_cuts, mix_cuts, cuts]
+        ready = [last_cuts]
+
+        def shaped(value):
+            return value.reshape(split + (value.shape[1],)).astype(BF16)
+
+        start_sums(work[-1], rows_s, rows_ref)
+        queue = back_pieces(parts, images, hidden, work, rows_s, tail, shaped)
+
+        def part_of(cut, which, size):
+            ref = grads_ref if cut < last_cuts else tail
+            at = cut if cut < last_cuts else cut - last_cuts
+            return ref.at[:, :, :, pl.ds(pl.multiple_of((3 * at + which) * size, 128), size)]
+
+        def between(tick):
+            if tick and queue:
+                piece, done = queue.pop(0)
+                piece()
+                ready[0] = whole[done]
+            return ready[0], 2 if queue else 1
+
+        reduce_kernel(cuts, lines, places, part_of, squares_ref, outs, between, *rest)
+
+    shape = jax.ShapeDtypeStruct
+    sems = pltpu.SemaphoreType.DMA
+    vmem = pl.BlockSpec(memory_space=pltpu.VMEM)
+    return pl.pallas_call(
+        kernel,
+        out_shape=[
+            shape((own, places[1]), F32),
+            shape((2, own, columns), F32),
+            shape((fsdp_count, own, model), F32),
+            shape((8, 128), F32),
+        ],
+        in_specs=[vmem] * len(ins),
+        out_specs=[vmem] * 4,
+        scratch_shapes=[pltpu.VMEM(split + (width - columns,), BF16)]
+        + back_scratch(images, count + TAIL, model, hidden, pixels, rows.shape)
+        + [pltpu.VMEM(blocks, BF16)] * 3
+        + [pltpu.VMEM((cuts, lines, own, size), BF16)] * 3
+        + [
+            pltpu.VMEM((cuts, 2, own, size), BF16),
+            pltpu.VMEM((own, width), BF16),
+            pltpu.VMEM((fsdp_count, own, model), BF16),
+            pltpu.VMEM((fsdp_count, 8, 128), F32),
+            sems((cuts, 4)),
+            sems((cuts, 4)),
+            sems((cuts, lines)),
+            sems((cuts, lines)),
+            sems((cuts, 4)),
+            sems((cuts, 4)),
+            sems((2, fsdp_count - 1)),
+            sems((2, fsdp_count)),
+        ],
+        compiler_params=pltpu.CompilerParams(
+            collective_id=collective_id, has_side_effects=True, vmem_limit_bytes=60 << 20
+        ),
+        name="back_reduce",
+    )(*ins)
+
+
+def packed_width_p(pixels):
+    return (pixels + 127) // 128 * 128
 
 
 def owners_of(low, high, rows, count):
@@ -1734,9 +1858,11 @@
     return (weight - step_rate * (direction + weight_decay * weight), moment, second)
 
 
-def own_kernels(local, head_rows, model, hidden, total):
+def own_kernels(local, head_rows, model, hidden, total, layer_columns):
     count = lax.axis_size("fsdp")
     if lax.axis_size("dp") != 4 or count not in (4, 8) or local != 4 or head_rows % 16:
+        return False
+    if model % (16 * count) or hidden % 256 or layer_columns % (3 * model):
         return False
     for low, high in ((0, model), (hidden + model, total)):
         rows = (high - low) // count
@@ -1872,7 +1998,7 @@
     fsdp_count = lax.axis_size("fsdp")
     own_rows, own_k = w_head.shape[0], w_proto.shape[0]
     total_rows = own_rows * fsdp_count
-    own = own_kernels(local, own_rows, model_width, hidden, total_rows)
+    own = own_kernels(local, own_rows, model_width, hidden, total_rows, columns)
     if own:
         ranges = ((0, model_width), (model_width + hidden, total_rows))
         full, teacher_rows, cls_rows, saved = gather_forward(
@@ -1905,25 +2031,32 @@
             own_centre, counted, counted_total, w_proto, teacher_proto, own_rows,
         )
     grad_rows = jnp.pad(grad_cls, ((0, TAIL - grad_cls.shape[0]), (0, 0)))
-    packed_grads = backward(
-        patches, covered, patch_full, layer_0, layer_1, vectors, ends, grad_rows, saved
-    )
-    cut_0 = packed_width_p(pixels)
-    cut_1, cut_2 = cut_0 + columns, cut_0 + 2 * columns
+    _, rows_table = split_table(vectors, patches.shape[1])
+    grads_1, grad_x, rows_grad = last_back(layer_1, rows_table, grad_rows, saved)
+    rows_grad = rows_grad.at[14:16].add(ends)
     if own:
-        places = (cut_0, cut_1, cut_2, model_width)
-        own_patch, own_layers, table, sums = reduce_rows(
-            packed_grads, part, places, fsdp_count, 9, 2
+        own_patch, own_layers, table, sums = back_reduce(
+            patches, covered, layer_0, rows_table, grad_x, saved, rows_grad, grads_1, part,
+            fsdp_count, 2,
         )
         vector_grad = table.reshape(model_width, model_width)[: vectors.shape[0]]
         own_patch = own_patch[:, :pixels]
         squares = jnp.sum(sums)
     else:
+        places, width = plan_of(pixels, columns, model_width, model_width)
+        tail = first_back_plain(
+            patches, covered, layer_0, rows_table, grad_x, saved, rows_grad, width - columns
+        )
+        packed_grads = jnp.concatenate([grads_1, tail], 1)
         owned = lax.psum_scatter(packed_grads, "fsdp", scatter_dimension=0, tiled=True)
         owned = lax.psum(owned, "dp").astype(F32)
-        own_patch = owned[:, :pixels]
-        own_layers = jnp.stack([owned[:, cut_0:cut_1], owned[:, cut_1:cut_2]])
-        own_table = owned[:, cut_2 : cut_2 + model_width]
+        patch_at, _, table_at, _, spans = places
+        own_patch = owned[:, patch_at : patch_at + pixels]
+        first_layer_parts = [
+            owned[:, start : start + span] for layer, _, start, span in spans if layer == 0
+        ]
+        own_layers = jnp.stack([jnp.concatenate(first_layer_parts, 1), owned[:, :columns]])
+        own_table = owned[:, table_at : table_at + model_width]
         table = lax.all_gather(own_table, "fsdp", axis=0, tiled=True)
         vector_grad = table[: vectors.shape[0]]
         parts = (own_patch, own_layers, grad_head, grad_proto, own_table)

time: 443 us -> 413 us (0.932)
  Pallas kernels: 358 us -> 330 us
    pallas_call x2, Pallas kernels: 128 us -> 110 us  [the longest x1 91 us: back_reduce(): pl.pallas_call(kernel, out_shape=[shape((own, places[1]), F32), shape((2,...]
    pallas_call x1, Pallas kernels: 151 us -> 140 us  [gather_forward(): pl.pallas_call(kernel, out_shape=[shape(dims, BF16) for dims in full] + [...]
where the time goes in v5:
time: 413 us; the launch traced here: 405 us
  Pallas kernels  330 us (80%)
  other arithmetic  30.9 us (7%)
  matrix products  23 us (6%)
  local copies, waits for them, and re-layouts  16.2 us (4%)
  between operations  5.08 us (1%)
    pallas_call x1, Pallas kernels, gather_forward(): pl.pallas_call(kernel, out_shape=[shape(dims, BF16) for dims in full] + [...  140 us
    pallas_call x1, Pallas kernels, back_reduce(): pl.pallas_call(kernel, out_shape=[shape((own, places[1]), F32), shape((2,...  91 us
    pallas_call x1, Pallas kernels, head_step(): pl.pallas_call(functools.partial(head_kernel, (count, dp_count, rows, chu...  79.6 us
    dot_general x1, matrix products, dot(): lax.dot_general(left, right, (dims, ((), ())), preferred_element_type=F32)  23 us
    pallas_call x1, Pallas kernels, last_back(): pl.pallas_call(functools.partial(last_back_kernel, images, hidden), grid=...  18.9 us
    add x4, other arithmetic, per_device(): TEACHER_KEEP * teachers[group] + (1.0 - TEACHER_KEEP) * updated  15.6 us

profile of v5, /device:TPU:0, one launch (start us, length us, event | category | flops | bytes accessed | tf_op | source)
XLA Modules:
  0.0 405.0 jit_solution(16270358190964863112)
XLA Ops:
  0.7 0.0 copy-start.14
  0.7 1.0 convert.16
  1.7 0.6 pad.15.refs_0_
  2.3 1.6 convert.19
  3.9 0.0 copy-done.14
  3.9 0.0 copy-start.25
  3.9 0.0 copy-start.9
  3.9 0.1 convert.17
  4.0 1.2 slice_bitcast_fusion
  5.3 0.0 copy-done.25
  5.3 0.6 pad.16.refs_3_
  5.9 0.5 copy-done.9
  6.4 1.3 convert_element_type.35.refs_6_.shard_s
  7.7 0.0 copy-done.11
  7.7 0.0 copy-start.22
  7.7 1.3 convert_element_type.36.refs_7_.shard_t
  9.0 0.3 copy-done.24
  9.3 2.3 copy.51.refs_8_.refs_0_
  11.6 1.0 copy.52.refs_9_.refs_1_
  12.7 0.0 copy-done.22
  12.7 0.1 pad.29.clone
  12.8 1.0 maximum_maximum_fusion.1
  13.9 0.6 slice.94.refs_11_
  14.5 0.6 slice.98.refs_13_.rows_table.refs_3_
  15.1 140.3 %gather_forward.1 = (bf16[384,640]{1,0:T(8,128)(2,1)}, bf16[384,4608]{1,0:T(8,128)(2,1)}, bf16[384,4608]{1,0:T(8,128)(2,1)}, bf16[384,640]{1,0:T(8,128)(2,1)}, b...) custom-call(bf16[48,640]{1,0:T(8,128)(2,1)} %pad.15.refs_0_, ...), custom_call_target="tpu_custom_call" | custom-call | tf_op jit(solution)/shard_map/gather_forward/pallas_call | solution.py:403
  155.4 0.7 slice.100
  156.1 0.7 slice.99
  156.8 0.6 pad_maximum_fusion.1.cls
  157.4 0.6 pad_maximum_fusion.gains
  158.1 1.4 dynamic_slice.3
  159.4 0.5 convert_bitcast_fusion.1
  160.0 0.7 copy.53.counted_col
  160.7 0.0 copy-start.5
  160.7 0.0 copy-start.7
  160.7 0.0 copy-start.8
  160.7 79.6 %head_step.1 = (f32[8,384]{1,0:T(8,128)}, f32[8,384]{1,0:T(8,128)}, f32[1,128]{1,0:T(1,128)}, f32[8,8,1024]{2,1,0:T(8,128)}, bf16[128,8192]{1,0:T(8,128)(2,1)}, ...) custom-call(f32[8,384]{1,0:T(8,128)} %pad_maximum_fusion.1.cls, f32[16,384]{1,0:T(8,128)} %pad_maximum_fusion.gains, ...), custom_call_target="tpu_custom_call" | custom-call | tf_op jit(solution)/shard_map/head_step/pallas_call | solution.py:1766
  240.4 1.2 reduce_sum.27
  241.6 0.6 convert_reduce_fusion
  242.8 0.7 pad.17.grad_cls
  243.6 18.9 %last_layer_backward.1 = (bf16[384,4608]{1,0:T(8,128)(2,1)}, f32[4,272,384]{2,1,0:T(8,128)S(1)}, f32[16,384]{1,0:T(8,128)S(1)}) custom-call(bf16[384,4608]{1,0:T(8,128)(2,1)} %get-tuple-element.78.weight_1, f32[16,384]{1,0:T(8,128)S(1)} %copy-done.3, f32[16,384]{1,0:T(8,128)S(1)} %pad.17.grad_cls, f32[4,272,384]{2,1,0:T(8,128)S(1)} %copy-done.1, ...), custom_call_target="tpu_custom_call" | custom-call | tf_op jit(solution)/shard_map/last_layer_backward/pallas_call | solution.py:998
  262.5 1.2 copy-done
  263.7 0.6 copy-done.6
  264.3 1.3 add_dynamic-update-slice_fusion.refs_10_
  265.6 91.0 %back_reduce.1 = (f32[48,640]{1,0:T(8,128)}, f32[2,48,4608]{2,1,0:T(8,128)}, f32[8,48,384]{2,1,0:T(8,128)}, f32[8,128]{1,0:T(8,128)}) custom-call(bf16[4,256,588]{2,1,0:T(8,128)(2,1)} %copy.51.refs_8_.refs_0_, f32[4,256,1]{2,1,0:T(8,128)} %copy.52.refs_9_.refs_1_, bf16[384,4608]{1,0:T(8,128)(2,1)} %get-tuple-element.77.refs_2_, ...), custom_call_target="tpu_custom_call" | custom-call | tf_op jit(solution)/shard_map/back_reduce/pallas_call | solution.py:1247
  356.6 0.0 copy-start.13
  356.6 1.4 reduce_sum.29
  358.7 1.0 divide_bitcast_fusion
  359.8 1.7 multiply_add_fusion.8
  361.5 2.0 multiply_add_fusion.9
  363.5 0.0 copy-done.13
  363.5 0.0 copy-start.12
  363.5 0.0 copy-start.16
  363.5 0.0 copy-start.17
  363.6 7.1 %multiply_add_fusion.4 = (f32[2,48,4608]{2,1,0:T(8,128)}, f32[2,48,4608]{2,1,0:T(8,128)}, f32[2,48,4608]{2,1,0:T(8,128)}, f32[2,48,4608]{2,1,0:T(8,128)}) fusion(f32[2,48,4608]{2,1,0:T(8,128)S(1)} %copy-done.15, f32[2,48,4608]{2,1,0:T(8,128)S(1)} %copy-done.13, f32[2,48,4608]{2,1,0:T(8,128)} %get-tuple-element.99, f32[]{:T(128)S(6)} %div.90, ...), kind=kLoop, calls=%fused_computation.13 | loop fusion | flops 8404992 | bytes 15925252 | tf_op jit(solution)/shard_map/add | solution.py:2089
  370.6 0.0 copy-done.12
  370.6 1.2 copy-done.17
  371.9 0.8 copy-done.18
  372.6 5.1 %multiply_add_fusion.2 = (f32[336,2048]{1,0:T(8,128)}, f32[336,2048]{1,0:T(8,128)}, f32[336,2048]{1,0:T(8,128)}, f32[336,2048]{1,0:T(8,128)}) fusion(f32[336,2048]{1,0:T(8,128)S(1)} %copy-done.12, f32[336,2048]{1,0:T(8,128)S(1)} %copy-done.10, f32[336,2048]{1,0:T(8,128)S(1)} %copy-done.18, f32[]{:T(128)S(6)} %div.90, f32[336,2048]{1,0:T(8,128)S(1)} %copy-done.16, ...), kind=kLoop, calls=%fused_computation.8 | loop fusion | flops 13074432 | bytes 24772612 | tf_op jit(solution)/shard_map/add | solution.py:2089
  377.7 0.0 copy-done.19
  377.7 0.0 copy-start.23
  377.8 0.0 copy-start.26
  377.8 0.0 copy-start.27
  377.8 23.0 %multiply_add_fusion = (f32[8192,256]{1,0:T(8,128)}, f32[8192,256]{1,0:T(8,128)}, f32[8192,256]{1,0:T(8,128)}, f32[8192,256]{1,0:T(8,128)}) fusion(f32[8192,256]{1,0:T(8,128)} %proto_t.1, f32[8192,256]{1,0:T(8,128)} %proto_s.1, f32[8192,256]{1,0:T(8,128)} %param.43, f32[8192,256]{1,0:T(8,128)} %param.44, f32[]{:T(128)S(6)} %div.90, ...), kind=kOutput, calls=%fused_computation.3 | convolution fusion | flops 576716800 | bytes 69271552 | tf_op jit(solution)/shard_map/dot_general | solution.py:1822
  400.8 1.5 multiply_add_fusion.6
  (48 shorter events, 0.2 us)
Async XLA Ops:
  0.7 3.3 copy-start.14
  3.9 1.4 copy-start.25
  3.9 2.5 copy-start.9
  5.3 2.4 copy-start.11
  7.7 1.6 copy-start.24
  7.7 3.9 copy-start.30
  7.7 4.9 %copy-start.20 = (f32[274,384]{1,0:T(8,128)S(1)}, f32[274,384]{1,0:T(8,128)}, u32[]{:S(2)}) copy-start(f32[274,384]{1,0:T(8,128)} %param.49) | copy-start | bytes 1262596
  7.7 4.9 %copy-start.22 = (f32[274,384]{1,0:T(8,128)S(1)}, f32[274,384]{1,0:T(8,128)}, u32[]{:S(2)}) copy-start(f32[274,384]{1,0:T(8,128)} %param.46) | copy-start | bytes 1262596
  15.1 144.4 %copy-start.31 = (s32[128]{0:T(128)S(1)}, s32[128]{0:T(128)}, u32[]{:S(2)}) copy-start(s32[128]{0:T(128)} %param.28) | copy-start | bytes 1540
  160.7 82.8 %copy-start.1 = (f32[4,272,384]{2,1,0:T(8,128)S(1)}, f32[4,272,384]{2,1,0:T(8,128)}, u32[]{:S(2)}) copy-start(f32[4,272,384]{2,1,0:T(8,128)} %get-tuple-element.80.x2_in) | copy-start | bytes 5013508
  160.7 82.8 %copy-start.2 = (bf16[4,272,768]{2,1,0:T(8,128)(2,1)S(1)}, bf16[4,272,768]{2,1,0:T(8,128)(2,1)}, u32[]{:S(2)}) copy-start(bf16[4,272,768]{2,1,0:T(8,128)(2,1)} %get-tuple-element.81.kv_in) | copy-start | bytes 5013508
  160.7 82.8 %copy-start.3 = (f32[16,384]{1,0:T(8,128)S(1)}, f32[16,384]{1,0:T(8,128)}, u32[]{:S(2)}) copy-start(f32[16,384]{1,0:T(8,128)} %slice.98.refs_13_.rows_table.refs_3_) | copy-start | bytes 73732
  160.7 82.8 %copy-start.4 = (bf16[4,16,384]{2,1,0:T(8,128)(2,1)S(1)}, bf16[4,16,384]{2,1,0:T(8,128)(2,1)}, u32[]{:S(2)}) copy-start(bf16[4,16,384]{2,1,0:T(8,128)(2,1)} %get-tuple-element.82.q1_in) | copy-start | bytes 147460
  160.7 82.9 %copy-start.5 = (f32[4,16,128]{2,1,0:T(8,128)S(1)}, f32[4,16,128]{2,1,0:T(8,128)}, u32[]{:S(2)}) copy-start(f32[4,16,128]{2,1,0:T(8,128)} %get-tuple-element.83.lse1_in) | copy-start | bytes 98308
  160.7 82.9 %copy-start.7 = (f32[16,384]{1,0:T(8,128)S(1)}, f32[16,384]{1,0:T(8,128)}, u32[]{:S(2)}) copy-start(f32[16,384]{1,0:T(8,128)} %get-tuple-element.84.x1c_in) | copy-start | bytes 73732
  160.7 82.9 %copy-start.8 = (bf16[16,384]{1,0:T(8,128)(2,1)S(1)}, bf16[16,384]{1,0:T(8,128)(2,1)}, u32[]{:S(2)}) copy-start(bf16[16,384]{1,0:T(8,128)(2,1)} %get-tuple-element.85.o1_in) | copy-start | bytes 36868
  262.5 1.2 copy-start
  263.7 0.6 copy-start.6
  265.6 97.9 %copy-start.15 = (f32[2,48,4608]{2,1,0:T(8,128)S(1)}, f32[2,48,4608]{2,1,0:T(8,128)}, u32[]{:S(2)}) copy-start(f32[2,48,4608]{2,1,0:T(8,128)} %param.37) | copy-start | bytes 5308420
  356.6 6.9 %copy-start.13 = (f32[2,48,4608]{2,1,0:T(8,128)S(1)}, f32[2,48,4608]{2,1,0:T(8,128)}, u32[]{:S(2)}) copy-start(f32[2,48,4608]{2,1,0:T(8,128)} %param.34) | copy-start | bytes 5308420
  363.5 7.1 %copy-start.10 = (f32[336,2048]{1,0:T(8,128)S(1)}, f32[336,2048]{1,0:T(8,128)}, u32[]{:S(2)}) copy-start(f32[336,2048]{1,0:T(8,128)} %param.38) | copy-start | bytes 8257540
  363.5 7.1 %copy-start.12 = (f32[336,2048]{1,0:T(8,128)S(1)}, f32[336,2048]{1,0:T(8,128)}, u32[]{:S(2)}) copy-start(f32[336,2048]{1,0:T(8,128)} %param.41) | copy-start | bytes 8257540
  363.5 7.1 %copy-start.16 = (f32[336,2048]{1,0:T(8,128)S(1)}, f32[336,2048]{1,0:T(8,128)}, u32[]{:S(2)}) copy-start(f32[336,2048]{1,0:T(8,128)} %param.39) | copy-start | bytes 8257540
  363.5 8.3 %copy-start.17 = (f32[336,2048]{1,0:T(8,128)S(1)}, f32[336,2048]{1,0:T(8,128)}, u32[]{:S(2)}) copy-start(f32[336,2048]{1,0:T(8,128)} %param.40) | copy-start | bytes 8257540
  363.5 9.1 %copy-start.18 = (f32[336,2048]{1,0:T(8,128)S(1)}, f32[336,2048]{1,0:T(8,128)}, u32[]{:S(2)}) copy-start(f32[336,2048]{1,0:T(8,128)} %get-tuple-element.100) | copy-start | bytes 8257540
  372.6 5.1 %copy-start.19 = (bf16[128,8192]{1,0:T(8,128)(2,1)S(1)}, bf16[128,8192]{1,0:T(8,128)(2,1)}, u32[]{:S(2)}) copy-start(bf16[128,8192]{1,0:T(8,128)(2,1)} %get-tuple-element.101) | copy-start | bytes 6291460
  372.6 5.1 %copy-start.29 = (bf16[128,256]{1,0:T(8,128)(2,1)S(1)}, bf16[128,256]{1,0:T(8,128)(2,1)}, u32[]{:S(2)}) copy-start(bf16[128,256]{1,0:T(8,128)(2,1)} %get-tuple-element.102) | copy-start | bytes 196612
  377.7 23.1 %copy-start.21 = (f32[274,384]{1,0:T(8,128)S(1)}, f32[274,384]{1,0:T(8,128)}, u32[]{:S(2)}) copy-start(f32[274,384]{1,0:T(8,128)} %param.49) | copy-start | bytes 1262596
  377.7 23.1 %copy-start.23 = (f32[274,384]{1,0:T(8,128)S(1)}, f32[274,384]{1,0:T(8,128)}, u32[]{:S(2)}) copy-start(f32[274,384]{1,0:T(8,128)} %param.46) | copy-start | bytes 1262596
  377.8 23.1 %copy-start.26 = (f32[274,384]{1,0:T(8,128)S(1)}, f32[274,384]{1,0:T(8,128)}, u32[]{:S(2)}) copy-start(f32[274,384]{1,0:T(8,128)} %param.47) | copy-start | bytes 1262596
  377.8 23.1 %copy-start.27 = (f32[274,384]{1,0:T(8,128)S(1)}, f32[274,384]{1,0:T(8,128)}, u32[]{:S(2)}) copy-start(f32[274,384]{1,0:T(8,128)} %param.48) | copy-start | bytes 1262596
  377.8 23.1 %copy-start.28 = (f32[8,48,384]{2,1,0:T(8,128)S(1)}, f32[8,48,384]{2,1,0:T(8,128)}, u32[]{:S(2)}) copy-start(f32[8,48,384]{2,1,0:T(8,128)} %get-tuple-element.103) | copy-start | bytes 1769476
